TPU v7x, 32 devices: a whole 2x2x4 slice. The times are simulated.
32 devices in a mesh: fsdp: 4 (over y, x), ctx: 4 (over z), tp: 2 (over core).
Axes of the slice: x: 2, y: 2, z: 4, core: 2. Of those that a mesh axis runs over, the one named last changes fastest.
Arguments:
- block_in: bfloat16 [4, 1024, 2048], P('fsdp', 'ctx'), may hold values from -6 to 6
- span_order: int32 [4, 8], P('fsdp'), may hold values from 0 to 7, each once within a row
- attn_gain: bfloat16 [2048], P(('fsdp', 'ctx')), may hold values from 0.5 to 1.5
- w_query: bfloat16 [2048, 2048], P(('fsdp', 'ctx'), 'tp'), may hold values from -0.125 to 0.125
- w_key: bfloat16 [2048, 2048], P(('fsdp', 'ctx'), 'tp'), may hold values from -0.125 to 0.125
- w_value: bfloat16 [2048, 2048], P(('fsdp', 'ctx'), 'tp'), may hold values from -0.125 to 0.125
- w_out: bfloat16 [2048, 2048], P('tp', ('fsdp', 'ctx')), may hold values from -1.5 to 1.5
- mlp_gain: bfloat16 [2048], P(('fsdp', 'ctx')), may hold values from 0.5 to 1.5
- w_gate: bfloat16 [2048, 8192], P(('fsdp', 'ctx'), 'tp'), may hold values from -0.125 to 0.125
- w_up: bfloat16 [2048, 8192], P(('fsdp', 'ctx'), 'tp'), may hold values from -0.125 to 0.125
- w_down: bfloat16 [8192, 2048], P('tp', ('fsdp', 'ctx')), may hold values from -0.0625 to 0.0625
- clip_limit: float32 [32], P('tp'), may hold values from 3 to 12
- cotangent: bfloat16 [4, 1024, 2048], P('fsdp', 'ctx'), may hold values from -6 to 6
Outputs:
- block_out: bfloat16 [4, 1024, 2048], P('fsdp', 'ctx')
- input_grad: float32 [4, 1024, 2048], P('fsdp', 'ctx')
- grad_attn_gain: float32 [2048], P(('fsdp', 'ctx'))
- grad_w_query: float32 [2048, 2048], P(('fsdp', 'ctx'), 'tp')
- grad_w_key: float32 [2048, 2048], P(('fsdp', 'ctx'), 'tp')
- grad_w_value: float32 [2048, 2048], P(('fsdp', 'ctx'), 'tp')
- grad_w_out: float32 [2048, 2048], P('tp', ('fsdp', 'ctx'))
- grad_mlp_gain: float32 [2048], P(('fsdp', 'ctx'))
- grad_w_gate: float32 [2048, 8192], P(('fsdp', 'ctx'), 'tp')
- grad_w_up: float32 [2048, 8192], P(('fsdp', 'ctx'), 'tp')
- grad_w_down: float32 [8192, 2048], P('tp', ('fsdp', 'ctx'))
- logit_max: float32 [32], P('tp')
- clipped_query: float32 [2048, 2048], P(('fsdp', 'ctx'), 'tp')
- clipped_key: float32 [2048, 2048], P(('fsdp', 'ctx'), 'tp')
Inputs may be any that keep to these rules, and one draw needn't show every extreme that they name: Each row is a permutation: slot j of sequence s holds the tokens at positions span_order[s, j] * 128 to span_order[s, j] * 128 + 127.
All inputs are finite; a program needn't handle non-finite values.
Results may differ from a plain program's by a relative error of at most 0.014.
Values may be sent and summed in bfloat16 or wider, within the bound.
No kernel may reach another device: no remote copies, remote signals or barrier semaphores. Data moves between devices by JAX's collectives and lax.ppermute only.
A program may use at most 320 MiB of HBM per device.

v0:
```python
import jax
import jax.numpy as jnp
from jax import lax
from jax.sharding import PartitionSpec as P

HEAD_DIM = 64


NORM_EPS = 1e-05
ROPE_BASE = 130000.0


def span_positions(order_row, span_len):
    slot_count = order_row.shape[0]
    offsets = jnp.arange(span_len, dtype=jnp.int32)
    return (order_row[:, None] * span_len + offsets[None, :]).reshape(slot_count * span_len)


def rope_tables(positions, half_dim):
    step_index = jnp.arange(half_dim, dtype=jnp.float32)
    frequency = jnp.power(ROPE_BASE, -2.0 * step_index / (2 * half_dim))
    angles = positions.astype(jnp.float32)[:, None] * frequency[None, :]
    return (jnp.cos(angles), jnp.sin(angles))


def rotate(tensor, cosine_tab, sine_tab):
    half_dim = tensor.shape[-1] // 2
    first_half, second_half = (tensor[..., :half_dim], tensor[..., half_dim:])
    cosine_b, sine_b = (cosine_tab[:, None, :], sine_tab[:, None, :])
    return jnp.concatenate(
        [
            first_half * cosine_b - second_half * sine_b,
            second_half * cosine_b + first_half * sine_b,
        ],
        -1,
    )


def rotate_back(tensor, cosine_tab, sine_tab):
    half_dim = tensor.shape[-1] // 2
    first_half, second_half = (tensor[..., :half_dim], tensor[..., half_dim:])
    cosine_b, sine_b = (cosine_tab[:, None, :], sine_tab[:, None, :])
    return jnp.concatenate(
        [
            first_half * cosine_b + second_half * sine_b,
            second_half * cosine_b - first_half * sine_b,
        ],
        -1,
    )


def on_device(
    block_in,
    span_order,
    attn_gain,
    w_query,
    w_key,
    w_value,
    w_out,
    mlp_gain,
    w_gate,
    w_up,
    w_down,
    clip_limit,
    cotangent,
):
    f32 = jnp.float32
    bf16 = jnp.bfloat16
    row_count = block_in.shape[1]
    span_len = row_count // 2
    score_scale = HEAD_DIM ** (-0.5)
    all_pos = span_positions(span_order[0], span_len)
    my_pos = lax.dynamic_slice_in_dim(all_pos, lax.axis_index("ctx") * row_count, row_count)
    causal_mask = all_pos[None, :] <= my_pos[:, None]
    cosine_mine, sine_mine = rope_tables(my_pos, HEAD_DIM // 2)
    gain_one, query_full, key_full, value_full, out_full = (
        lax.all_gather(attn_gain, ("fsdp", "ctx"), axis=0, tiled=True),
        lax.all_gather(w_query, ("fsdp", "ctx"), axis=0, tiled=True),
        lax.all_gather(w_key, ("fsdp", "ctx"), axis=0, tiled=True),
        lax.all_gather(w_value, ("fsdp", "ctx"), axis=0, tiled=True),
        lax.all_gather(w_out, ("fsdp", "ctx"), axis=1, tiled=True),
    )
    local_width = query_full.shape[1]
    heads_here = local_width // HEAD_DIM
    group_size = 2
    group_count = heads_here // group_size
    inputs = block_in[0].astype(f32)
    inv_one = lax.rsqrt(jnp.mean(inputs * inputs, -1, keepdims=True) + NORM_EPS)
    normed_one = (inputs * inv_one * gain_one.astype(f32)).astype(bf16)
    proj_query = jnp.dot(normed_one, query_full, preferred_element_type=f32)
    proj_key = jnp.dot(normed_one, key_full, preferred_element_type=f32)
    proj_value = jnp.dot(normed_one, value_full, preferred_element_type=f32)
    query_rot = (
        rotate(proj_query.reshape(row_count, heads_here, HEAD_DIM), cosine_mine, sine_mine)
        .astype(bf16)
        .reshape(row_count, local_width)
    )
    key_rot = (
        rotate(proj_key.reshape(row_count, heads_here, HEAD_DIM), cosine_mine, sine_mine)
        .astype(bf16)
        .reshape(row_count, local_width)
    )
    value_low = proj_value.astype(bf16)
    key_all, value_all = (
        lax.all_gather(key_rot, "ctx", axis=0, tiled=True),
        lax.all_gather(value_low, "ctx", axis=0, tiled=True),
    )
    length = key_all.shape[0]

    def split_heads(tensor, count_rows):
        return tensor.reshape(count_rows, group_count, group_size, HEAD_DIM).transpose(1, 0, 2, 3)

    def join_heads(tensor, count_rows):
        return tensor.transpose(1, 0, 2, 3).reshape(count_rows, local_width)

    def forward_group(operands):
        query_grp, key_grp, value_grp = operands
        scores = (
            jnp.einsum("qhd,khd->hqk", query_grp, key_grp, preferred_element_type=f32) * score_scale
        )
        masked = jnp.where(causal_mask[None], scores, -1e30)
        head_max = jnp.max(masked, axis=(1, 2))
        row_max = jnp.max(masked, axis=2, keepdims=True)
        exp_terms = jnp.exp(masked - row_max)
        row_total = jnp.sum(exp_terms, axis=2, keepdims=True)
        probabilities = (exp_terms / row_total).astype(bf16)
        attended = jnp.einsum("hqk,khd->qhd", probabilities, value_grp, preferred_element_type=f32)
        log_total = row_max[..., 0] + jnp.log(row_total[..., 0])
        return (attended, log_total, head_max)

    query_groups = split_heads(query_rot, row_count)
    key_groups = split_heads(key_all, length)
    value_groups = split_heads(value_all, length)
    attended, log_total, head_max = lax.map(forward_group, (query_groups, key_groups, value_groups))
    attn_low = join_heads(attended, row_count).astype(bf16)
    attn_sum = lax.psum(jnp.dot(attn_low, out_full, preferred_element_type=f32), "tp")
    resid = inputs + attn_sum
    head_peak = lax.pmax(head_max.reshape(heads_here), ("fsdp", "ctx"))
    gain_two, gate_full, up_full, down_full = (
        lax.all_gather(mlp_gain, ("fsdp", "ctx"), axis=0, tiled=True),
        lax.all_gather(w_gate, ("fsdp", "ctx"), axis=0, tiled=True),
        lax.all_gather(w_up, ("fsdp", "ctx"), axis=0, tiled=True),
        lax.all_gather(w_down, ("fsdp", "ctx"), axis=1, tiled=True),
    )
    inv_two = lax.rsqrt(jnp.mean(resid * resid, -1, keepdims=True) + NORM_EPS)
    scaled_two = resid * inv_two
    normed_two = (scaled_two * gain_two.astype(f32)).astype(bf16)
    gate_act = jnp.dot(normed_two, gate_full, preferred_element_type=f32)
    up_act = jnp.dot(normed_two, up_full, preferred_element_type=f32)
    sig_gate = jax.nn.sigmoid(gate_act)
    silu_gate = gate_act * sig_gate
    hidden = (silu_gate * up_act).astype(bf16)
    mlp_sum = lax.psum(
        jnp.dot(hidden, down_full, preferred_element_type=f32).astype(jnp.bfloat16), "tp"
    ).astype(jnp.float32)
    block_out = (resid + mlp_sum).astype(bf16)[None]
    grad_top = cotangent[0]
    grad_hidden = jnp.dot(grad_top, down_full.T, preferred_element_type=f32)
    silu_slope = sig_gate * (1.0 + gate_act * (1.0 - sig_gate))
    grad_gate = (grad_hidden * up_act * silu_slope).astype(bf16)
    grad_up = (grad_hidden * silu_gate).astype(bf16)
    grad_normed_two = lax.psum(
        jnp.dot(grad_gate, gate_full.T, preferred_element_type=f32)
        + jnp.dot(grad_up, up_full.T, preferred_element_type=f32),
        "tp",
    )
    grad_gain_two = jnp.sum(grad_normed_two * scaled_two, axis=0)
    weighted_two = grad_normed_two * gain_two.astype(f32)
    grad_resid = grad_top.astype(f32) + inv_two * (
        weighted_two - scaled_two * jnp.mean(weighted_two * scaled_two, -1, keepdims=True)
    )
    grad_down = jnp.dot(hidden.T, grad_top, preferred_element_type=f32)
    grad_w_gate = jnp.dot(normed_two.T, grad_gate, preferred_element_type=f32)
    grad_w_up = jnp.dot(normed_two.T, grad_up, preferred_element_type=f32)
    gain_two_out, gate_out, up_out, down_out = (
        lax.psum_scatter(grad_gain_two, ("fsdp", "ctx"), scatter_dimension=0, tiled=True),
        lax.psum_scatter(grad_w_gate, ("fsdp", "ctx"), scatter_dimension=0, tiled=True),
        lax.psum_scatter(grad_w_up, ("fsdp", "ctx"), scatter_dimension=0, tiled=True),
        lax.psum_scatter(grad_down, ("fsdp", "ctx"), scatter_dimension=1, tiled=True),
    )
    grad_low = grad_resid.astype(bf16)
    grad_attended = jnp.dot(grad_low, out_full.T, preferred_element_type=f32).astype(bf16)

    def backward_group(operands):
        query_grp, key_grp, value_grp, grad_out_grp, log_grp = operands
        scores = (
            jnp.einsum("qhd,khd->hqk", query_grp, key_grp, preferred_element_type=f32) * score_scale
        )
        masked = jnp.where(causal_mask[None], scores, -1e30)
        probabilities = jnp.exp(masked - log_grp[..., None])
        grad_probs = jnp.einsum("qhd,khd->hqk", grad_out_grp, value_grp, preferred_element_type=f32)
        row_delta = jnp.sum(probabilities * grad_probs, axis=2, keepdims=True)
        grad_scores = (probabilities * (grad_probs - row_delta)).astype(bf16)
        grad_query_grp = (
            jnp.einsum("hqk,khd->qhd", grad_scores, key_grp, preferred_element_type=f32)
            * score_scale
        )
        grad_key_grp = (
            jnp.einsum("hqk,qhd->khd", grad_scores, query_grp, preferred_element_type=f32)
            * score_scale
        )
        grad_value_grp = jnp.einsum(
            "hqk,qhd->khd", probabilities.astype(bf16), grad_out_grp, preferred_element_type=f32
        )
        return (grad_query_grp, grad_key_grp, grad_value_grp)

    grad_attended_groups = split_heads(grad_attended, row_count)
    grad_query_g, grad_key_g, grad_value_g = lax.map(
        backward_group, (query_groups, key_groups, value_groups, grad_attended_groups, log_total)
    )
    grad_query_rot = join_heads(grad_query_g, row_count)
    grad_key_all = join_heads(grad_key_g, length)
    grad_value_all = join_heads(grad_value_g, length)
    grad_key_mine, grad_value_mine = (
        lax.psum_scatter(grad_key_all, "ctx", scatter_dimension=0, tiled=True),
        lax.psum_scatter(grad_value_all, "ctx", scatter_dimension=0, tiled=True),
    )
    grad_query_proj = (
        rotate_back(grad_query_rot.reshape(row_count, heads_here, HEAD_DIM), cosine_mine, sine_mine)
        .reshape(row_count, local_width)
        .astype(bf16)
    )
    grad_key_proj = (
        rotate_back(grad_key_mine.reshape(row_count, heads_here, HEAD_DIM), cosine_mine, sine_mine)
        .reshape(row_count, local_width)
        .astype(bf16)
    )
    grad_value_proj = grad_value_mine.astype(bf16)
    grad_normed_one = lax.psum(
        jnp.dot(grad_query_proj, query_full.T, preferred_element_type=f32)
        + jnp.dot(grad_key_proj, key_full.T, preferred_element_type=f32)
        + jnp.dot(grad_value_proj, value_full.T, preferred_element_type=f32),
        "tp",
    )
    scaled_one = inputs * inv_one
    grad_gain_one = jnp.sum(grad_normed_one * scaled_one, axis=0)
    weighted_one = grad_normed_one * gain_one.astype(f32)
    input_grad = grad_resid + inv_one * (
        weighted_one - scaled_one * jnp.mean(weighted_one * scaled_one, -1, keepdims=True)
    )
    grad_w_out = jnp.dot(attn_low.T, grad_low, preferred_element_type=f32)
    grad_w_query = jnp.dot(normed_one.T, grad_query_proj, preferred_element_type=f32)
    grad_w_key = jnp.dot(normed_one.T, grad_key_proj, preferred_element_type=f32)
    grad_w_value = jnp.dot(normed_one.T, grad_value_proj, preferred_element_type=f32)
    gain_one_out, query_out, key_out, value_out, out_proj_out = (
        lax.psum_scatter(grad_gain_one, ("fsdp", "ctx"), scatter_dimension=0, tiled=True),
        lax.psum_scatter(grad_w_query, ("fsdp", "ctx"), scatter_dimension=0, tiled=True),
        lax.psum_scatter(grad_w_key, ("fsdp", "ctx"), scatter_dimension=0, tiled=True),
        lax.psum_scatter(grad_w_value, ("fsdp", "ctx"), scatter_dimension=0, tiled=True),
        lax.psum_scatter(grad_w_out, ("fsdp", "ctx"), scatter_dimension=1, tiled=True),
    )
    factor = jnp.sqrt(clip_limit / jnp.maximum(clip_limit, head_peak))
    column_factor = jnp.repeat(factor, HEAD_DIM)
    clipped_query = w_query.astype(f32) * column_factor[None, :]
    clipped_key = w_key.astype(f32) * column_factor[None, :]
    return (
        block_out,
        input_grad[None],
        gain_one_out,
        query_out,
        key_out,
        value_out,
        out_proj_out,
        gain_two_out,
        gate_out,
        up_out,
        down_out,
        head_peak,
        clipped_query,
        clipped_key,
    )


def solution(mesh):
    placed = (
        P("fsdp", "ctx", None),
        P("fsdp", None),
        P(("fsdp", "ctx")),
        P(("fsdp", "ctx"), "tp"),
        P(("fsdp", "ctx"), "tp"),
        P(("fsdp", "ctx"), "tp"),
        P("tp", ("fsdp", "ctx")),
        P(("fsdp", "ctx")),
        P(("fsdp", "ctx"), "tp"),
        P(("fsdp", "ctx"), "tp"),
        P("tp", ("fsdp", "ctx")),
        P("tp"),
        P("fsdp", "ctx", None),
    )
    return jax.shard_map(
        on_device,
        mesh=mesh,
        in_specs=placed,
        out_specs=(
            P("fsdp", "ctx", None),
            P("fsdp", "ctx", None),
            P(("fsdp", "ctx")),
            P(("fsdp", "ctx"), "tp"),
            P(("fsdp", "ctx"), "tp"),
            P(("fsdp", "ctx"), "tp"),
            P("tp", ("fsdp", "ctx")),
            P(("fsdp", "ctx")),
            P(("fsdp", "ctx"), "tp"),
            P(("fsdp", "ctx"), "tp"),
            P("tp", ("fsdp", "ctx")),
            P("tp"),
            P(("fsdp", "ctx"), "tp"),
            P(("fsdp", "ctx"), "tp"),
        ),
        check_vma=False,
    )
```

profile of v0, /device:TPU:0, one launch (start us, length us, event | category | flops | bytes accessed | tf_op | source)
XLA Modules:
  0.0 4249.9 jit_solution(9692700291380512646)
XLA Ops:
  9.4 42.4 all-gather
  53.4 36.0 all-gather.12.cloned.1.call-done
  89.4 4.6 convolution_convert_fusion.2
  94.5 72.1 %all-gather.18.cloned.1.call-done = bf16[2048,1024]{1,0:T(8,128)(2,1)} async-done(((bf16[128,1024]{1,0:T(8,128)(2,1)}), bf16[2048,1024]{1,0:T(8,128)(2,1)}) %all-gather.18.cloned.1.call-update) | async-done | bytes 4194320 | tf_op jit(solution)/shard_map/all_gather | solution.py:79
  166.6 6.5 copy.37
  173.1 70.8 %all-gather.16.cloned.1.call-done = bf16[2048,1024]{1,0:T(8,128)(2,1)} async-done(((bf16[128,1024]{1,0:T(8,128)(2,1)}), bf16[2048,1024]{1,0:T(8,128)(2,1)}) %all-gather.16.cloned.1.call-update) | async-done | bytes 4194320 | tf_op jit(solution)/shard_map/all_gather | solution.py:78
  243.9 6.7 copy.36
  250.5 3.9 fusion.64
  259.4 31.0 all-gather.14.cloned.1.call-done
  290.4 2.9 copy.35
  293.3 44.1 %all-gather.20.cloned.1.call-done = bf16[1024,1024]{0,1:T(8,128)(2,1)} async-done(((bf16[256,1024]{0,1:T(8,128)(2,1)}), bf16[1024,1024]{0,1:T(8,128)(2,1)}) %all-gather.20.cloned.1.call-update) | async-done | bytes 2097168 | tf_op jit(solution)/shard_map/all_gather | solution.py:105
  337.4 40.0 while.32
  377.4 50.1 %all-gather.22.cloned.1.call-done = bf16[1024,2048]{1,0:T(8,128)(2,1)} async-done(((bf16[1024,128]{1,0:T(8,128)(2,1)}), bf16[1024,2048]{1,0:T(8,128)(2,1)}) %all-gather.22.cloned.1.call-update) | async-done | bytes 4194320 | tf_op jit(solution)/shard_map/all_gather | solution.py:81
  427.5 4.9 fusion.89
  434.6 37.9 all-gather.1
  475.9 172.1 %all-gather.24.cloned.1.call-done = bf16[2048,4096]{1,0:T(8,128)(2,1)} async-done(((bf16[128,4096]{1,0:T(8,128)(2,1)}), bf16[2048,4096]{1,0:T(8,128)(2,1)}) %all-gather.24.cloned.1.call-update) | async-done | bytes 16777232 | tf_op jit(solution)/shard_map/all_gather | solution.py:141
  648.0 12.6 fusion.90
  660.6 180.4 %all-gather.26.cloned.1.call-done = bf16[2048,4096]{1,0:T(8,128)(2,1)} async-done(((bf16[128,4096]{1,0:T(8,128)(2,1)}), bf16[2048,4096]{1,0:T(8,128)(2,1)}) %all-gather.26.cloned.1.call-update) | async-done | bytes 16777232 | tf_op jit(solution)/shard_map/all_gather | solution.py:142
  840.9 12.6 fusion.91
  853.5 238.2 %all-gather.28.cloned.1.call-done = bf16[4096,2048]{1,0:T(8,128)(2,1)} async-done(((bf16[4096,128]{1,0:T(8,128)(2,1)}), bf16[4096,2048]{1,0:T(8,128)(2,1)}) %all-gather.28.cloned.1.call-update) | async-done | bytes 16777232 | tf_op jit(solution)/shard_map/all_gather | solution.py:143
  1091.7 13.6 multiply_convert_fusion.1
  1105.3 12.2 fusion.92
  1117.5 12.8 convolution_add_fusion.2
  1130.6 12.7 convolution_convert_fusion
  1143.4 6.5 all-reduce.12.cloned.1.call-done
  1152.1 21.4 all-reduce.10.cloned.1.call-done
  1173.5 4.0 multiply_add_fusion
  1180.3 67.0 %while.33 = (s32[]{:T(128)}, f32[8,256,2,64]{1,3,2,0:T(8,128)S(1)}, f32[8,1024,2,64]{1,3,2,0:T(8,128)}, f32[8,1024,2,64]{1,3,2,0:T(8,128)}, bf16[8,1024,2,64]{1,...) while((s32[]{:T(128)}, f32[8,256,2,64]{1,3,2,0:T(8,128)S(1)}, ...), condition=%wide.region_13.14_spmd.clone.clone, body=%wide.region_11.13_spmd.clone.sunk.clone | while | flops 340688384 | bytes 18501752 | solution.py:208
  1248.2 77.3 %reduce-scatter.10.cloned.1.call-done = f32[256,1024]{0,1:T(8,128)} async-done(((f32[1024,1024]{0,1:T(8,128)}), f32[256,1024]{0,1:T(8,128)}) %reduce-scatter.10.cloned.1.call-update) | async-done | bytes 1048592 | tf_op jit(solution)/shard_map/reduce_scatter | solution.py:215
  1331.5 73.4 %reduce-scatter.12.cloned.1.call-done = f32[256,1024]{0,1:T(8,128)} async-done(((f32[1024,1024]{0,1:T(8,128)}), f32[256,1024]{0,1:T(8,128)}) %reduce-scatter.12.cloned.1.call-update) | async-done | bytes 1048592 | tf_op jit(solution)/shard_map/reduce_scatter | solution.py:216
  1404.9 5.2 convolution_add_fusion
  1411.7 5.8 fusion.72
  1417.5 5.8 fusion.70
  1423.3 6.0 fusion.68
  1429.4 6.1 fusion.75
  1435.8 17.7 fusion.94
  1453.6 17.8 fusion.95
  1471.7 17.7 fusion.60
  1491.4 44.1 %pmax.7 = f32[16]{0:T(128)S(1)} all-reduce(f32[16]{0:T(128)S(1)} %reshape.268), channel_id=1, replica_groups=mesh['fsdp'=4,'ctx'=4,'tp'=2] {'fsdp','ctx'}, use_global_device_ids=true, to_apply=%region_29.30 | all-reduce | flops 16 | bytes 128 | tf_op jit(solution)/shard_map/pmax | solution.py:138
  1537.8 2.2 fusion.55
  1540.0 77.7 %all-reduce.2 = (f32[2048]{0:T(1024)S(1)}, f32[2048]{0:T(1024)S(1)}) all-reduce(f32[2048]{0:T(1024)S(1)} %get-tuple-element.170, f32[2048]{0:T(1024)S(1)} %get-tuple-element.168), channel_id=4, replica_groups=mesh['fsdp'=4,'ctx'=4,'tp'=2] {'fsdp','ctx'}, use_global_device_ids=true, to_apply=%region_19.20.clone | all-reduce | flops 4096 | bytes 32768
  1618.8 3.5 fusion.54
  1622.3 181.8 %reduce-scatter.14.cloned.1.call-done = f32[128,1024]{1,0:T(8,128)} async-done(((f32[2048,1024]{1,0:T(8,128)}), f32[128,1024]{1,0:T(8,128)}) %reduce-scatter.14.cloned.1.call-update) | async-done | bytes 524304 | tf_op jit(solution)/shard_map/reduce_scatter | solution.py:247
  1804.1 182.6 %reduce-scatter.16.cloned.1.call-done = f32[128,1024]{1,0:T(8,128)} async-done(((f32[2048,1024]{1,0:T(8,128)}), f32[128,1024]{1,0:T(8,128)}) %reduce-scatter.16.cloned.1.call-update) | async-done | bytes 524304 | tf_op jit(solution)/shard_map/reduce_scatter | solution.py:248
  1986.7 182.7 %reduce-scatter.18.cloned.1.call-done = f32[128,1024]{1,0:T(8,128)} async-done(((f32[2048,1024]{1,0:T(8,128)}), f32[128,1024]{1,0:T(8,128)}) %reduce-scatter.18.cloned.1.call-update) | async-done | bytes 524304 | tf_op jit(solution)/shard_map/reduce_scatter | solution.py:249
  2169.4 690.1 %reduce-scatter.22.cloned.1.call-done = f32[128,4096]{1,0:T(8,128)} async-done(((f32[2048,4096]{1,0:T(8,128)}), f32[128,4096]{1,0:T(8,128)}) %reduce-scatter.22.cloned.1.call-update) | async-done | bytes 2097168 | tf_op jit(solution)/shard_map/reduce_scatter | solution.py:177
  2859.5 691.6 %reduce-scatter.24.cloned.1.call-done = f32[128,4096]{1,0:T(8,128)} async-done(((f32[2048,4096]{1,0:T(8,128)}), f32[128,4096]{1,0:T(8,128)}) %reduce-scatter.24.cloned.1.call-update) | async-done | bytes 2097168 | tf_op jit(solution)/shard_map/reduce_scatter | solution.py:178
  3551.0 691.6 %reduce-scatter.26.cloned.1.call-done = f32[4096,128]{1,0:T(8,128)} async-done(((f32[4096,2048]{1,0:T(8,128)}), f32[4096,128]{1,0:T(8,128)}) %reduce-scatter.26.cloned.1.call-update) | async-done | bytes 2097168 | tf_op jit(solution)/shard_map/reduce_scatter | solution.py:179
  (234 shorter events, 140.4 us)
Async XLA Ops:
  7.2 82.2 %all-gather.12.cloned.1.call-start = ((), (), s32[]{:S(2)}) async-start(), calls=%async_computation.9 | async-start | bytes 4456448 | tf_op jit(solution)/shard_map/all_gather | solution.py:80
  7.9 158.7 %all-gather.18.cloned.1.call-start = ((), (), s32[]{:S(2)}) async-start(), calls=%async_computation.12 | async-start | bytes 4456448 | tf_op jit(solution)/shard_map/all_gather | solution.py:79
  8.7 235.2 %all-gather.16.cloned.1.call-start = ((), (), s32[]{:S(2)}) async-start(), calls=%async_computation.11 | async-start | bytes 4456448 | tf_op jit(solution)/shard_map/all_gather | solution.py:78
  9.4 281.0 %all-gather.14.cloned.1.call-start = ((), (), s32[]{:S(2)}) async-start(), calls=%async_computation.10 | async-start | bytes 2621440 | tf_op jit(solution)/shard_map/all_gather | solution.py:106
  89.4 4.7 copy-start.14
  94.0 243.4 %all-gather.20.cloned.1.call-start = ((), (), s32[]{:S(2)}) async-start(), calls=%async_computation.13 | async-start | bytes 2621440 | tf_op jit(solution)/shard_map/all_gather | solution.py:105
  243.9 6.7 copy-start
  250.5 3.9 copy-start.7
  257.1 170.4 %all-gather.22.cloned.1.call-start = ((), (), s32[]{:S(2)}) async-start(), calls=%async_computation.14 | async-start | bytes 4456448 | tf_op jit(solution)/shard_map/all_gather | solution.py:81
  257.7 214.9 %all-reduce.8.cloned.1.call-start = ((), (), s32[]{:S(2)}) async-start(), calls=%async_computation.15 | async-start | bytes 4194304 | tf_op jit(solution)/shard_map/psum | solution.py:136
  377.4 55.0 %copy-start.4 = (bf16[8,1024,2,64]{1,3,2,0:T(8,128)(2,1)}, bf16[8,1024,2,64]{1,3,2,0:T(8,128)(2,1)S(1)}, u32[]{:S(2)}) copy-start(bf16[8,1024,2,64]{1,3,2,0:T(8,128)(2,1)S(1)} %get-tuple-element.533) | copy-start | bytes 6291460
  432.5 2.1 copy-start.12
  432.5 215.5 %all-gather.24.cloned.1.call-start = ((), (), s32[]{:S(2)}) async-start(), calls=%async_computation.16 | async-start | bytes 17825792 | tf_op jit(solution)/shard_map/all_gather | solution.py:141
  433.2 407.7 %all-gather.26.cloned.1.call-start = ((), (), s32[]{:S(2)}) async-start(), calls=%async_computation.17 | async-start | bytes 17825792 | tf_op jit(solution)/shard_map/all_gather | solution.py:142
  434.0 657.7 %all-gather.28.cloned.1.call-start = ((), (), s32[]{:S(2)}) async-start(), calls=%async_computation.18 | async-start | bytes 17825792 | tf_op jit(solution)/shard_map/all_gather | solution.py:143
  434.6 715.3 %all-reduce.12.cloned.1.call-start = ((), (), s32[]{:S(2)}) async-start(), calls=%async_computation.20 | async-start | bytes 4194304 | tf_op jit(solution)/shard_map/psum | solution.py:162
  1130.3 43.1 %all-reduce.10.cloned.1.call-start = ((), (), s32[]{:S(2)}) async-start(), calls=%async_computation.19 | async-start | bytes 2097152 | tf_op jit(solution)/shard_map/psum | solution.py:153
  1143.3 182.1 %reduce-scatter.10.cloned.1.call-start = ((), (), s32[]{:S(2)}) async-start(), calls=%async_computation.21 | async-start | bytes 5242880 | tf_op jit(solution)/shard_map/reduce_scatter | solution.py:215
  1173.5 5.4 copy-start.13
  1177.5 1.3 copy-start.1
  1178.8 1.5 copy-start.9
  1247.4 157.5 %reduce-scatter.12.cloned.1.call-start = ((), (), s32[]{:S(2)}) async-start(), calls=%async_computation.22 | async-start | bytes 5242880 | tf_op jit(solution)/shard_map/reduce_scatter | solution.py:216
  1247.9 289.8 %all-reduce.14.cloned.1.call-start = ((), (), s32[]{:S(2)}) async-start(), calls=%async_computation.23 | async-start | bytes 4194304 | tf_op jit(solution)/shard_map/psum | solution.py:229
  1325.5 2.5 copy-start.6
  1327.2 2.1 copy-start.8
  1327.2 2.1 copy-start.5
  1328.0 2.2 copy-start.3
  1410.1 1.6 copy-start.2
  1410.1 212.2 %reduce-scatter.20.cloned.1.call-start = ((), (), s32[]{:S(2)}) async-start(), calls=%async_computation.27 | async-start | bytes 8912896 | tf_op jit(solution)/shard_map/reduce_scatter | solution.py:250
  1417.5 386.7 %reduce-scatter.14.cloned.1.call-start = ((), (), s32[]{:S(2)}) async-start(), calls=%async_computation.24 | async-start | bytes 8912896 | tf_op jit(solution)/shard_map/reduce_scatter | solution.py:247
  1423.3 563.4 %reduce-scatter.16.cloned.1.call-start = ((), (), s32[]{:S(2)}) async-start(), calls=%async_computation.25 | async-start | bytes 8912896 | tf_op jit(solution)/shard_map/reduce_scatter | solution.py:248
  1429.4 740.0 %reduce-scatter.18.cloned.1.call-start = ((), (), s32[]{:S(2)}) async-start(), calls=%async_computation.26 | async-start | bytes 8912896 | tf_op jit(solution)/shard_map/reduce_scatter | solution.py:249
  1435.5 1423.9 %reduce-scatter.22.cloned.1.call-start = ((), (), s32[]{:S(2)}) async-start(), calls=%async_computation.28 | async-start | bytes 35651584 | tf_op jit(solution)/shard_map/reduce_scatter | solution.py:177
  1453.5 2097.5 %reduce-scatter.24.cloned.1.call-start = ((), (), s32[]{:S(2)}) async-start(), calls=%async_computation.29 | async-start | bytes 35651584 | tf_op jit(solution)/shard_map/reduce_scatter | solution.py:178
  1471.4 2771.2 %reduce-scatter.26.cloned.1.call-start = ((), (), s32[]{:S(2)}) async-start(), calls=%async_computation.30 | async-start | bytes 35651584 | tf_op jit(solution)/shard_map/reduce_scatter | solution.py:179
  1489.5 0.7 copy-start.16
  1489.5 1.9 copy-start.11
  1489.5 46.1 %copy-start.15 = (f32[16]{0:T(128)S(1)}, f32[16]{0:T(128)}, u32[]{:S(2)}) copy-start(f32[16]{0:T(128)} %param.28) | copy-start | bytes 196
  1489.5 46.2 %copy-start.10 = (bf16[128,1024]{1,0:T(8,128)(2,1)S(1)}, bf16[128,1024]{1,0:T(8,128)(2,1)}, u32[]{:S(2)}) copy-start(bf16[128,1024]{1,0:T(8,128)(2,1)} %param.21) | copy-start | bytes 786436
  1535.5 4.5 copy-start.17
Sparse Core Ops, SparseCore 0:
  10.8 78.5 all-gather.11
  92.1 74.3 all-gather.17
  169.3 74.4 all-gather.15
  245.9 44.5 all-gather.13
  292.4 44.9 all-gather.19
  340.0 87.4 all-gather.21
  432.6 19.3 all-reduce.7
  455.1 192.7 all-gather.23
  651.1 189.7 all-gather.25
  843.9 247.8 all-gather.27
  1130.5 19.3 all-reduce.11
  1152.7 20.7 all-reduce.9
  1247.5 77.9 reduce-scatter.9
  1327.6 77.2 reduce-scatter.11
  1410.2 21.7 all-reduce.13
  1434.7 186.8 reduce-scatter.19
  1624.3 179.8 reduce-scatter.13
  1806.8 179.8 reduce-scatter.15
  1989.6 179.8 reduce-scatter.17
  2172.2 687.2 reduce-scatter.21
  2862.4 688.5 reduce-scatter.23
  3553.9 688.6 reduce-scatter.25
where the time goes:
time: 4260 us; the launch traced here: 4250 us
  waiting for transfers between devices  3700 us (87%)
  matrix products  264 us (6%)
  blocking collectives  202 us (5%)
    reduce_scatter x1, waiting for transfers between devices, on_device(): lax.psum_scatter(grad_down, ('fsdp', 'ctx'), scatter_dimension=1, tiled=T...  692 us
    reduce_scatter x1, waiting for transfers between devices, on_device(): lax.psum_scatter(grad_w_up, ('fsdp', 'ctx'), scatter_dimension=0, tiled=T...  692 us
    reduce_scatter x1, waiting for transfers between devices, on_device(): lax.psum_scatter(grad_w_gate, ('fsdp', 'ctx'), scatter_dimension=0, tiled...  690 us
    all_gather x1, waiting for transfers between devices, on_device(): lax.all_gather(w_down, ('fsdp', 'ctx'), axis=1, tiled=True)  238 us
    reduce_scatter x1, waiting for transfers between devices, on_device(): lax.psum_scatter(grad_w_value, ('fsdp', 'ctx'), scatter_dimension=0, tile...  183 us
    reduce_scatter x1, waiting for transfers between devices, on_device(): lax.psum_scatter(grad_w_key, ('fsdp', 'ctx'), scatter_dimension=0, tiled=...  183 us
    reduce_scatter x1, waiting for transfers between devices, on_device(): lax.psum_scatter(grad_w_query, ('fsdp', 'ctx'), scatter_dimension=0, tile...  182 us
    all_gather x1, waiting for transfers between devices, on_device(): lax.all_gather(w_up, ('fsdp', 'ctx'), axis=0, tiled=True)  180 us
  transfers between devices with their start and end apart: 22, of which 19 were waited for; matrix products, arithmetic and copies ran while one was open for 5% of the time, Pallas kernels for 0%

commit v1 on v0

v1 whole, which is shorter than its diff:
```python
import jax
import jax.numpy as jnp
from jax import lax
from jax.sharding import PartitionSpec as P

HEAD_DIM = 64
NORM_EPS = 1e-05
ROPE_BASE = 130000.0

f32 = jnp.float32
bf16 = jnp.bfloat16


def rope_tables(positions, half_dim):
    step_index = jnp.arange(half_dim, dtype=f32)
    frequency = jnp.power(ROPE_BASE, -2.0 * step_index / (2 * half_dim))
    angles = positions.astype(f32)[:, None] * frequency[None, :]
    return (jnp.cos(angles), jnp.sin(angles))


def rotate(tensor, cosine_tab, sine_tab):
    half_dim = tensor.shape[-1] // 2
    first_half, second_half = (tensor[..., :half_dim], tensor[..., half_dim:])
    cosine_b, sine_b = (cosine_tab[:, None, :], sine_tab[:, None, :])
    return jnp.concatenate(
        [
            first_half * cosine_b - second_half * sine_b,
            second_half * cosine_b + first_half * sine_b,
        ],
        -1,
    )


def dot(left, right):
    return jnp.dot(left, right, preferred_element_type=f32)


def dot_lt(left, right):
    return lax.dot_general(left, right, (((0,), (0,)), ((), ())), preferred_element_type=f32)


def dot_rt(left, right):
    return lax.dot_general(left, right, (((1,), (1,)), ((), ())), preferred_element_type=f32)


def on_device(
    block_in,
    span_order,
    attn_gain,
    w_query,
    w_key,
    w_value,
    w_out,
    mlp_gain,
    w_gate,
    w_up,
    w_down,
    clip_limit,
    cotangent,
):
    n_ctx = lax.axis_size("ctx")
    n_fsdp = lax.axis_size("fsdp")
    n_bits = n_fsdp.bit_length() - 1
    c_at = lax.axis_index("ctx")
    f_at = lax.axis_index("fsdp")
    t_at = lax.axis_index("tp")
    row_count, width = block_in.shape[1:]
    span_len = row_count // 2
    feature_block = width // n_fsdp
    score_scale = HEAD_DIM ** (-0.5)

    def along(tensor, shift):
        if shift % n_ctx == 0:
            return tensor
        return lax.ppermute(tensor, "ctx", [(i, (i + shift) % n_ctx) for i in range(n_ctx)])

    def across(tensor, mask):
        return lax.ppermute(tensor, "fsdp", [(i, i ^ mask) for i in range(n_fsdp)])

    def twin(tensor):
        return lax.ppermute(tensor, "tp", [(0, 1), (1, 0)])

    def bit_order(part):
        return [1 << ((part + step) % n_bits) for step in range(n_bits)]

    def part_count(size):
        return n_bits if size % n_bits == 0 else 1

    def reorder(tensor):
        return jnp.concatenate(
            [
                lax.dynamic_slice_in_dim(tensor, (f_at ^ m) * feature_block, feature_block, -1)
                for m in range(n_fsdp)
            ],
            -1,
        )

    def swap_ctx(tensor, split_axis, place_axis):
        piece = tensor.shape[split_axis] // n_ctx
        length = tensor.shape[place_axis]
        shape = list(tensor.shape)
        shape[split_axis] = piece
        shape[place_axis] = length * n_ctx
        placed = jnp.zeros(shape, tensor.dtype)
        for shift in range(n_ctx):
            sent = lax.dynamic_slice_in_dim(
                tensor, ((c_at + shift) % n_ctx) * piece, piece, split_axis
            )
            came = along(sent, shift)
            placed = lax.dynamic_update_slice_in_dim(
                placed, came, ((c_at - shift) % n_ctx) * length, place_axis
            )
        return placed

    def swap_ctx_low(tensor, split_axis, place_axis):
        piece = tensor.shape[split_axis] // n_ctx
        length = tensor.shape[place_axis]
        shape = list(tensor.shape)
        shape[split_axis] = piece
        shape[place_axis] = length * n_ctx
        placed = jnp.zeros(shape, f32)
        for shift in range(n_ctx):
            sent = lax.dynamic_slice_in_dim(
                tensor, ((c_at + shift) % n_ctx) * piece, piece, split_axis
            )
            came = along(sent.astype(bf16), shift).astype(f32) if shift else sent
            placed = lax.dynamic_update_slice_in_dim(
                placed, came, ((c_at - shift) % n_ctx) * length, place_axis
            )
        return placed

    def gather_plane(tensor, axis):
        other = 1 - axis
        parts = part_count(tensor.shape[other])
        part_size = tensor.shape[other] // parts
        done = []
        for part in range(parts):
            held = {0: lax.slice_in_dim(tensor, part * part_size, (part + 1) * part_size, axis=other)}
            for bit in bit_order(part):
                keys = sorted(held)
                came = across(jnp.concatenate([held[k] for k in keys], axis) if len(keys) > 1 else held[keys[0]], bit)
                size = tensor.shape[axis]
                for at, k in enumerate(keys):
                    held[k ^ bit] = lax.slice_in_dim(came, at * size, (at + 1) * size, axis=axis)
            done.append(jnp.concatenate([held[m] for m in range(n_fsdp)], axis))
        return jnp.concatenate(done, other)

    def scatter_plane(tensor, axis):
        other = 1 - axis
        parts = part_count(tensor.shape[other])
        part_size = tensor.shape[other] // parts
        size = tensor.shape[axis] // n_fsdp
        done = []
        for part in range(parts):
            own = lax.slice_in_dim(tensor, part * part_size, (part + 1) * part_size, axis=other)
            held = {m: lax.slice_in_dim(own, m * size, (m + 1) * size, axis=axis) for m in range(n_fsdp)}
            for bit in bit_order(part):
                kept = [m for m in sorted(held) if not m & bit]
                sent = [held[m | bit].astype(bf16) for m in kept]
                came = across(jnp.concatenate(sent, axis) if len(sent) > 1 else sent[0], bit)
                held = {
                    m: held[m] + lax.slice_in_dim(came, at * size, (at + 1) * size, axis=axis).astype(f32)
                    for at, m in enumerate(kept)
                }
            done.append(held[0])
        return jnp.concatenate(done, other)

    def gather_tokens(own):
        spans, held = [], own
        for step in range(n_ctx):
            if step:
                held = along(held, 1)
            spans += [held, twin(held)]
        return jnp.concatenate(spans, 0)

    def scatter_tokens(partial):
        spans = partial.reshape(n_ctx, 2, span_len, width)
        total = None
        for slot in list(range(1, n_ctx)) + [0]:
            mine = spans[slot, 0] + twin(spans[slot, 1].astype(bf16)).astype(f32)
            total = mine if total is None else mine + along(total.astype(bf16), 1).astype(f32)
        return total

    order_row = span_order[0]
    slot_spans = jnp.stack(
        [order_row[2 * ((c_at - s) % n_ctx) + (t_at ^ u)] for s in range(n_ctx) for u in range(2)]
    )
    positions = (
        slot_spans[:, None] * span_len + jnp.arange(span_len, dtype=jnp.int32)[None, :]
    ).reshape(-1)
    causal_mask = positions[None, :] <= positions[:, None]
    cosine, sine = rope_tables(positions, HEAD_DIM // 2)
    length = positions.shape[0]

    def own_rows(tensor):
        return reorder(lax.dynamic_slice_in_dim(tensor[0], t_at * span_len, span_len, 0))

    inputs_own = own_rows(block_in)
    cot_own = own_rows(cotangent)

    inputs_low = gather_tokens(inputs_own)

    gains = jnp.stack([attn_gain, mlp_gain])
    gains = gather_plane_small(swap_small(gains, along, c_at, n_ctx), across, n_bits)
    gain_one, gain_two = gains[0].astype(f32), gains[1].astype(f32)

    heads_width = w_query.shape[1] // n_ctx
    qkv = jnp.stack([w_query, w_key, w_value], 1)
    rows_here = w_query.shape[0]
    qkv = qkv.reshape(rows_here, 3, n_ctx, heads_width).transpose(0, 2, 1, 3).reshape(rows_here, -1)
    qkv_full = gather_plane(swap_ctx(qkv, 1, 0), 0)
    out_full = gather_plane(swap_ctx(w_out, 0, 1), 1)
    gate_full = gather_plane(swap_ctx(w_gate, 1, 0), 0)
    up_full = gather_plane(swap_ctx(w_up, 1, 0), 0)
    down_full = gather_plane(swap_ctx(w_down, 0, 1), 1)
    cot_all = gather_tokens(cot_own)

    inputs = inputs_low.astype(f32)
    inv_one = lax.rsqrt(jnp.mean(inputs * inputs, -1, keepdims=True) + NORM_EPS)
    normed_one = (inputs * inv_one * gain_one).astype(bf16)
    heads_here = heads_width // HEAD_DIM
    proj = dot(normed_one, qkv_full)

    def heads_first(tensor):
        return tensor.reshape(length, heads_here, HEAD_DIM).transpose(1, 0, 2)

    def heads_last(tensor):
        return tensor.transpose(1, 0, 2).reshape(length, heads_width)

    def turned(tensor, sine_tab):
        return rotate(tensor.reshape(length, heads_here, HEAD_DIM), cosine, sine_tab)

    query = turned(proj[:, :heads_width], sine).astype(bf16).transpose(1, 0, 2)
    key = turned(proj[:, heads_width : 2 * heads_width], sine).astype(bf16).transpose(1, 0, 2)
    value = heads_first(proj[:, 2 * heads_width :].astype(bf16))

    def forward_head(operands):
        query_h, key_h, value_h = operands
        scores = dot_rt(query_h, key_h) * score_scale
        masked = jnp.where(causal_mask, scores, -1e30)
        row_max = jnp.max(masked, axis=1, keepdims=True)
        exp_terms = jnp.exp(masked - row_max)
        row_total = jnp.sum(exp_terms, axis=1, keepdims=True)
        attended = dot((exp_terms / row_total).astype(bf16), value_h)
        return (attended.astype(bf16), row_max[:, 0] + jnp.log(row_total[:, 0]), jnp.max(row_max))

    attended, log_total, head_max = lax.map(forward_head, (query, key, value))
    attn_low = heads_last(attended)
    attn_sum = scatter_tokens(dot(attn_low, out_full))

    peak = head_max
    for step in range(n_bits):
        peak = jnp.maximum(peak, across(peak, 1 << step))
    head_peak = jnp.zeros((n_ctx * heads_here,), f32)
    for shift in range(n_ctx):
        head_peak = lax.dynamic_update_slice_in_dim(
            head_peak, along(peak, shift), ((c_at - shift) % n_ctx) * heads_here, 0
        )

    inputs_mine = inputs_own.astype(f32)
    resid = inputs_mine + attn_sum
    inv_two = lax.rsqrt(jnp.mean(resid * resid, -1, keepdims=True) + NORM_EPS)
    scaled_two = resid * inv_two
    normed_two = gather_tokens((scaled_two * gain_two).astype(bf16))
    gate_act = dot(normed_two, gate_full)
    up_act = dot(normed_two, up_full)
    sig_gate = jax.nn.sigmoid(gate_act)
    silu_gate = gate_act * sig_gate
    hidden = (silu_gate * up_act).astype(bf16)
    grad_hidden = dot_rt(cot_all, down_full)
    silu_slope = sig_gate * (1.0 + gate_act * (1.0 - sig_gate))
    grad_gate = (grad_hidden * up_act * silu_slope).astype(bf16)
    grad_up = (grad_hidden * silu_gate).astype(bf16)
    grad_normed_two = scatter_tokens(dot_rt(grad_gate, gate_full) + dot_rt(grad_up, up_full))
    mlp_sum = scatter_tokens(dot(hidden, down_full))
    block_out_mine = (resid + mlp_sum).astype(bf16)

    grad_gain_two = jnp.sum(grad_normed_two * scaled_two, axis=0)
    weighted_two = grad_normed_two * gain_two
    grad_resid = cot_own.astype(f32) + inv_two * (
        weighted_two - scaled_two * jnp.mean(weighted_two * scaled_two, -1, keepdims=True)
    )
    grad_low = gather_tokens(grad_resid.astype(bf16))

    def own_weight(grad, axis):
        return swap_ctx_low(scatter_plane(grad, axis), axis, 1 - axis)

    down_out = own_weight(dot_lt(hidden, cot_all), 1)
    gate_out = own_weight(dot_lt(normed_two, grad_gate), 0)
    up_out = own_weight(dot_lt(normed_two, grad_up), 0)

    grad_attended = heads_first(dot_rt(grad_low, out_full).astype(bf16))
    out_proj_out = own_weight(dot_lt(attn_low, grad_low), 1)

    def backward_head(operands):
        query_h, key_h, value_h, grad_h, log_h = operands
        scores = dot_rt(query_h, key_h) * score_scale
        masked = jnp.where(causal_mask, scores, -1e30)
        probabilities = jnp.exp(masked - log_h[:, None])
        grad_probs = dot_rt(grad_h, value_h)
        row_delta = jnp.sum(probabilities * grad_probs, axis=1, keepdims=True)
        grad_scores = (probabilities * (grad_probs - row_delta)).astype(bf16)
        return (
            dot(grad_scores, key_h) * score_scale,
            dot_lt(grad_scores, query_h) * score_scale,
            dot_lt(probabilities.astype(bf16), grad_h).astype(bf16),
        )

    grad_query, grad_key, grad_value = lax.map(
        backward_head, (query, key, value, grad_attended, log_total)
    )
    grad_proj = jnp.concatenate(
        [
            rotate(grad_query.transpose(1, 0, 2), cosine, -sine).reshape(length, heads_width).astype(bf16),
            rotate(grad_key.transpose(1, 0, 2), cosine, -sine).reshape(length, heads_width).astype(bf16),
            heads_last(grad_value),
        ],
        1,
    )
    grad_normed_one = scatter_tokens(dot_rt(grad_proj, qkv_full))
    grad_qkv = scatter_plane(dot_lt(normed_one, grad_proj), 0)
    query_out, key_out, value_out = (
        swap_ctx_low(grad_qkv[:, i * heads_width : (i + 1) * heads_width], 0, 1) for i in range(3)
    )

    inv_mine = lax.rsqrt(jnp.mean(inputs_mine * inputs_mine, -1, keepdims=True) + NORM_EPS)
    scaled_one = inputs_mine * inv_mine
    grad_gain_one = jnp.sum(grad_normed_one * scaled_one, axis=0)
    weighted_one = grad_normed_one * gain_one
    input_grad_mine = grad_resid + inv_mine * (
        weighted_one - scaled_one * jnp.mean(weighted_one * scaled_one, -1, keepdims=True)
    )

    gain_grads = jnp.stack([grad_gain_one, grad_gain_two])
    gain_grads = gain_grads + twin(gain_grads)
    held = {m: gain_grads[:, m * feature_block : (m + 1) * feature_block] for m in range(n_fsdp)}
    for bit in bit_order(0):
        kept = [m for m in sorted(held) if not m & bit]
        came = across(jnp.concatenate([held[m | bit] for m in kept], 1), bit)
        held = {
            m: held[m] + came[:, at * feature_block : (at + 1) * feature_block]
            for at, m in enumerate(kept)
        }
    piece = feature_block // n_ctx
    gain_total = None
    for shift in range(n_ctx):
        came = along(
            lax.dynamic_slice_in_dim(held[0], ((c_at + shift) % n_ctx) * piece, piece, 1), shift
        )
        gain_total = came if gain_total is None else gain_total + came

    def both_cores(mine):
        mine = reorder(mine)
        other = twin(mine)
        first = jnp.where(t_at == 0, mine, other)
        second = jnp.where(t_at == 0, other, mine)
        return jnp.concatenate([first, second], 0)[None]

    factor = jnp.sqrt(clip_limit / jnp.maximum(clip_limit, head_peak))
    column_factor = jnp.repeat(factor, HEAD_DIM)
    clipped_query = w_query.astype(f32) * column_factor[None, :]
    clipped_key = w_key.astype(f32) * column_factor[None, :]
    return (
        both_cores(block_out_mine),
        both_cores(input_grad_mine),
        gain_total[0],
        query_out,
        key_out,
        value_out,
        out_proj_out,
        gain_total[1],
        gate_out,
        up_out,
        down_out,
        head_peak,
        clipped_query,
        clipped_key,
    )


def swap_small(gains, along, c_at, n_ctx):
    piece = gains.shape[1]
    placed = jnp.zeros((gains.shape[0], piece * n_ctx), gains.dtype)
    for shift in range(n_ctx):
        placed = lax.dynamic_update_slice_in_dim(
            placed, along(gains, shift), ((c_at - shift) % n_ctx) * piece, 1
        )
    return placed


def gather_plane_small(gains, across, n_bits):
    for step in range(n_bits):
        gains = jnp.concatenate([gains, across(gains, 1 << step)], 1)
    return gains


def solution(mesh):
    placed = (
        P("fsdp", "ctx", None),
        P("fsdp", None),
        P(("fsdp", "ctx")),
        P(("fsdp", "ctx"), "tp"),
        P(("fsdp", "ctx"), "tp"),
        P(("fsdp", "ctx"), "tp"),
        P("tp", ("fsdp", "ctx")),
        P(("fsdp", "ctx")),
        P(("fsdp", "ctx"), "tp"),
        P(("fsdp", "ctx"), "tp"),
        P("tp", ("fsdp", "ctx")),
        P("tp"),
        P("fsdp", "ctx", None),
    )
    return jax.shard_map(
        on_device,
        mesh=mesh,
        in_specs=placed,
        out_specs=(
            P("fsdp", "ctx", None),
            P("fsdp", "ctx", None),
            P(("fsdp", "ctx")),
            P(("fsdp", "ctx"), "tp"),
            P(("fsdp", "ctx"), "tp"),
            P(("fsdp", "ctx"), "tp"),
            P("tp", ("fsdp", "ctx")),
            P(("fsdp", "ctx")),
            P(("fsdp", "ctx"), "tp"),
            P(("fsdp", "ctx"), "tp"),
            P("tp", ("fsdp", "ctx")),
            P("tp"),
            P(("fsdp", "ctx"), "tp"),
            P(("fsdp", "ctx"), "tp"),
        ),
        check_vma=False,
    )
```

time: 4260 us -> 1010 us (0.24)
  waiting for transfers between devices: 3700 us -> 531 us
  blocking collectives: 202 us -> 0 us
  starting transfers between devices: 1.81 us -> 133 us
  matrix products: 264 us -> 176 us
  local copies, waits for them, and re-layouts: 33.8 us -> 94.3 us
    reduce_scatter x9 -> x0, waiting for transfers between devices: 2770 us -> none  [the longest x1 692 us: on_device(): lax.psum_scatter(grad_down, ('fsdp', 'ctx'), scatter_dimension=1, tiled=T...]
    all_gather x9 -> x0, waiting for transfers between devices: 895 us -> none  [the longest x1 238 us: on_device(): lax.all_gather(w_down, ('fsdp', 'ctx'), axis=1, tiled=True)]
    ppermute x0 -> x150, waiting for transfers between devices: none -> 531 us  [the longest x69 272 us: along(): lax.ppermute(tensor, 'ctx', [(i, (i + shift) % n_ctx) for i in range(n_ct...]
    ppermute x0 -> x150, starting transfers between devices: none -> 133 us  [the longest x69 79.8 us: along(): lax.ppermute(tensor, 'ctx', [(i, (i + shift) % n_ctx) for i in range(n_ct...]
    dot_general x77 -> x43, matrix products: 264 us -> 176 us  [the longest x17 84.5 us: dot_rt(): lax.dot_general(left, right, (((1,), (1,)), ((), ())), preferred_element_...]
    all_gather x2 -> x0, blocking collectives: 80.3 us -> none  [the longest x1 42.4 us: on_device(): lax.all_gather(attn_gain, ('fsdp', 'ctx'), axis=0, tiled=True)]
    unnamed x1 -> x0, blocking collectives: 77.7 us -> none
    pmax x1 -> x0, blocking collectives: 44.1 us -> none  [on_device(): head_peak = lax.pmax(head_max.reshape(heads_here), ('fsdp', 'ctx'))]
  transfers between devices with their start and end apart: 22 -> 150, of which waited for: 19 -> 73; matrix products, arithmetic and copies ran while one was open for 5% -> 20% of each run, Pallas kernels for 0% -> 0%
where the time goes in v1:
time: 1010 us; the launch traced here: 1000 us
  waiting for transfers between devices  531 us (53%)
  matrix products  176 us (17%)
  starting transfers between devices  133 us (13%)
  local copies, waits for them, and re-layouts  94.3 us (9%)
  other arithmetic  60 us (6%)
    ppermute x69, waiting for transfers between devices, along(): lax.ppermute(tensor, 'ctx', [(i, (i + shift) % n_ctx) for i in range(n_ct...  272 us
    ppermute x46, waiting for transfers between devices, across(): return lax.ppermute(tensor, 'fsdp', [(i, i ^ mask) for i in range(n_fsdp)])  255 us
    dot_general x17, matrix products, dot_rt(): lax.dot_general(left, right, (((1,), (1,)), ((), ())), preferred_element_...  84.5 us
    ppermute x69, starting transfers between devices, along(): lax.ppermute(tensor, 'ctx', [(i, (i + shift) % n_ctx) for i in range(n_ct...  79.8 us
    dot_general x13, matrix products, dot(): return jnp.dot(left, right, preferred_element_type=f32)  52.9 us
    ppermute x46, starting transfers between devices, across(): return lax.ppermute(tensor, 'fsdp', [(i, i ^ mask) for i in range(n_fsdp)])  48.1 us
    dot_general x13, matrix products, dot_lt(): lax.dot_general(left, right, (((0,), (0,)), ((), ())), preferred_element_...  39.1 us
    unnamed x256, local copies, waits for them, and re-layouts  25.5 us
  transfers between devices with their start and end apart: 150, of which 73 were waited for; matrix products, arithmetic and copies ran while one was open for 20% of the time, Pallas kernels for 0%

profile of v1, /device:TPU:0, one launch (start us, length us, event | category | flops | bytes accessed | tf_op | source)
XLA Modules:
  0.0 999.6 jit_solution(15008404697120905223)
XLA Ops:
  65.6 10.5 %collective-permute-done.13 = bf16[128,768]{0,1:T(8,128)(2,1)S(1)} collective-permute-done((bf16[128,768]{0,1:T(8,128)(2,1)}, bf16[128,768]{0,1:T(8,128)(2,1)S(1)}, u32[]{:S(2)}, u32[]{:S(2)}) %collective-permute-start.13) | collective-permute-done | bytes 196640 | tf_op jit(solution)/shard_map/ppermute | solution.py:75
  80.8 10.4 %collective-permute-start.47 = (bf16[128,1024]{1,0:T(8,128)(2,1)S(1)}, bf16[128,1024]{1,0:T(8,128)(2,1)S(1)}, u32[]{:S(2)}, u32[]{:S(2)}) collective-permute-start(bf16[128,1024]{1,0:T(8,128)(2,1)S(1)} %copy-done.92), channel_id=1, source_target_pairs={{0,2},{2,4},{4,6},{6,0},{1,3},{3,5},{5,7},{7,1},{8,10},{10,12},{12... | collective-permute-start | bytes 786440 | tf_op jit(solution)/shard_map/ppermute | solution.py:75
  98.9 18.4 %collective-permute-start.40 = (bf16[128,1024]{1,0:T(8,128)(2,1)S(1)}, bf16[128,1024]{1,0:T(8,128)(2,1)S(1)}, u32[]{:S(2)}, u32[]{:S(2)}) collective-permute-start(bf16[128,1024]{1,0:T(8,128)(2,1)S(1)} %copy-done.90), channel_id=1, source_target_pairs={{0,2},{2,4},{4,6},{6,0},{1,3},{3,5},{5,7},{7,1},{8,10},{10,12},{12... | collective-permute-start | bytes 786440 | tf_op jit(solution)/shard_map/ppermute | solution.py:75
  118.2 7.0 collective-permute-done.48
  135.7 16.1 %collective-permute-done.42 = bf16[128,1024]{1,0:T(8,128)(2,1)S(1)} collective-permute-done((bf16[128,1024]{1,0:T(8,128)(2,1)}, bf16[128,1024]{1,0:T(8,128)(2,1)S(1)}, u32[]{:S(2)}, u32[]{:S(2)}) %collective-permute-start.42) | collective-permute-done | bytes 262176 | tf_op jit(solution)/shard_map/ppermute | solution.py:75
  175.5 7.6 collective-permute-done.59
  186.1 6.4 collective-permute-done.18
  199.7 22.9 %collective-permute-done.16 = bf16[1024,384]{0,1:T(8,128)(2,1)S(1)} collective-permute-done((bf16[1024,384]{0,1:T(8,128)(2,1)S(1)}, bf16[1024,384]{0,1:T(8,128)(2,1)S(1)}, u32[]{:S(2)}, u32[]{:S(2)}) %collective-permute-start.16) | collective-permute-done | bytes 786464 | tf_op jit(solution)/shard_map/ppermute | solution.py:78
  232.8 30.0 %while.30 = (s32[]{:T(128)}, bf16[4,1024,64]{1,2,0:T(8,128)(2,1)S(1)}, f32[4,1024]{1,0:T(4,128)}, f32[4]{0:T(128)}, bf16[4,1024,64]{2,1,0:T(8,128)(2,1)S(1)}, /*...) while((s32[]{:T(128)}, ...), condition=%wide.region_5.6_spmd.clone, body=%wide.region_1.5_spmd.clone.sunk | while | flops 278985728 | bytes 13551745 | solution.py:247
  280.7 7.7 collective-permute-done.72
  288.6 11.1 %collective-permute-done.30 = bf16[128,2048]{1,0:T(8,128)(2,1)S(1)} collective-permute-done((bf16[128,2048]{1,0:T(8,128)(2,1)S(1)}, bf16[128,2048]{1,0:T(8,128)(2,1)S(1)}, u32[]{:S(2)}, u32[]{:S(2)}) %collective-permute-start.30) | collective-permute-done | bytes 524320 | tf_op jit(solution)/shard_map/ppermute | solution.py:75
  300.5 10.4 %collective-permute-done.74 = bf16[128,2048]{1,0:T(8,128)(2,1)S(1)} collective-permute-done((bf16[128,2048]{1,0:T(8,128)(2,1)S(1)}, bf16[128,2048]{1,0:T(8,128)(2,1)S(1)}, u32[]{:S(2)}, u32[]{:S(2)}) %collective-permute-start.74) | collective-permute-done | bytes 524320 | tf_op jit(solution)/shard_map/ppermute | solution.py:75
  312.9 8.4 collective-permute-done.31
  323.1 21.0 %collective-permute-done.46 = bf16[1024,512]{1,0:T(8,128)(2,1)S(1)} collective-permute-done((bf16[1024,512]{1,0:T(8,128)(2,1)S(1)}, bf16[1024,512]{1,0:T(8,128)(2,1)S(1)}, u32[]{:S(2)}, u32[]{:S(2)}) %collective-permute-start.46) | collective-permute-done | bytes 1048608 | tf_op jit(solution)/shard_map/ppermute | solution.py:78
  351.2 23.9 %fusion.179 = f32[1024,1024]{1,0:T(8,128)} fusion(bf16[1024,2048]{1,0:T(8,128)(2,1)S(1)} %constant_dynamic-update-slice_fusion.16, bf16[512,512]{1,0:T(8,128)(2,1)S(1)} %get-tuple-element.332, bf16[512,512]{1,0:T(8,128)(2,1)S(1)} %copy-done.65, bf16[512,512]{1,0:T(8,128)(2,1)S(1)} %get-tuple-element.331, bf16[512,512]{1,0:T(8,128)(2,1)S(1)} %copy-done.22, ...), kind=kOutput, calls=%fused_computation.482 | convolution fusion | flops 4324327424 | bytes 12582912 | tf_op jit(solution)/shard_map/dot_general | solution.py:43
  376.2 15.2 %collective-permute-done.146 = f32[4]{0:T(128)S(1)} collective-permute-done((f32[4]{0:T(128)S(1)}, f32[4]{0:T(128)S(1)}, u32[]{:S(2)}, u32[]{:S(2)}) %collective-permute-start.146) | collective-permute-done | bytes 48 | tf_op jit(solution)/shard_map/ppermute | solution.py:78
  411.5 11.2 %collective-permute-done.38 = bf16[128,2048]{1,0:T(8,128)(2,1)S(1)} collective-permute-done((bf16[128,2048]{1,0:T(8,128)(2,1)}, bf16[128,2048]{1,0:T(8,128)(2,1)S(1)}, u32[]{:S(2)}, u32[]{:S(2)}) %collective-permute-start.38) | collective-permute-done | bytes 524320 | tf_op jit(solution)/shard_map/ppermute | solution.py:75
  427.2 13.1 %fusion.182 = f32[1024,1024]{1,0:T(8,128)} fusion(bf16[1024,2048]{1,0:T(8,128)(2,1)} %constant_dynamic-update-slice_fusion.8, bf16[512,512]{1,0:T(8,128)(2,1)S(1)} %copy-done.74, bf16[512,512]{1,0:T(8,128)(2,1)} %collective-permute-done.52, bf16[512,512]{1,0:T(8,128)(2,1)S(1)} %copy-done.73, bf16[512,512]{1,0:T(8,128)(2,1)} %get-tuple-element.346, ...), kind=kOutput, calls=%fused_computation.485 | convolution fusion | flops 4324327424 | bytes 12582912 | tf_op jit(solution)/shard_map/dot_general | solution.py:35
  440.4 15.8 %multiply_convert_fusion.2 = (bf16[1024,1024]{1,0:T(8,128)(2,1)S(1)}, bf16[1024,1024]{1,0:T(8,128)(2,1)}, bf16[1024,1024]{1,0:T(8,128)(2,1)S(1)}) fusion(f32[1024,1024]{1,0:T(8,128)} %fusion.179, f32[1024,1024]{1,0:T(8,128)} %fusion.182, bf16[1024,2048]{1,0:T(8,128)(2,1)S(1)} %copy-done.97, bf16[512,512]{1,0:T(8,128)(2,1)S(1)} %copy-done.76, ...), kind=kOutput, calls=%fused_computation.63 | convolution fusion | flops 4340056064 | bytes 23068672 | tf_op jit(solution)/shard_map/dot_general | solution.py:35
  456.1 7.1 fusion.206
  465.2 7.6 fusion.207
  472.7 15.4 %fusion.181 = f32[1024,2048]{1,0:T(8,128)} fusion(bf16[1024,1024]{1,0:T(8,128)(2,1)S(1)} %copy-done.110, bf16[512,512]{1,0:T(8,128)(2,1)S(1)} %copy-done.74, bf16[512,512]{1,0:T(8,128)(2,1)} %collective-permute-done.52, bf16[512,512]{1,0:T(8,128)(2,1)S(1)} %copy-done.73, bf16[512,512]{1,0:T(8,128)(2,1)} %get-tuple-element.346, ...), kind=kOutput, calls=%fused_computation.484 | convolution fusion | flops 4324327424 | bytes 14680064 | tf_op jit(solution)/shard_map/dot_general | solution.py:43
  488.1 22.2 %bitcast_convert_fusion = (bf16[4,2,128,2048]{3,2,1,0:T(8,128)(2,1)S(1)}, f32[1024,2048]{1,0:T(8,128)}) fusion(f32[1024,2048]{1,0:T(8,128)} %fusion.181, bf16[1024,1024]{1,0:T(8,128)(2,1)} %copy-done.109, bf16[512,512]{1,0:T(8,128)(2,1)S(1)} %copy-done.76, bf16[512,512]{1,0:T(8,128)(2,1)} %collective-permute-done.45, bf16[512,512]{1,0:T(8,128)(2,1)S(1)} %copy-done.75, ...), kind=kOutput, calls=%fused_computation.479 | convolution fusion | flops 4328521728 | bytes 27262976 | tf_op jit(solution)/shard_map/dot_general | solution.py:43
  513.2 6.3 fusion.208
  533.7 14.0 %collective-permute-done.80 = bf16[128,2048]{1,0:T(8,128)(2,1)S(1)} collective-permute-done((bf16[128,2048]{1,0:T(8,128)(2,1)S(1)}, bf16[128,2048]{1,0:T(8,128)(2,1)S(1)}, u32[]{:S(2)}, u32[]{:S(2)}) %collective-permute-start.80) | collective-permute-done | bytes 524320 | tf_op jit(solution)/shard_map/ppermute | solution.py:75
  556.3 6.8 collective-permute-done.65
  563.9 12.4 %collective-permute-done.133 = bf16[1024,512]{1,0:T(8,128)(2,1)S(1)} collective-permute-done((bf16[1024,512]{1,0:T(8,128)(2,1)S(1)}, bf16[1024,512]{1,0:T(8,128)(2,1)S(1)}, u32[]{:S(2)}, u32[]{:S(2)}) %collective-permute-start.133) | collective-permute-done | bytes 1048608 | tf_op jit(solution)/shard_map/ppermute | solution.py:78
  576.5 21.3 %collective-permute-done.140 = bf16[512,1024]{1,0:T(8,128)(2,1)S(1)} collective-permute-done((bf16[512,1024]{1,0:T(8,128)(2,1)S(1)}, bf16[512,1024]{1,0:T(8,128)(2,1)S(1)}, u32[]{:S(2)}, u32[]{:S(2)}) %collective-permute-start.140) | collective-permute-done | bytes 1048608 | tf_op jit(solution)/shard_map/ppermute | solution.py:78
  602.2 10.5 %collective-permute-done.66 = bf16[128,2048]{1,0:T(8,128)(2,1)S(1)} collective-permute-done((bf16[128,2048]{1,0:T(8,128)(2,1)S(1)}, bf16[128,2048]{1,0:T(8,128)(2,1)S(1)}, u32[]{:S(2)}, u32[]{:S(2)}) %collective-permute-start.66) | collective-permute-done | bytes 524320 | tf_op jit(solution)/shard_map/ppermute | solution.py:75
  613.5 44.4 %collective-permute-done.127 = bf16[512,512]{1,0:T(8,128)(2,1)S(1)} collective-permute-done((bf16[512,512]{1,0:T(8,128)(2,1)S(1)}, bf16[512,512]{1,0:T(8,128)(2,1)S(1)}, u32[]{:S(2)}, u32[]{:S(2)}) %collective-permute-start.127) | collective-permute-done | bytes 524320 | tf_op jit(solution)/shard_map/ppermute | solution.py:78
  660.7 8.5 collective-permute-done.134
  669.6 8.9 collective-permute-done.141
  682.0 6.2 collective-permute-done.67
  695.6 9.1 collective-permute-done.132
  705.2 7.8 collective-permute-done.139
  724.4 13.1 %collective-permute-done.129 = bf16[128,1024]{1,0:T(8,128)(2,1)S(1)} collective-permute-done((bf16[128,1024]{1,0:T(8,128)(2,1)S(1)}, bf16[128,1024]{1,0:T(8,128)(2,1)S(1)}, u32[]{:S(2)}, u32[]{:S(2)}) %collective-permute-start.129) | collective-permute-done | bytes 262176 | tf_op jit(solution)/shard_map/ppermute | solution.py:75
  749.4 6.3 collective-permute-done.137
  763.1 8.7 collective-permute-done.143
  780.8 14.1 %collective-permute-done.86 = bf16[128,2048]{1,0:T(8,128)(2,1)S(1)} collective-permute-done((bf16[128,2048]{1,0:T(8,128)(2,1)S(1)}, bf16[128,2048]{1,0:T(8,128)(2,1)S(1)}, u32[]{:S(2)}, u32[]{:S(2)}) %collective-permute-start.86) | collective-permute-done | bytes 524320 | tf_op jit(solution)/shard_map/ppermute | solution.py:75
  795.1 15.3 %collective-permute-done.88 = bf16[128,2048]{1,0:T(8,128)(2,1)S(1)} collective-permute-done((bf16[128,2048]{1,0:T(8,128)(2,1)S(1)}, bf16[128,2048]{1,0:T(8,128)(2,1)S(1)}, u32[]{:S(2)}, u32[]{:S(2)}) %collective-permute-start.88) | collective-permute-done | bytes 524320 | tf_op jit(solution)/shard_map/ppermute | solution.py:75
  821.5 36.5 %while.31 = (s32[]{:T(128)}, f32[4,1024,64]{1,2,0:T(8,128)}, f32[4,1024,64]{1,2,0:T(8,128)}, bf16[4,1024,64]{1,2,0:T(8,128)(2,1)}, bf16[4,1024,64]{2,1,0:T(8,128...) while((s32[]{:T(128)}, f32[4,1024,64]{1,2,0:T(8,128)}, ...), condition=%wide.region_11.12_spmd.clone, body=%wide.region_9.11_spmd.clone.sunk | while | flops 681769984 | bytes 33981560 | solution.py:309
  872.0 7.4 collective-permute-done.119
  885.7 16.0 %collective-permute-done.118 = bf16[128,512]{1,0:T(8,128)(2,1)S(1)} collective-permute-done((bf16[128,512]{1,0:T(8,128)(2,1)S(1)}, bf16[128,512]{1,0:T(8,128)(2,1)S(1)}, u32[]{:S(2)}, u32[]{:S(2)}) %collective-permute-start.118) | collective-permute-done | bytes 131104 | tf_op jit(solution)/shard_map/ppermute | solution.py:78
  901.9 6.0 collective-permute-done.121
  919.9 16.2 %collective-permute-done.104 = bf16[1024,384]{1,0:T(8,128)(2,1)S(1)} collective-permute-done((bf16[1024,384]{1,0:T(8,128)(2,1)S(1)}, bf16[1024,384]{1,0:T(8,128)(2,1)S(1)}, u32[]{:S(2)}, u32[]{:S(2)}) %collective-permute-start.104) | collective-permute-done | bytes 786464 | tf_op jit(solution)/shard_map/ppermute | solution.py:78
  942.0 6.7 collective-permute-done.114
  948.7 9.5 collective-permute-done.115
  968.7 6.5 collective-permute-done.106
  (791 shorter events, 424.0 us)
Async XLA Ops:
  2.5 159.1 %collective-permute-start = (bf16[128,2048]{1,0:T(8,128)(2,1)S(1)}, bf16[128,2048]{1,0:T(8,128)(2,1)}, u32[]{:S(2)}, u32[]{:S(2)}) collective-permute-start(bf16[128,2048]{1,0:T(8,128)(2,1)S(1)} %get-tuple-element.244), channel_id=1, source_target_pairs={{0,1},{1,0},{2,3},{3,2},{4,5},{5,4},{6,7},{7,6},{8,9},{9,8},{10,11... | collective-permute-start | bytes 1572872 | tf_op jit(solution)/shard_map/ppermute | solution.py:81
  3.0 161.2 %collective-permute-start.1 = (bf16[128,2048]{1,0:T(8,128)(2,1)S(1)}, bf16[128,2048]{1,0:T(8,128)(2,1)}, u32[]{:S(2)}, u32[]{:S(2)}) collective-permute-start(bf16[128,2048]{1,0:T(8,128)(2,1)S(1)} %get-tuple-element.244), channel_id=1, source_target_pairs={{0,2},{2,4},{4,6},{6,0},{1,3},{3,5},{5,7},{7,1},{8,10},{10,12},{12... | collective-permute-start | bytes 1572872 | tf_op jit(solution)/shard_map/ppermute | solution.py:75
  6.3 29.6 %collective-permute-start.7 = (bf16[2,128]{1,0:T(2,128)(2,1)S(1)}, bf16[2,128]{1,0:T(2,128)(2,1)}, u32[]{:S(2)}, u32[]{:S(2)}) collective-permute-start(bf16[2,128]{1,0:T(2,128)(2,1)S(1)} %get-tuple-element.250), channel_id=1, source_target_pairs={{0,2},{2,4},{4,6},{6,0},{1,3},{3,5},{5,7},{7,1},{8,10},{10,12},{12... | collective-permute-start | bytes 1544 | tf_op jit(solution)/shard_map/ppermute | solution.py:75
  7.9 28.6 %collective-permute-start.8 = (bf16[2,128]{1,0:T(2,128)(2,1)S(1)}, bf16[2,128]{1,0:T(2,128)(2,1)}, u32[]{:S(2)}, u32[]{:S(2)}) collective-permute-start(bf16[2,128]{1,0:T(2,128)(2,1)S(1)} %get-tuple-element.250), channel_id=1, source_target_pairs={{0,4},{2,6},{4,0},{6,2},{1,5},{3,7},{5,1},{7,3},{8,12},{10,14},{12... | collective-permute-start | bytes 1544 | tf_op jit(solution)/shard_map/ppermute | solution.py:75
  9.0 29.2 %collective-permute-start.9 = (bf16[2,128]{1,0:T(2,128)(2,1)S(1)}, bf16[2,128]{1,0:T(2,128)(2,1)S(1)}, u32[]{:S(2)}, u32[]{:S(2)}) collective-permute-start(bf16[2,128]{1,0:T(2,128)(2,1)S(1)} %get-tuple-element.250), channel_id=1, source_target_pairs={{0,6},{2,0},{4,2},{6,4},{1,7},{3,1},{5,3},{7,5},{8,14},{10,8},{12,... | collective-permute-start | bytes 1544 | tf_op jit(solution)/shard_map/ppermute | solution.py:75
  80.8 36.6 %collective-permute-start.47 = (bf16[128,1024]{1,0:T(8,128)(2,1)S(1)}, bf16[128,1024]{1,0:T(8,128)(2,1)S(1)}, u32[]{:S(2)}, u32[]{:S(2)}) collective-permute-start(bf16[128,1024]{1,0:T(8,128)(2,1)S(1)} %copy-done.92), channel_id=1, source_target_pairs={{0,2},{2,4},{4,6},{6,0},{1,3},{3,5},{5,7},{7,1},{8,10},{10,12},{12... | collective-permute-start | bytes 786440 | tf_op jit(solution)/shard_map/ppermute | solution.py:75
  94.4 30.8 %collective-permute-start.48 = (bf16[128,1024]{1,0:T(8,128)(2,1)S(1)}, bf16[128,1024]{1,0:T(8,128)(2,1)S(1)}, u32[]{:S(2)}, u32[]{:S(2)}) collective-permute-start(bf16[128,1024]{1,0:T(8,128)(2,1)S(1)} %copy-done.91), channel_id=1, source_target_pairs={{0,4},{2,6},{4,0},{6,2},{1,5},{3,7},{5,1},{7,3},{8,12},{10,14},{12... | collective-permute-start | bytes 786440 | tf_op jit(solution)/shard_map/ppermute | solution.py:75
  98.9 27.0 %collective-permute-start.40 = (bf16[128,1024]{1,0:T(8,128)(2,1)S(1)}, bf16[128,1024]{1,0:T(8,128)(2,1)S(1)}, u32[]{:S(2)}, u32[]{:S(2)}) collective-permute-start(bf16[128,1024]{1,0:T(8,128)(2,1)S(1)} %copy-done.90), channel_id=1, source_target_pairs={{0,2},{2,4},{4,6},{6,0},{1,3},{3,5},{5,7},{7,1},{8,10},{10,12},{12... | collective-permute-start | bytes 786440 | tf_op jit(solution)/shard_map/ppermute | solution.py:75
  125.2 41.2 %collective-permute-start.69 = (bf16[128,2048]{1,0:T(8,128)(2,1)}, bf16[128,2048]{1,0:T(8,128)(2,1)S(1)}, u32[]{:S(2)}, u32[]{:S(2)}) collective-permute-start(bf16[128,2048]{1,0:T(8,128)(2,1)} %get-tuple-element.374), channel_id=1, source_target_pairs={{0,1},{1,0},{2,3},{3,2},{4,5},{5,4},{6,7},{7,6},{8,9},{9,8},{10,11... | collective-permute-start | bytes 1572872 | tf_op jit(solution)/shard_map/ppermute | solution.py:81
  135.3 36.7 %collective-permute-start.70 = (bf16[128,2048]{1,0:T(8,128)(2,1)S(1)}, bf16[128,2048]{1,0:T(8,128)(2,1)S(1)}, u32[]{:S(2)}, u32[]{:S(2)}) collective-permute-start(bf16[128,2048]{1,0:T(8,128)(2,1)S(1)} %copy-done.56), channel_id=1, source_target_pairs={{0,2},{2,4},{4,6},{6,0},{1,3},{3,5},{5,7},{7,1},{8,10},{10,12},{12... | collective-permute-start | bytes 1572872 | tf_op jit(solution)/shard_map/ppermute | solution.py:75
  174.5 89.8 %collective-permute-start.23 = (bf16[128,1024]{1,0:T(8,128)(2,1)}, bf16[128,1024]{1,0:T(8,128)(2,1)}, u32[]{:S(2)}, u32[]{:S(2)}) collective-permute-start(bf16[128,1024]{1,0:T(8,128)(2,1)} %pad_maximum_fusion.22), channel_id=1, source_target_pairs={{0,16},{8,24},{16,0},{24,8},{1,17},{9,25},{17,1},{25,9},{2,18},{10... | collective-permute-start | bytes 786440 | tf_op jit(solution)/shard_map/ppermute | solution.py:78
  183.2 85.4 %collective-permute-start.57 = (bf16[512,512]{1,0:T(8,128)(2,1)}, bf16[512,512]{1,0:T(8,128)(2,1)}, u32[]{:S(2)}, u32[]{:S(2)}) collective-permute-start(bf16[512,512]{1,0:T(8,128)(2,1)} %get-tuple-element.329), channel_id=1, source_target_pairs={{0,8},{8,0},{16,24},{24,16},{1,9},{9,1},{17,25},{25,17},{2,10},{10... | collective-permute-start | bytes 1572872 | tf_op jit(solution)/shard_map/ppermute | solution.py:78
  192.5 77.6 %collective-permute-start.52 = (bf16[512,512]{1,0:T(8,128)(2,1)}, bf16[512,512]{1,0:T(8,128)(2,1)}, u32[]{:S(2)}, u32[]{:S(2)}) collective-permute-start(bf16[512,512]{1,0:T(8,128)(2,1)} %get-tuple-element.346), channel_id=1, source_target_pairs={{0,16},{8,24},{16,0},{24,8},{1,17},{9,25},{17,1},{25,9},{2,18},{10... | collective-permute-start | bytes 1572872 | tf_op jit(solution)/shard_map/ppermute | solution.py:78
  196.2 75.7 %collective-permute-start.50 = (bf16[512,512]{1,0:T(8,128)(2,1)}, bf16[512,512]{1,0:T(8,128)(2,1)}, u32[]{:S(2)}, u32[]{:S(2)}) collective-permute-start(bf16[512,512]{1,0:T(8,128)(2,1)} %get-tuple-element.345), channel_id=1, source_target_pairs={{0,8},{8,0},{16,24},{24,16},{1,9},{9,1},{17,25},{25,17},{2,10},{10... | collective-permute-start | bytes 1572872 | tf_op jit(solution)/shard_map/ppermute | solution.py:78
  222.7 50.6 %collective-permute-start.45 = (bf16[512,512]{1,0:T(8,128)(2,1)}, bf16[512,512]{1,0:T(8,128)(2,1)}, u32[]{:S(2)}, u32[]{:S(2)}) collective-permute-start(bf16[512,512]{1,0:T(8,128)(2,1)} %get-tuple-element.338), channel_id=1, source_target_pairs={{0,16},{8,24},{16,0},{24,8},{1,17},{9,25},{17,1},{25,9},{2,18},{10... | collective-permute-start | bytes 1572872 | tf_op jit(solution)/shard_map/ppermute | solution.py:78
  273.3 38.2 %collective-permute-start.60 = (bf16[512,1024]{1,0:T(8,128)(2,1)S(1)}, bf16[512,1024]{1,0:T(8,128)(2,1)S(1)}, u32[]{:S(2)}, u32[]{:S(2)}) collective-permute-start(bf16[512,1024]{1,0:T(8,128)(2,1)S(1)} %copy-done.44), channel_id=1, source_target_pairs={{0,8},{8,0},{16,24},{24,16},{1,9},{9,1},{17,25},{25,17},{2,10},{10... | collective-permute-start | bytes 3145736 | tf_op jit(solution)/shard_map/ppermute | solution.py:78
  278.3 43.7 %collective-permute-start.53 = (bf16[1024,512]{1,0:T(8,128)(2,1)S(1)}, bf16[1024,512]{1,0:T(8,128)(2,1)S(1)}, u32[]{:S(2)}, u32[]{:S(2)}) collective-permute-start(bf16[1024,512]{1,0:T(8,128)(2,1)S(1)} %pad_maximum_fusion.4), channel_id=1, source_target_pairs={{0,8},{8,0},{16,24},{24,16},{1,9},{9,1},{17,25},{25,17},{2,10},{10... | collective-permute-start | bytes 3145736 | tf_op jit(solution)/shard_map/ppermute | solution.py:78
  310.9 33.1 %collective-permute-start.46 = (bf16[1024,512]{1,0:T(8,128)(2,1)S(1)}, bf16[1024,512]{1,0:T(8,128)(2,1)S(1)}, u32[]{:S(2)}, u32[]{:S(2)}) collective-permute-start(bf16[1024,512]{1,0:T(8,128)(2,1)S(1)} %pad_maximum_fusion.2), channel_id=1, source_target_pairs={{0,8},{8,0},{16,24},{24,16},{1,9},{9,1},{17,25},{25,17},{2,10},{10... | collective-permute-start | bytes 3145736 | tf_op jit(solution)/shard_map/ppermute | solution.py:78
  311.5 39.6 %collective-permute-start.58 = (bf16[512,1024]{1,0:T(8,128)(2,1)S(1)}, bf16[512,1024]{1,0:T(8,128)(2,1)S(1)}, u32[]{:S(2)}, u32[]{:S(2)}) collective-permute-start(bf16[512,1024]{1,0:T(8,128)(2,1)S(1)} %pad_maximum_fusion.5), channel_id=1, source_target_pairs={{0,16},{8,24},{16,0},{24,8},{1,17},{9,25},{17,1},{25,9},{2,18},{10... | collective-permute-start | bytes 3145736 | tf_op jit(solution)/shard_map/ppermute | solution.py:78
  312.8 33.2 %collective-permute-start.75 = (bf16[128,2048]{1,0:T(8,128)(2,1)S(1)}, bf16[128,2048]{1,0:T(8,128)(2,1)S(1)}, u32[]{:S(2)}, u32[]{:S(2)}) collective-permute-start(bf16[128,2048]{1,0:T(8,128)(2,1)S(1)} %collective-permute-done.74), channel_id=1, source_target_pairs={{0,1},{1,0},{2,3},{3,2},{4,5},{5,4},{6,7},{7,6},{8,9},{9,8},{10,11... | collective-permute-start | bytes 1572872 | tf_op jit(solution)/shard_map/ppermute | solution.py:81
  321.3 25.9 %collective-permute-start.26 = (bf16[128,2048]{1,0:T(8,128)(2,1)S(1)}, bf16[128,2048]{1,0:T(8,128)(2,1)S(1)}, u32[]{:S(2)}, u32[]{:S(2)}) collective-permute-start(bf16[128,2048]{1,0:T(8,128)(2,1)S(1)} %get-tuple-element.284), channel_id=1, source_target_pairs={{0,1},{1,0},{2,3},{3,2},{4,5},{5,4},{6,7},{7,6},{8,9},{9,8},{10,11... | collective-permute-start | bytes 1572872 | tf_op jit(solution)/shard_map/ppermute | solution.py:81
  322.0 26.7 %collective-permute-start.32 = (bf16[128,2048]{1,0:T(8,128)(2,1)S(1)}, bf16[128,2048]{1,0:T(8,128)(2,1)S(1)}, u32[]{:S(2)}, u32[]{:S(2)}) collective-permute-start(bf16[128,2048]{1,0:T(8,128)(2,1)S(1)} %fusion.120), channel_id=1, source_target_pairs={{0,2},{2,4},{4,6},{6,0},{1,3},{3,5},{5,7},{7,1},{8,10},{10,12},{12... | collective-permute-start | bytes 1572872 | tf_op jit(solution)/shard_map/ppermute | solution.py:75
  344.0 83.2 %collective-permute-start.51 = (bf16[1024,512]{1,0:T(8,128)(2,1)S(1)}, bf16[1024,512]{1,0:T(8,128)(2,1)}, u32[]{:S(2)}, u32[]{:S(2)}) collective-permute-start(bf16[1024,512]{1,0:T(8,128)(2,1)S(1)} %pad_maximum_fusion.3), channel_id=1, source_target_pairs={{0,16},{8,24},{16,0},{24,8},{1,17},{9,25},{17,1},{25,9},{2,18},{10... | collective-permute-start | bytes 3145736 | tf_op jit(solution)/shard_map/ppermute | solution.py:78
  346.0 94.3 %collective-permute-start.44 = (bf16[1024,512]{1,0:T(8,128)(2,1)}, bf16[1024,512]{1,0:T(8,128)(2,1)}, u32[]{:S(2)}, u32[]{:S(2)}) collective-permute-start(bf16[1024,512]{1,0:T(8,128)(2,1)} %pad_maximum_fusion.1), channel_id=1, source_target_pairs={{0,16},{8,24},{16,0},{24,8},{1,17},{9,25},{17,1},{25,9},{2,18},{10... | collective-permute-start | bytes 3145736 | tf_op jit(solution)/shard_map/ppermute | solution.py:78
  347.2 28.0 %collective-permute-start.145 = (f32[4]{0:T(128)S(1)}, f32[4]{0:T(128)S(1)}, u32[]{:S(2)}, u32[]{:S(2)}) collective-permute-start(f32[4]{0:T(128)S(1)} %copy-done.107), channel_id=1, source_target_pairs={{0,8},{8,0},{16,24},{24,16},{1,9},{9,1},{17,25},{25,17},{2,10},{10... | collective-permute-start | bytes 56 | tf_op jit(solution)/shard_map/ppermute | solution.py:78
  376.1 30.2 %collective-permute-start.33 = (bf16[128,2048]{1,0:T(8,128)(2,1)S(1)}, bf16[128,2048]{1,0:T(8,128)(2,1)}, u32[]{:S(2)}, u32[]{:S(2)}) collective-permute-start(bf16[128,2048]{1,0:T(8,128)(2,1)S(1)} %get-tuple-element.246), channel_id=1, source_target_pairs={{0,1},{1,0},{2,3},{3,2},{4,5},{5,4},{6,7},{7,6},{8,9},{9,8},{10,11... | collective-permute-start | bytes 1572872 | tf_op jit(solution)/shard_map/ppermute | solution.py:81
  376.2 30.2 %collective-permute-start.36 = (bf16[128,2048]{1,0:T(8,128)(2,1)}, bf16[128,2048]{1,0:T(8,128)(2,1)}, u32[]{:S(2)}, u32[]{:S(2)}) collective-permute-start(bf16[128,2048]{1,0:T(8,128)(2,1)} %collective-permute-done.34), channel_id=1, source_target_pairs={{0,2},{2,4},{4,6},{6,0},{1,3},{3,5},{5,7},{7,1},{8,10},{10,12},{12... | collective-permute-start | bytes 1572872 | tf_op jit(solution)/shard_map/ppermute | solution.py:75
  512.1 85.9 %collective-permute-start.77 = (bf16[128,2048]{1,0:T(8,128)(2,1)}, bf16[128,2048]{1,0:T(8,128)(2,1)S(1)}, u32[]{:S(2)}, u32[]{:S(2)}) collective-permute-start(bf16[128,2048]{1,0:T(8,128)(2,1)} %get-tuple-element.279), channel_id=1, source_target_pairs={{0,1},{1,0},{2,3},{3,2},{4,5},{5,4},{6,7},{7,6},{8,9},{9,8},{10,11... | collective-permute-start | bytes 1572872 | tf_op jit(solution)/shard_map/ppermute | solution.py:81
  527.6 26.2 %collective-permute-start.126 = (bf16[1024,512]{1,0:T(8,128)(2,1)}, bf16[1024,512]{1,0:T(8,128)(2,1)S(1)}, u32[]{:S(2)}, u32[]{:S(2)}) collective-permute-start(bf16[1024,512]{1,0:T(8,128)(2,1)} %slice.753), channel_id=1, source_target_pairs={{0,16},{8,24},{16,0},{24,8},{1,17},{9,25},{17,1},{25,9},{2,18},{10... | collective-permute-start | bytes 3145736 | tf_op jit(solution)/shard_map/ppermute | solution.py:78
  532.7 43.6 %collective-permute-start.133 = (bf16[1024,512]{1,0:T(8,128)(2,1)S(1)}, bf16[1024,512]{1,0:T(8,128)(2,1)S(1)}, u32[]{:S(2)}, u32[]{:S(2)}) collective-permute-start(bf16[1024,512]{1,0:T(8,128)(2,1)S(1)} %slice.764), channel_id=1, source_target_pairs={{0,16},{8,24},{16,0},{24,8},{1,17},{9,25},{17,1},{25,9},{2,18},{10... | collective-permute-start | bytes 3145736 | tf_op jit(solution)/shard_map/ppermute | solution.py:78
  553.9 44.0 %collective-permute-start.140 = (bf16[512,1024]{1,0:T(8,128)(2,1)S(1)}, bf16[512,1024]{1,0:T(8,128)(2,1)S(1)}, u32[]{:S(2)}, u32[]{:S(2)}) collective-permute-start(bf16[512,1024]{1,0:T(8,128)(2,1)S(1)} %slice.775), channel_id=1, source_target_pairs={{0,16},{8,24},{16,0},{24,8},{1,17},{9,25},{17,1},{25,9},{2,18},{10... | collective-permute-start | bytes 3145736 | tf_op jit(solution)/shard_map/ppermute | solution.py:78
  556.2 42.5 %collective-permute-start.62 = (bf16[128,2048]{1,0:T(8,128)(2,1)}, bf16[128,2048]{1,0:T(8,128)(2,1)S(1)}, u32[]{:S(2)}, u32[]{:S(2)}) collective-permute-start(bf16[128,2048]{1,0:T(8,128)(2,1)} %get-tuple-element.283), channel_id=1, source_target_pairs={{0,1},{1,0},{2,3},{3,2},{4,5},{5,4},{6,7},{7,6},{8,9},{9,8},{10,11... | collective-permute-start | bytes 1572872 | tf_op jit(solution)/shard_map/ppermute | solution.py:81
  563.1 50.3 %collective-permute-start.124 = (bf16[1024,512]{1,0:T(8,128)(2,1)S(1)}, bf16[1024,512]{1,0:T(8,128)(2,1)S(1)}, u32[]{:S(2)}, u32[]{:S(2)}) collective-permute-start(bf16[1024,512]{1,0:T(8,128)(2,1)S(1)} %pad_maximum_fusion.8), channel_id=1, source_target_pairs={{0,8},{8,0},{16,24},{24,16},{1,9},{9,1},{17,25},{25,17},{2,10},{10... | collective-permute-start | bytes 3145736 | tf_op jit(solution)/shard_map/ppermute | solution.py:78
  598.1 62.4 %collective-permute-start.131 = (bf16[1024,512]{1,0:T(8,128)(2,1)S(1)}, bf16[1024,512]{1,0:T(8,128)(2,1)S(1)}, u32[]{:S(2)}, u32[]{:S(2)}) collective-permute-start(bf16[1024,512]{1,0:T(8,128)(2,1)S(1)} %pad_maximum_fusion.9), channel_id=1, source_target_pairs={{0,8},{8,0},{16,24},{24,16},{1,9},{9,1},{17,25},{25,17},{2,10},{10... | collective-permute-start | bytes 3145736 | tf_op jit(solution)/shard_map/ppermute | solution.py:78
  598.7 61.9 %collective-permute-start.138 = (bf16[512,1024]{1,0:T(8,128)(2,1)S(1)}, bf16[512,1024]{1,0:T(8,128)(2,1)S(1)}, u32[]{:S(2)}, u32[]{:S(2)}) collective-permute-start(bf16[512,1024]{1,0:T(8,128)(2,1)S(1)} %pad_maximum_fusion.10), channel_id=1, source_target_pairs={{0,8},{8,0},{16,24},{24,16},{1,9},{9,1},{17,25},{25,17},{2,10},{10... | collective-permute-start | bytes 3145736 | tf_op jit(solution)/shard_map/ppermute | solution.py:78
  600.2 57.8 %collective-permute-start.127 = (bf16[512,512]{1,0:T(8,128)(2,1)S(1)}, bf16[512,512]{1,0:T(8,128)(2,1)S(1)}, u32[]{:S(2)}, u32[]{:S(2)}) collective-permute-start(bf16[512,512]{1,0:T(8,128)(2,1)S(1)} %fusion.77), channel_id=1, source_target_pairs={{0,8},{8,0},{16,24},{24,16},{1,9},{9,1},{17,25},{25,17},{2,10},{10... | collective-permute-start | bytes 1572872 | tf_op jit(solution)/shard_map/ppermute | solution.py:78
  612.6 56.5 %collective-permute-start.134 = (bf16[512,512]{1,0:T(8,128)(2,1)S(1)}, bf16[512,512]{1,0:T(8,128)(2,1)S(1)}, u32[]{:S(2)}, u32[]{:S(2)}) collective-permute-start(bf16[512,512]{1,0:T(8,128)(2,1)S(1)} %fusion.73), channel_id=1, source_target_pairs={{0,8},{8,0},{16,24},{24,16},{1,9},{9,1},{17,25},{25,17},{2,10},{10... | collective-permute-start | bytes 1572872 | tf_op jit(solution)/shard_map/ppermute | solution.py:78
  613.4 66.5 %collective-permute-start.76 = (bf16[128,2048]{1,0:T(8,128)(2,1)S(1)}, bf16[128,2048]{1,0:T(8,128)(2,1)S(1)}, u32[]{:S(2)}, u32[]{:S(2)}) collective-permute-start(bf16[128,2048]{1,0:T(8,128)(2,1)S(1)} %copy-done.77), channel_id=1, source_target_pairs={{0,1},{1,0},{2,3},{3,2},{4,5},{5,4},{6,7},{7,6},{8,9},{9,8},{10,11... | collective-permute-start | bytes 1572872 | tf_op jit(solution)/shard_map/ppermute | solution.py:81
  681.1 31.9 %collective-permute-start.139 = (bf16[512,512]{1,0:T(8,128)(2,1)S(1)}, bf16[512,512]{1,0:T(8,128)(2,1)S(1)}, u32[]{:S(2)}, u32[]{:S(2)}) collective-permute-start(bf16[512,512]{1,0:T(8,128)(2,1)S(1)} %get-tuple-element.256), channel_id=1, source_target_pairs={{0,16},{8,24},{16,0},{24,8},{1,17},{9,25},{17,1},{25,9},{2,18},{10... | collective-permute-start | bytes 1572872 | tf_op jit(solution)/shard_map/ppermute | solution.py:78
  693.0 101.8 %collective-permute-start.83 = (bf16[128,2048]{1,0:T(8,128)(2,1)S(1)}, bf16[128,2048]{1,0:T(8,128)(2,1)S(1)}, u32[]{:S(2)}, u32[]{:S(2)}) collective-permute-start(bf16[128,2048]{1,0:T(8,128)(2,1)S(1)} %get-tuple-element.241), channel_id=1, source_target_pairs={{0,1},{1,0},{2,3},{3,2},{4,5},{5,4},{6,7},{7,6},{8,9},{9,8},{10,11... | collective-permute-start | bytes 1572872 | tf_op jit(solution)/shard_map/ppermute | solution.py:81
  693.0 81.6 %collective-permute-start.84 = (bf16[128,2048]{1,0:T(8,128)(2,1)S(1)}, bf16[128,2048]{1,0:T(8,128)(2,1)S(1)}, u32[]{:S(2)}, u32[]{:S(2)}) collective-permute-start(bf16[128,2048]{1,0:T(8,128)(2,1)S(1)} %get-tuple-element.241), channel_id=1, source_target_pairs={{0,2},{2,4},{4,6},{6,0},{1,3},{3,5},{5,7},{7,1},{8,10},{10,12},{12... | collective-permute-start | bytes 1572872 | tf_op jit(solution)/shard_map/ppermute | solution.py:75
  693.4 86.1 %collective-permute-start.68 = (bf16[128,2048]{1,0:T(8,128)(2,1)S(1)}, bf16[128,2048]{1,0:T(8,128)(2,1)S(1)}, u32[]{:S(2)}, u32[]{:S(2)}) collective-permute-start(bf16[128,2048]{1,0:T(8,128)(2,1)S(1)} %pad_maximum_fusion.18), channel_id=1, source_target_pairs={{0,1},{1,0},{2,3},{3,2},{4,5},{5,4},{6,7},{7,6},{8,9},{9,8},{10,11... | collective-permute-start | bytes 1572872 | tf_op jit(solution)/shard_map/ppermute | solution.py:81
  870.2 48.8 %collective-permute-start.92 = (bf16[128,2048]{1,0:T(8,128)(2,1)S(1)}, bf16[128,2048]{1,0:T(8,128)(2,1)S(1)}, u32[]{:S(2)}, u32[]{:S(2)}) collective-permute-start(bf16[128,2048]{1,0:T(8,128)(2,1)S(1)} %get-tuple-element.274), channel_id=1, source_target_pairs={{0,1},{1,0},{2,3},{3,2},{4,5},{5,4},{6,7},{7,6},{8,9},{9,8},{10,11... | collective-permute-start | bytes 1572872 | tf_op jit(solution)/shard_map/ppermute | solution.py:81
  870.6 92.4 %collective-permute-start.91 = (bf16[128,2048]{1,0:T(8,128)(2,1)S(1)}, bf16[128,2048]{1,0:T(8,128)(2,1)S(1)}, u32[]{:S(2)}, u32[]{:S(2)}) collective-permute-start(bf16[128,2048]{1,0:T(8,128)(2,1)S(1)} %get-tuple-element.275), channel_id=1, source_target_pairs={{0,1},{1,0},{2,3},{3,2},{4,5},{5,4},{6,7},{7,6},{8,9},{9,8},{10,11... | collective-permute-start | bytes 1572872 | tf_op jit(solution)/shard_map/ppermute | solution.py:81
  880.1 38.8 %collective-permute-start.109 = (bf16[1024,384]{1,0:T(8,128)(2,1)S(1)}, bf16[1024,384]{1,0:T(8,128)(2,1)S(1)}, u32[]{:S(2)}, u32[]{:S(2)}) collective-permute-start(bf16[1024,384]{1,0:T(8,128)(2,1)S(1)} %slice.730), channel_id=1, source_target_pairs={{0,16},{8,24},{16,0},{24,8},{1,17},{9,25},{17,1},{25,9},{2,18},{10... | collective-permute-start | bytes 2359304 | tf_op jit(solution)/shard_map/ppermute | solution.py:78
  885.6 34.0 %collective-permute-start.94 = (bf16[128,2048]{1,0:T(8,128)(2,1)S(1)}, bf16[128,2048]{1,0:T(8,128)(2,1)S(1)}, u32[]{:S(2)}, u32[]{:S(2)}) collective-permute-start(bf16[128,2048]{1,0:T(8,128)(2,1)S(1)} %fusion.82), channel_id=1, source_target_pairs={{0,2},{2,4},{4,6},{6,0},{1,3},{3,5},{5,7},{7,1},{8,10},{10,12},{12... | collective-permute-start | bytes 1572872 | tf_op jit(solution)/shard_map/ppermute | solution.py:75
  918.9 62.8 %collective-permute-start.90 = (bf16[128,2048]{1,0:T(8,128)(2,1)S(1)}, bf16[128,2048]{1,0:T(8,128)(2,1)S(1)}, u32[]{:S(2)}, u32[]{:S(2)}) collective-permute-start(bf16[128,2048]{1,0:T(8,128)(2,1)S(1)} %get-tuple-element.272), channel_id=1, source_target_pairs={{0,1},{1,0},{2,3},{3,2},{4,5},{5,4},{6,7},{7,6},{8,9},{9,8},{10,11... | collective-permute-start | bytes 1572872 | tf_op jit(solution)/shard_map/ppermute | solution.py:81
  919.8 43.2 %collective-permute-start.95 = (bf16[128,2048]{1,0:T(8,128)(2,1)S(1)}, bf16[128,2048]{1,0:T(8,128)(2,1)S(1)}, u32[]{:S(2)}, u32[]{:S(2)}) collective-permute-start(bf16[128,2048]{1,0:T(8,128)(2,1)S(1)} %fusion.85), channel_id=1, source_target_pairs={{0,2},{2,4},{4,6},{6,0},{1,3},{3,5},{5,7},{7,1},{8,10},{10,12},{12... | collective-permute-start | bytes 1572872 | tf_op jit(solution)/shard_map/ppermute | solution.py:75
  (215 other events, 5096.8 us)

commit v2 on v1

v2 whole, which is shorter than its diff:
```python
import functools

import jax
import jax.numpy as jnp
from jax import lax
from jax.experimental import pallas as pl
from jax.experimental.pallas import tpu as pltpu
from jax.sharding import PartitionSpec as P

HEAD_DIM = 64
NORM_EPS = 1e-05
ROPE_BASE = 130000.0

f32 = jnp.float32
bf16 = jnp.bfloat16

PAIR = 2 * HEAD_DIM
ROWS = 256
VMEM_LIMIT = 48 * 1024 * 1024


def rope_tables(positions):
    half_dim = HEAD_DIM // 2
    step_index = jnp.arange(half_dim, dtype=f32)
    frequency = jnp.power(ROPE_BASE, -2.0 * step_index / (2 * half_dim))
    angles = positions.astype(f32)[:, None] * frequency[None, :]
    cosine, sine = jnp.cos(angles), jnp.sin(angles)
    return (
        jnp.concatenate([cosine, cosine, cosine, cosine], 1),
        jnp.concatenate([-sine, sine, -sine, sine], 1),
    )


def dot(left, right):
    return jnp.dot(left, right, preferred_element_type=f32)


def dot_lt(left, right):
    return lax.dot_general(left, right, (((0,), (0,)), ((), ())), preferred_element_type=f32)


def dot_rt(left, right):
    return lax.dot_general(left, right, (((1,), (1,)), ((), ())), preferred_element_type=f32)


def turn(pair, cosine, sine):
    lane = lax.broadcasted_iota(jnp.int32, pair.shape, 1)
    half_dim = HEAD_DIM // 2
    swapped = jnp.where(
        lane % HEAD_DIM < half_dim,
        pltpu.roll(pair, PAIR - half_dim, 1),
        pltpu.roll(pair, half_dim, 1),
    )
    return pair * cosine + swapped * sine


def project_kernel(pieces, heads_width, x_ref, gain_ref, cosine_ref, sine_ref, *refs):
    weights, normed_ref, out_ref = refs[:pieces], refs[pieces], refs[pieces + 1]
    inputs = x_ref[...].astype(f32)
    inverse = lax.rsqrt(jnp.mean(inputs * inputs, -1, keepdims=True) + NORM_EPS)
    normed = (inputs * inverse * gain_ref[...]).astype(bf16)
    normed_ref[...] = normed
    block = normed.shape[1] // pieces
    proj = None
    for at, weight in enumerate(weights):
        term = dot(normed[:, at * block : (at + 1) * block], weight[:, : 3 * heads_width])
        proj = term if proj is None else proj + term
    cosine, sine = cosine_ref[...], sine_ref[...]
    for at in range(3 * heads_width // PAIR):
        pair = proj[:, at * PAIR : (at + 1) * PAIR]
        if at < 2 * heads_width // PAIR:
            pair = turn(pair, cosine, sine)
        out_ref[:, at * PAIR : (at + 1) * PAIR] = pair.astype(bf16)


def project(tokens, gain, cosine, sine, weights, heads_width, row_block):
    length, width = tokens.shape
    rows = lambda columns: pl.BlockSpec((row_block, columns), lambda i: (i, 0))
    whole = lambda tensor: pl.BlockSpec(tensor.shape, lambda i: (0, 0))
    return pl.pallas_call(
        functools.partial(project_kernel, len(weights), heads_width),
        grid=(length // row_block,),
        out_shape=(
            jax.ShapeDtypeStruct((length, width), bf16),
            jax.ShapeDtypeStruct((length, 3 * heads_width), bf16),
        ),
        in_specs=[rows(width), whole(gain), rows(PAIR), rows(PAIR)] + [whole(w) for w in weights],
        out_specs=(rows(width), rows(3 * heads_width)),
        compiler_params=pltpu.CompilerParams(vmem_limit_bytes=VMEM_LIMIT),
        cost_estimate=pl.CostEstimate(
            flops=6 * length * width * heads_width,
            bytes_accessed=4 * length * width + 8 * width * heads_width,
            transcendentals=length,
        ),
        name="project",
    )(tokens, gain, cosine, sine, *weights)


def sort_spans(order_ref, source, sorted_ref):
    span = sorted_ref.shape[0] // order_ref.shape[0]
    for at in range(order_ref.shape[0]):
        start = pl.multiple_of(order_ref[at] * span, span)
        sorted_ref[pl.ds(start, span), :] = source[at * span : (at + 1) * span, :]


def unsorted_span(order_ref, sorted_ref, at):
    span = sorted_ref.shape[0] // order_ref.shape[0]
    start = pl.multiple_of(order_ref[at] * span, span)
    return sorted_ref[pl.ds(start, span), :]


def causal(scores, first_row):
    row = lax.broadcasted_iota(jnp.int32, scores.shape, 0) + first_row
    column = lax.broadcasted_iota(jnp.int32, scores.shape, 1)
    return jnp.where(column <= row, scores, -1e30)


def forward_kernel(order_ref, q_ref, k_ref, v_ref, out_ref, log_ref, peak_ref, q_s, k_s, v_s, o_s):
    length = q_ref.shape[0]
    block = min(ROWS, length)
    scale = HEAD_DIM ** (-0.5)
    for source, held in ((q_ref, q_s), (k_ref, k_s), (v_ref, v_s)):
        sort_spans(order_ref, source, held)
    lane = lax.broadcasted_iota(jnp.int32, (block, PAIR), 1)
    peaks = [None, None]
    for start in range(0, length, block):
        end = start + block
        query, key, value = q_s[start:end, :], k_s[:end, :], v_s[:end, :]
        attended, logs = [], []
        for head in range(2):
            mine = (lane // HEAD_DIM) == head
            scores = causal(dot_rt(jnp.where(mine, query, 0), key) * scale, start)
            row_max = jnp.max(scores, 1, keepdims=True)
            terms = jnp.exp(scores - row_max)
            total = jnp.sum(terms, 1, keepdims=True)
            attended.append(dot((terms * (1.0 / total)).astype(bf16), value))
            logs.append(row_max + jnp.log(total))
            top = jnp.max(row_max)
            peaks[head] = top if peaks[head] is None else jnp.maximum(peaks[head], top)
        o_s[start:end, :] = jnp.where(lane < HEAD_DIM, attended[0], attended[1])
        log_ref[0, start:end, :] = jnp.where(lane < HEAD_DIM, logs[0], logs[1])
    for at in range(order_ref.shape[0]):
        span = length // order_ref.shape[0]
        out_ref[at * span : (at + 1) * span, :] = unsorted_span(order_ref, o_s, at).astype(bf16)
    lane = lax.broadcasted_iota(jnp.int32, peak_ref.shape, 2)
    peak_ref[...] = jnp.where(lane < HEAD_DIM, peaks[0], peaks[1])


def attend(order, qkv):
    length = qkv.shape[0]
    pairs = qkv.shape[1] // (3 * PAIR)
    column = lambda first: pl.BlockSpec((length, PAIR), lambda g, order: (0, first + g))
    return pl.pallas_call(
        forward_kernel,
        grid_spec=pltpu.PrefetchScalarGridSpec(
            num_scalar_prefetch=1,
            grid=(pairs,),
            in_specs=[column(0), column(pairs), column(2 * pairs)],
            out_specs=(
                column(0),
                pl.BlockSpec((1, length, PAIR), lambda g, order: (g, 0, 0)),
                pl.BlockSpec((1, 8, PAIR), lambda g, order: (g, 0, 0)),
            ),
            scratch_shapes=[pltpu.VMEM((length, PAIR), bf16)] * 3 + [pltpu.VMEM((length, PAIR), f32)],
        ),
        out_shape=(
            jax.ShapeDtypeStruct((length, pairs * PAIR), bf16),
            jax.ShapeDtypeStruct((pairs, length, PAIR), f32),
            jax.ShapeDtypeStruct((pairs, 8, PAIR), f32),
        ),
        compiler_params=pltpu.CompilerParams(vmem_limit_bytes=VMEM_LIMIT),
        cost_estimate=pl.CostEstimate(
            flops=16 * pairs * length * length * PAIR,
            bytes_accessed=8 * pairs * length * PAIR,
            transcendentals=2 * pairs * length * length,
        ),
        name="attend",
    )(order, qkv, qkv, qkv)


def backward_kernel(
    order_ref, q_ref, k_ref, v_ref, g_ref, log_ref, cosine_ref, sine_ref, out_ref, *held
):
    q_s, k_s, v_s, g_s, dq_s, dk_s, dv_s = held
    length = q_ref.shape[0]
    block = min(ROWS, length)
    scale = HEAD_DIM ** (-0.5)
    for source, into in ((q_ref, q_s), (k_ref, k_s), (v_ref, v_s), (g_ref, g_s)):
        sort_spans(order_ref, source, into)
    dk_s[...] = jnp.zeros_like(dk_s)
    dv_s[...] = jnp.zeros_like(dv_s)
    lane = lax.broadcasted_iota(jnp.int32, (block, PAIR), 1)
    for start in range(0, length, block):
        end = start + block
        query, grad = q_s[start:end, :], g_s[start:end, :]
        key, value = k_s[:end, :], v_s[:end, :]
        grad_query = []
        for head in range(2):
            mine = (lane // HEAD_DIM) == head
            query_h = jnp.where(mine, query, 0)
            grad_h = jnp.where(mine, grad, 0)
            log_h = log_ref[0, start:end, head * HEAD_DIM : head * HEAD_DIM + 1]
            scores = causal(dot_rt(query_h, key) * scale, start)
            prob = jnp.exp(scores - log_h)
            grad_prob = dot_rt(grad_h, value)
            delta = jnp.sum(prob * grad_prob, 1, keepdims=True)
            grad_score = (prob * (grad_prob - delta)).astype(bf16)
            grad_query.append(dot(grad_score, key))
            dk_s[:end, :] += dot_lt(grad_score, query_h)
            dv_s[:end, :] += dot_lt(prob.astype(bf16), grad_h)
        dq_s[start:end, :] = jnp.where(lane < HEAD_DIM, grad_query[0], grad_query[1])
    pairs = out_ref.shape[1] // (3 * PAIR)
    column = pl.program_id(0)
    span = length // order_ref.shape[0]
    for at in range(order_ref.shape[0]):
        rows = slice(at * span, (at + 1) * span)
        cosine, sine = cosine_ref[rows, :], sine_ref[rows, :]
        for which, source in enumerate((dq_s, dk_s, dv_s)):
            part = unsorted_span(order_ref, source, at)
            if which < 2:
                part = turn(part * scale, cosine, -sine)
            start = pl.multiple_of((which * pairs + column) * PAIR, PAIR)
            out_ref[rows, pl.ds(start, PAIR)] = part.astype(bf16)


def attend_back(order, qkv, grad, logs, cosine, sine):
    length = qkv.shape[0]
    pairs = qkv.shape[1] // (3 * PAIR)
    column = lambda first: pl.BlockSpec((length, PAIR), lambda g, order: (0, first + g))
    whole = pl.BlockSpec((length, PAIR), lambda g, order: (0, 0))
    return pl.pallas_call(
        backward_kernel,
        grid_spec=pltpu.PrefetchScalarGridSpec(
            num_scalar_prefetch=1,
            grid=(pairs,),
            in_specs=[
                column(0),
                column(pairs),
                column(2 * pairs),
                column(0),
                pl.BlockSpec((1, length, PAIR), lambda g, order: (g, 0, 0)),
                whole,
                whole,
            ],
            out_specs=pl.BlockSpec((length, 3 * pairs * PAIR), lambda g, order: (0, 0)),
            scratch_shapes=[pltpu.VMEM((length, PAIR), bf16)] * 4
            + [pltpu.VMEM((length, PAIR), f32)] * 3,
        ),
        out_shape=jax.ShapeDtypeStruct(qkv.shape, bf16),
        compiler_params=pltpu.CompilerParams(vmem_limit_bytes=VMEM_LIMIT),
        cost_estimate=pl.CostEstimate(
            flops=40 * pairs * length * length * PAIR,
            bytes_accessed=16 * pairs * length * PAIR,
            transcendentals=2 * pairs * length * length,
        ),
        name="attend_back",
    )(order, qkv, qkv, qkv, grad, logs, cosine, sine)


def on_device(
    block_in,
    span_order,
    attn_gain,
    w_query,
    w_key,
    w_value,
    w_out,
    mlp_gain,
    w_gate,
    w_up,
    w_down,
    clip_limit,
    cotangent,
):
    n_ctx = lax.axis_size("ctx")
    n_fsdp = lax.axis_size("fsdp")
    n_bits = n_fsdp.bit_length() - 1
    c_at = lax.axis_index("ctx")
    f_at = lax.axis_index("fsdp")
    t_at = lax.axis_index("tp")
    row_count, width = block_in.shape[1:]
    span_len = row_count // 2
    feature_block = width // n_fsdp

    def along(tensor, shift):
        if shift % n_ctx == 0:
            return tensor
        return lax.ppermute(tensor, "ctx", [(i, (i + shift) % n_ctx) for i in range(n_ctx)])

    def across(tensor, mask):
        return lax.ppermute(tensor, "fsdp", [(i, i ^ mask) for i in range(n_fsdp)])

    def twin(tensor):
        return lax.ppermute(tensor, "tp", [(0, 1), (1, 0)])

    def after(tensor, *earlier):
        return lax.optimization_barrier((tensor, *earlier))[0]

    def reorder(tensor):
        return jnp.concatenate(
            [
                lax.dynamic_slice_in_dim(tensor, (f_at ^ m) * feature_block, feature_block, -1)
                for m in range(n_fsdp)
            ],
            -1,
        )

    def swap_ctx(tensor):
        piece = tensor.shape[0] // n_ctx
        columns = tensor.shape[1]
        placed = jnp.zeros((piece, n_ctx * columns), f32)
        for shift in range(n_ctx):
            sent = lax.dynamic_slice_in_dim(tensor, ((c_at + shift) % n_ctx) * piece, piece, 0)
            placed = lax.dynamic_update_slice_in_dim(
                placed, along(sent, shift).astype(f32), ((c_at - shift) % n_ctx) * columns, 1
            )
        return placed

    def swap_columns(*tensors):
        rows, columns = tensors[0].shape
        piece = columns // n_ctx
        width_here = piece * len(tensors)
        placed = jnp.zeros((n_ctx, rows, width_here), tensors[0].dtype)
        for shift in range(n_ctx):
            start = ((c_at + shift) % n_ctx) * piece
            sent = jnp.concatenate(
                [lax.dynamic_slice_in_dim(tensor, start, piece, 1) for tensor in tensors], 1
            )
            placed = lax.dynamic_update_slice_in_dim(
                placed, along(sent, shift)[None], (c_at - shift) % n_ctx, 0
            )
        return placed.reshape(n_ctx * rows, width_here)

    def swap_side(tensor, count, turn_last):
        piece = tensor.shape[0] // n_ctx
        columns = tensor.shape[1] // count
        placed = [jnp.zeros((piece, n_ctx * columns), f32)] * count
        if turn_last:
            placed[-1] = placed[-1].T
        for shift in range(n_ctx):
            sent = lax.dynamic_slice_in_dim(tensor, ((c_at + shift) % n_ctx) * piece, piece, 0)
            came = along(sent, shift)
            start = ((c_at - shift) % n_ctx) * columns
            for at in range(count):
                part = came[:, at * columns : (at + 1) * columns].astype(f32)
                turned_here = turn_last and at == count - 1
                placed[at] = lax.dynamic_update_slice_in_dim(
                    placed[at], part.T if turned_here else part, start, 0 if turned_here else 1
                )
        return placed

    def plane_pieces(tensor):
        return [tensor] + [across(tensor, m) for m in range(1, n_fsdp)]

    def gather_plane(tensor):
        return jnp.concatenate(plane_pieces(tensor), 0)

    def scatter_plane(*tensors, late=()):
        size = tensors[0].shape[0] // n_fsdp
        total = jnp.concatenate([tensor[:size] for tensor in tensors], 1)
        for m in range(1, n_fsdp):
            sent = jnp.concatenate(
                [tensor[m * size : (m + 1) * size].astype(bf16) for tensor in tensors], 1
            )
            total = total + after(across(sent, m), *late).astype(f32)
        return total.astype(bf16)

    def gather_tokens(own):
        return lax.all_gather(own, ("ctx", "tp"), axis=0, tiled=True)

    def scatter_tokens(partial):
        return lax.psum_scatter(
            partial.astype(bf16), ("ctx", "tp"), scatter_dimension=0, tiled=True
        ).astype(f32)

    order_row = span_order[0]
    positions = (
        order_row[:, None] * span_len + jnp.arange(span_len, dtype=jnp.int32)[None, :]
    ).reshape(-1)
    cosine, sine = rope_tables(positions)
    length = positions.shape[0]

    def own_rows(tensor):
        return reorder(lax.dynamic_slice_in_dim(tensor[0], t_at * span_len, span_len, 0))

    inputs_own = own_rows(block_in)
    cot_own = own_rows(cotangent)

    gains = jnp.stack([attn_gain, mlp_gain])
    gains = gather_plane_small(swap_small(gains, along, c_at, n_ctx), across, n_bits)
    gain_one, gain_two = gains[0].astype(f32), gains[1].astype(f32)

    heads_width = w_query.shape[1] // n_ctx
    attn_part = swap_columns(w_query, w_key, w_value, w_out.T)
    inputs_low = gather_tokens(after(inputs_own, attn_part))
    attn_pieces = plane_pieces(attn_part)
    attn_full = jnp.concatenate(attn_pieces, 0)
    gate_part = swap_columns(after(w_gate, inputs_low))
    late_part = swap_columns(after(w_up, gate_part), w_down.T)
    gate_full = gather_plane(gate_part)
    hidden_here = gate_full.shape[1]
    up_full = gather_plane(after(late_part, gate_full)[:, :hidden_here])
    down_full = gather_plane(after(late_part, up_full)[:, hidden_here:])
    qkv_full = attn_full[:, : 3 * heads_width]
    out_full = attn_full[:, 3 * heads_width :]

    heads_here = heads_width // HEAD_DIM
    normed_one, qkv = project(
        inputs_low, gain_one[None], cosine, sine, attn_pieces, heads_width, row_count
    )
    qkv = after(qkv, gate_part)
    attn_low, log_total, peaks = attend(order_row, qkv)
    head_max = peaks[:, 0, ::HEAD_DIM].reshape(-1)
    attn_low = after(attn_low, late_part, gate_full)
    attn_sum = scatter_tokens(dot_rt(attn_low, out_full))
    attn_sum = after(attn_sum, up_full)

    peak = head_max
    for step in range(n_bits):
        peak = jnp.maximum(peak, across(peak, 1 << step))
    head_peak = jnp.zeros((n_ctx * heads_here,), f32)
    for shift in range(n_ctx):
        head_peak = lax.dynamic_update_slice_in_dim(
            head_peak, along(peak, shift), ((c_at - shift) % n_ctx) * heads_here, 0
        )

    inputs_mine = inputs_own.astype(f32)
    resid = inputs_mine + attn_sum
    inv_two = lax.rsqrt(jnp.mean(resid * resid, -1, keepdims=True) + NORM_EPS)
    scaled_two = resid * inv_two
    normed_two = gather_tokens((scaled_two * gain_two).astype(bf16))
    cot_all = gather_tokens(after(cot_own, normed_two))
    gate_act = dot(normed_two, gate_full)
    up_act = dot(normed_two, up_full)
    sig_gate = jax.nn.sigmoid(gate_act)
    silu_gate = gate_act * sig_gate
    hidden = (silu_gate * up_act).astype(bf16)
    grad_hidden = dot(cot_all, down_full)
    silu_slope = sig_gate * (1.0 + gate_act * (1.0 - sig_gate))
    grad_gate = (grad_hidden * up_act * silu_slope).astype(bf16)
    grad_up = (grad_hidden * silu_gate).astype(bf16)
    back_two = (dot_rt(grad_gate, gate_full) + dot_rt(grad_up, up_full)).astype(bf16)
    grad_normed_two = scatter_tokens(back_two)
    hidden_late, gate_late, up_late = (after(g, back_two) for g in (hidden, grad_gate, grad_up))
    grad_w_down = dot_lt(cot_all, hidden_late)
    grad_w_gate = dot_lt(normed_two, gate_late)
    grad_w_up = dot_lt(normed_two, up_late)
    mlp_partial = dot_rt(hidden_late, down_full).astype(bf16)
    grad_normed_two = after(grad_normed_two, grad_w_down, grad_w_gate, grad_w_up, mlp_partial)

    grad_gain_two = jnp.sum(grad_normed_two * scaled_two, axis=0)
    weighted_two = grad_normed_two * gain_two
    grad_resid = cot_own.astype(f32) + inv_two * (
        weighted_two - scaled_two * jnp.mean(weighted_two * scaled_two, -1, keepdims=True)
    )
    grad_low = gather_tokens(grad_resid.astype(bf16))
    down_sum = scatter_plane(grad_w_down, late=(grad_normed_two,))
    grad_low = after(grad_low, down_sum)
    mlp_sum = scatter_tokens(after(mlp_partial, grad_low))
    block_out_mine = (resid + mlp_sum).astype(bf16)

    grad_attended = dot(grad_low, out_full).astype(bf16)
    down_out = swap_ctx(after(down_sum, grad_low)).T
    late_sum = scatter_plane(after(grad_w_gate, down_sum), grad_w_up, late=(grad_attended,))

    grad_proj = attend_back(order_row, qkv, grad_attended, log_total, cosine, sine)
    grad_proj = after(grad_proj, late_sum, down_out)
    back_one = dot_rt(grad_proj, qkv_full).astype(bf16)
    grad_normed_one = scatter_tokens(back_one)
    proj_late = after(grad_proj, back_one)
    attn_sum_grad = scatter_plane(dot_lt(normed_one, proj_late), dot_lt(grad_low, attn_low))
    gate_out, up_out = swap_side(after(late_sum, back_one), 2, False)
    query_out, key_out, value_out, out_proj_out = swap_side(after(attn_sum_grad, up_out), 4, True)
    inputs = inputs_low.astype(f32)
    inv_one = lax.rsqrt(jnp.mean(inputs * inputs, -1, keepdims=True) + NORM_EPS)
    grad_gain_one = jnp.sum(back_one.astype(f32) * (inputs * inv_one), axis=0)

    inv_mine = lax.rsqrt(jnp.mean(inputs_mine * inputs_mine, -1, keepdims=True) + NORM_EPS)
    scaled_one = inputs_mine * inv_mine
    weighted_one = grad_normed_one * gain_one
    input_grad_mine = grad_resid + inv_mine * (
        weighted_one - scaled_one * jnp.mean(weighted_one * scaled_one, -1, keepdims=True)
    )

    gain_grads = jnp.stack([grad_gain_one, grad_gain_two])
    gain_grads = gain_grads + twin(gain_grads)
    held = {m: gain_grads[:, m * feature_block : (m + 1) * feature_block] for m in range(n_fsdp)}
    for bit in [1 << step for step in range(n_bits)]:
        kept = [m for m in sorted(held) if not m & bit]
        came = across(jnp.concatenate([held[m | bit] for m in kept], 1), bit)
        held = {
            m: held[m] + came[:, at * feature_block : (at + 1) * feature_block]
            for at, m in enumerate(kept)
        }
    piece = feature_block // n_ctx
    gain_total = None
    for shift in range(n_ctx):
        came = along(
            lax.dynamic_slice_in_dim(held[0], ((c_at + shift) % n_ctx) * piece, piece, 1), shift
        )
        gain_total = came if gain_total is None else gain_total + came

    def both_cores(mine):
        mine = reorder(mine)
        other = twin(mine)
        first = jnp.where(t_at == 0, mine, other)
        second = jnp.where(t_at == 0, other, mine)
        return jnp.concatenate([first, second], 0)[None]

    factor = jnp.sqrt(clip_limit / jnp.maximum(clip_limit, head_peak))
    column_factor = jnp.repeat(factor, HEAD_DIM)
    clipped_query = w_query.astype(f32) * column_factor[None, :]
    clipped_key = w_key.astype(f32) * column_factor[None, :]
    return (
        both_cores(block_out_mine),
        both_cores(input_grad_mine),
        gain_total[0],
        query_out,
        key_out,
        value_out,
        out_proj_out,
        gain_total[1],
        gate_out,
        up_out,
        down_out,
        head_peak,
        clipped_query,
        clipped_key,
    )


def swap_small(gains, along, c_at, n_ctx):
    piece = gains.shape[1]
    placed = jnp.zeros((gains.shape[0], piece * n_ctx), gains.dtype)
    for shift in range(n_ctx):
        placed = lax.dynamic_update_slice_in_dim(
            placed, along(gains, shift), ((c_at - shift) % n_ctx) * piece, 1
        )
    return placed


def gather_plane_small(gains, across, n_bits):
    for step in range(n_bits):
        gains = jnp.concatenate([gains, across(gains, 1 << step)], 1)
    return gains


def solution(mesh):
    placed = (
        P("fsdp", "ctx", None),
        P("fsdp", None),
        P(("fsdp", "ctx")),
        P(("fsdp", "ctx"), "tp"),
        P(("fsdp", "ctx"), "tp"),
        P(("fsdp", "ctx"), "tp"),
        P("tp", ("fsdp", "ctx")),
        P(("fsdp", "ctx")),
        P(("fsdp", "ctx"), "tp"),
        P(("fsdp", "ctx"), "tp"),
        P("tp", ("fsdp", "ctx")),
        P("tp"),
        P("fsdp", "ctx", None),
    )
    return jax.shard_map(
        on_device,
        mesh=mesh,
        in_specs=placed,
        out_specs=(
            P("fsdp", "ctx", None),
            P("fsdp", "ctx", None),
            P(("fsdp", "ctx")),
            P(("fsdp", "ctx"), "tp"),
            P(("fsdp", "ctx"), "tp"),
            P(("fsdp", "ctx"), "tp"),
            P("tp", ("fsdp", "ctx")),
            P(("fsdp", "ctx")),
            P(("fsdp", "ctx"), "tp"),
            P(("fsdp", "ctx"), "tp"),
            P("tp", ("fsdp", "ctx")),
            P("tp"),
            P(("fsdp", "ctx"), "tp"),
            P(("fsdp", "ctx"), "tp"),
        ),
        check_vma=False,
    )
```

time: 1010 us -> 868 us (0.86)
  waiting for transfers between devices: 531 us -> 385 us
  matrix products: 176 us -> 118 us
  local copies, waits for them, and re-layouts: 94.3 us -> 130 us
  starting transfers between devices: 133 us -> 100 us
  Pallas kernels: 0 us -> 31.6 us
  other arithmetic: 60 us -> 77.8 us
  between operations: 4.1 us -> 16.3 us
    ppermute x69 -> x27, waiting for transfers between devices: 272 us -> 88.8 us  [along(): lax.ppermute(tensor, 'ctx', [(i, (i + shift) % n_ctx) for i in range(n_ct...]
    all_gather x0 -> x4, waiting for transfers between devices: none -> 42.6 us  [gather_tokens(): return lax.all_gather(own, ('ctx', 'tp'), axis=0, tiled=True)]
    dot_general x17 -> x5, matrix products: 84.5 us -> 49.9 us  [dot_rt(): lax.dot_general(left, right, (((1,), (1,)), ((), ())), preferred_element_...]
    pallas_call x0 -> x3, Pallas kernels: none -> 31.6 us  [the longest x1 13.2 us: attend_back(): pl.pallas_call(backward_kernel, grid_spec=pltpu.PrefetchScalarGridSpec(nu...]
    convert_element_type x6 -> x24, local copies, waits for them, and re-layouts: 2.92 us -> 33.2 us  [the longest x20 25.5 us: swap_side(): part = came[:, at * columns:(at + 1) * columns].astype(f32)]
    ppermute x46 -> x27, waiting for transfers between devices: 255 us -> 232 us  [across(): return lax.ppermute(tensor, 'fsdp', [(i, i ^ mask) for i in range(n_fsdp)])]
    reduce_scatter x0 -> x4, waiting for transfers between devices: none -> 21.4 us  [scatter_tokens(): lax.psum_scatter(partial.astype(bf16), ('ctx', 'tp'), scatter_dimension=0...]
    dot_general x13 -> x4, matrix products: 52.9 us -> 33.3 us  [dot(): return jnp.dot(left, right, preferred_element_type=f32)]
  transfers between devices with their start and end apart: 150 -> 65, of which waited for: 73 -> 32; matrix products, arithmetic and copies ran while one was open for 20% -> 27% of each run, Pallas kernels for 0% -> 4%
where the time goes in v2:
time: 868 us; the launch traced here: 859 us
  waiting for transfers between devices  385 us (44%)
  local copies, waits for them, and re-layouts  130 us (15%)
  matrix products  118 us (14%)
  starting transfers between devices  100 us (12%)
  other arithmetic  77.8 us (9%)
  Pallas kernels  31.6 us (4%)
  between operations  16.3 us (2%)
    ppermute x27, waiting for transfers between devices, across(): return lax.ppermute(tensor, 'fsdp', [(i, i ^ mask) for i in range(n_fsdp)])  232 us
    ppermute x27, waiting for transfers between devices, along(): lax.ppermute(tensor, 'ctx', [(i, (i + shift) % n_ctx) for i in range(n_ct...  88.8 us
    ppermute x27, starting transfers between devices, along(): lax.ppermute(tensor, 'ctx', [(i, (i + shift) % n_ctx) for i in range(n_ct...  65.7 us
    dot_general x5, matrix products, dot_rt(): lax.dot_general(left, right, (((1,), (1,)), ((), ())), preferred_element_...  49.9 us
    all_gather x4, waiting for transfers between devices, gather_tokens(): return lax.all_gather(own, ('ctx', 'tp'), axis=0, tiled=True)  42.6 us
    dot_general x5, matrix products, dot_lt(): lax.dot_general(left, right, (((0,), (0,)), ((), ())), preferred_element_...  35 us
    dot_general x4, matrix products, dot(): return jnp.dot(left, right, preferred_element_type=f32)  33.3 us
    ppermute x27, starting transfers between devices, across(): return lax.ppermute(tensor, 'fsdp', [(i, i ^ mask) for i in range(n_fsdp)])  32.9 us
  transfers between devices with their start and end apart: 65, of which 32 were waited for; matrix products, arithmetic and copies ran while one was open for 27% of the time, Pallas kernels for 4%

profile of v2, /device:TPU:0, one launch (start us, length us, event | category | flops | bytes accessed | tf_op | source)
XLA Modules:
  0.0 858.6 jit_solution(3482125094502201355)
XLA Ops:
  23.3 10.2 %collective-permute-done.1 = bf16[128,1024]{0,1:T(8,128)(2,1)S(1)} collective-permute-done((bf16[128,1024]{0,1:T(8,128)(2,1)S(1)}, bf16[128,1024]{0,1:T(8,128)(2,1)S(1)}, u32[]{:S(2)}, u32[]{:S(2)}) %collective-permute-start.1) | collective-permute-done | bytes 262176 | tf_op jit(solution)/shard_map/ppermute | solution.py:288
  34.1 6.0 collective-permute-start.3
  50.8 4.4 pad_maximum_fusion.20
  65.2 28.2 %collective-permute-done.7 = bf16[2,1024]{1,0:T(2,128)(2,1)S(1)} collective-permute-done((bf16[2,1024]{1,0:T(2,128)(2,1)S(1)}, bf16[2,1024]{1,0:T(2,128)(2,1)S(1)}, u32[]{:S(2)}, u32[]{:S(2)}) %collective-permute-start.7) | collective-permute-done | bytes 4128 | tf_op jit(solution)/shard_map/ppermute | solution.py:291
  104.3 8.7 %project.1 = (bf16[1024,2048]{1,0:T(8,128)(2,1)}, bf16[1024,768]{1,0:T(8,128)(2,1)}) custom-call(bf16[1024,2048]{1,0:T(8,128)(2,1)} %all-gather.5.cloned.1.call-done.x_ref, f32[1,2048]{1,0:T(1,128)S(1)} %get-tuple-element.230.gain_ref, f32[1024,128]{1,0:T(8,128)S(1)} %copy-done.2, f32[1024,128]{1,0:T(8,128)S(1)} %copy-done.4, ...), custom_call_target="tpu_custom_call" | custom-call | flops 3221225472 | bytes 12582912 | tf_op jit(solution)/shard_map/project/pallas_call | solution.py:80
  114.3 3.8 collective-permute-done.12
  121.9 5.4 collective-permute-start.14
  127.7 9.7 %attend.1 = (bf16[1024,256]{1,0:T(8,128)(2,1)S(1)}, f32[2,1024,128]{2,1,0:T(8,128)S(1)}, f32[2,8,128]{2,1,0:T(8,128)S(1)}) custom-call(s32[8]{0:T(128)S(1)} %bitcast.110, bf16[1024,768]{1,0:T(8,128)(2,1)S(1)} %copy-done.7, bf16[1024,768]{1,0:T(8,128)(2,1)S(1)} %copy-done.7, bf16[1024,768]{1,0:T(8,128)(2,1)S(1)} %copy-done.7), custom_call_target="tpu_custom_call" | custom-call | flops 4294967296 | bytes 2097152 | tf_op jit(solution)/shard_map/attend/pallas_call | solution.py:153
  143.8 14.6 %collective-permute-done.15 = bf16[128,2048]{1,0:T(8,128)(2,1)S(1)} collective-permute-done((bf16[128,2048]{1,0:T(8,128)(2,1)S(1)}, bf16[128,2048]{1,0:T(8,128)(2,1)S(1)}, u32[]{:S(2)}, u32[]{:S(2)}) %collective-permute-start.15) | collective-permute-done | bytes 524320 | tf_op jit(solution)/shard_map/ppermute | solution.py:288
  159.2 10.1 %collective-permute-done.16 = bf16[128,2048]{1,0:T(8,128)(2,1)S(1)} collective-permute-done((bf16[128,2048]{1,0:T(8,128)(2,1)S(1)}, bf16[128,2048]{1,0:T(8,128)(2,1)S(1)}, u32[]{:S(2)}, u32[]{:S(2)}) %collective-permute-start.16) | collective-permute-done | bytes 524320 | tf_op jit(solution)/shard_map/ppermute | solution.py:288
  172.1 3.3 convolution_convert_fusion
  180.3 23.5 %collective-permute-done.22 = bf16[512,1024]{1,0:T(8,128)(2,1)S(1)} collective-permute-done((bf16[512,1024]{1,0:T(8,128)(2,1)S(1)}, bf16[512,1024]{1,0:T(8,128)(2,1)S(1)}, u32[]{:S(2)}, u32[]{:S(2)}) %collective-permute-start.22) | collective-permute-done | bytes 1048608 | tf_op jit(solution)/shard_map/ppermute | solution.py:291
  203.8 14.2 %collective-permute-done.21 = bf16[512,1024]{1,0:T(8,128)(2,1)S(1)} collective-permute-done((bf16[512,1024]{1,0:T(8,128)(2,1)S(1)}, bf16[512,1024]{1,0:T(8,128)(2,1)S(1)}, u32[]{:S(2)}, u32[]{:S(2)}) %collective-permute-start.21) | collective-permute-done | bytes 1048608 | tf_op jit(solution)/shard_map/ppermute | solution.py:291
  219.0 7.6 reduce-scatter.5.cloned.1.call-done
  234.1 42.5 %all-gather.7.cloned.1.call-done = bf16[1024,2048]{1,0:T(8,128)(2,1)} async-done(((bf16[128,2048]{1,0:T(8,128)(2,1)}), bf16[1024,2048]{1,0:T(8,128)(2,1)}) %all-gather.7.cloned.1.call-update) | async-done | bytes 4194320 | tf_op jit(solution)/shard_map/all_gather | solution.py:369
  281.8 10.2 %fusion.35 = f32[1024,1024]{1,0:T(8,128)} fusion(bf16[1024,2048]{1,0:T(8,128)(2,1)} %all-gather.7.cloned.1.call-done, bf16[512,1024]{1,0:T(8,128)(2,1)} %copy-done.61, bf16[512,1024]{1,0:T(8,128)(2,1)} %copy-done.63, bf16[512,1024]{1,0:T(8,128)(2,1)} %collective-permute-done.20, bf16[512,1024]{1,0:T(8,128)(2,1)} %copy-done.34), kind=kOutput, calls=%fused_computation.236 | convolution fusion | flops 4311744512 | bytes 12582912 | tf_op jit(solution)/shard_map/dot_general | solution.py:35
  292.1 13.2 %collective-permute-done.25 = bf16[512,1024]{1,0:T(8,128)(2,1)S(1)} collective-permute-done((bf16[512,1024]{1,0:T(8,128)(2,1)S(1)}, bf16[512,1024]{1,0:T(8,128)(2,1)S(1)}, u32[]{:S(2)}, u32[]{:S(2)}) %collective-permute-start.25) | collective-permute-done | bytes 1048608 | tf_op jit(solution)/shard_map/ppermute | solution.py:291
  305.3 21.7 %collective-permute-done.24 = bf16[512,1024]{1,0:T(8,128)(2,1)S(1)} collective-permute-done((bf16[512,1024]{1,0:T(8,128)(2,1)S(1)}, bf16[512,1024]{1,0:T(8,128)(2,1)S(1)}, u32[]{:S(2)}, u32[]{:S(2)}) %collective-permute-start.24) | collective-permute-done | bytes 1048608 | tf_op jit(solution)/shard_map/ppermute | solution.py:291
  328.0 10.0 %fusion.21 = f32[1024,1024]{1,0:T(8,128)} fusion(bf16[1024,2048]{1,0:T(8,128)(2,1)} %all-gather.9.cloned.1.call-done, bf16[512,1024]{1,0:T(8,128)(2,1)} %copy-done.65, bf16[512,1024]{1,0:T(8,128)(2,1)} %copy-done.67, bf16[512,1024]{1,0:T(8,128)(2,1)} %collective-permute-done.23, bf16[512,1024]{1,0:T(8,128)(2,1)} %copy-done.36), kind=kOutput, calls=%fused_computation.63 | convolution fusion | flops 4311744512 | bytes 12582912 | tf_op jit(solution)/shard_map/dot_general | solution.py:35
  338.1 9.2 %multiply_convert_fusion.1 = (bf16[1024,1024]{1,0:T(8,128)(2,1)}, bf16[1024,1024]{1,0:T(8,128)(2,1)S(1)}, bf16[1024,1024]{1,0:T(8,128)(2,1)}) fusion(f32[1024,1024]{1,0:T(8,128)} %fusion.21, f32[1024,1024]{1,0:T(8,128)S(1)} %copy-done.72, bf16[1024,2048]{1,0:T(8,128)(2,1)S(1)} %copy-done.53, bf16[512,1024]{1,0:T(8,128)(2,1)S(1)} %copy-done.56, ...), kind=kOutput, calls=%fused_computation.14 | convolution fusion | flops 4327473152 | bytes 23068672 | tf_op jit(solution)/shard_map/dot_general | solution.py:35
  347.3 10.0 %fusion.34 = f32[1024,2048]{1,0:T(8,128)} fusion(bf16[1024,1024]{1,0:T(8,128)(2,1)S(1)} %get-tuple-element.59, bf16[512,1024]{1,0:T(8,128)(2,1)S(1)} %copy-done.62, bf16[512,1024]{1,0:T(8,128)(2,1)S(1)} %copy-done.64, bf16[512,1024]{1,0:T(8,128)(2,1)} %collective-permute-done.20, bf16[512,1024]{1,0:T(8,128)(2,1)S(1)} %copy-done.35), kind=kOutput, calls=%fused_computation.235 | convolution fusion | flops 4311744512 | bytes 14680064 | tf_op jit(solution)/shard_map/dot_general | solution.py:43
  357.3 11.3 %add_convert_fusion = bf16[1024,2048]{1,0:T(8,128)(2,1)} fusion(f32[1024,2048]{1,0:T(8,128)} %fusion.34, bf16[1024,1024]{1,0:T(8,128)(2,1)S(1)} %copy-done.75, bf16[512,1024]{1,0:T(8,128)(2,1)S(1)} %copy-done.56, bf16[512,1024]{1,0:T(8,128)(2,1)S(1)} %copy-done.58, bf16[512,1024]{1,0:T(8,128)(2,1)S(1)} %copy-done.60, bf16[512,1024]{1,0:T(8,128)(2,1)S(1)} %bitcast.118), kind=kOutput, calls=%fused_computation.5 | convolution fusion | flops 4315938816 | bytes 18874368 | tf_op jit(solution)/shard_map/dot_general | solution.py:43
  369.2 12.2 %fusion.44 = (bf16[2048,1024]{1,0:T(8,128)(2,1)}, f32[2048,1024]{1,0:T(8,128)}) fusion(bf16[1024,2048]{1,0:T(8,128)(2,1)} %all-gather.9.cloned.1.call-done, bf16[1024,1024]{1,0:T(8,128)(2,1)} %get-tuple-element.57), kind=kOutput, calls=%fused_computation.245 | convolution fusion | flops 4297064448 | bytes 18874368 | tf_op jit(solution)/shard_map/dot_general | solution.py:39
  381.4 6.8 fusion.47
  388.2 7.0 fusion.48
  395.3 7.8 convolution_convert_fusion.2
  403.1 13.8 %reduce-scatter.7.cloned.1.call-done = bf16[128,2048]{1,0:T(8,128)(2,1)} async-done(((bf16[1024,2048]{1,0:T(8,128)(2,1)}), bf16[128,2048]{1,0:T(8,128)(2,1)}) %reduce-scatter.7.cloned.1.call-update) | async-done | bytes 524304 | tf_op jit(solution)/shard_map/reduce_scatter | solution.py:372
  422.3 3.6 fusion.40
  429.4 9.4 %copy.144 = f32[2048,1024]{1,0:T(8,128)} copy(f32[2048,1024]{0,1:T(8,128)} %fusion.48) | data formatting | bytes 16777216 | tf_op jit(solution)/shard_map/dot_general | solution.py:39
  438.8 4.3 convert.32
  443.4 9.8 %collective-permute-done.28 = bf16[512,1024]{1,0:T(8,128)(2,1)} collective-permute-done((bf16[512,1024]{1,0:T(8,128)(2,1)}, bf16[512,1024]{1,0:T(8,128)(2,1)}, u32[]{:S(2)}, u32[]{:S(2)}) %collective-permute-start.28) | collective-permute-done | bytes 1048608 | tf_op jit(solution)/shard_map/ppermute | solution.py:291
  453.2 19.1 %collective-permute-done.27 = bf16[512,1024]{1,0:T(8,128)(2,1)} collective-permute-done((bf16[512,1024]{1,0:T(8,128)(2,1)}, bf16[512,1024]{1,0:T(8,128)(2,1)}, u32[]{:S(2)}, u32[]{:S(2)}) %collective-permute-start.27) | collective-permute-done | bytes 1048608 | tf_op jit(solution)/shard_map/ppermute | solution.py:291
  472.4 4.2 fusion.10
  488.7 3.9 convolution_convert_fusion.3.g_ref
  492.6 36.2 %collective-permute-done.32 = bf16[512,2048]{1,0:T(8,128)(2,1)} collective-permute-done((bf16[512,2048]{1,0:T(8,128)(2,1)}, bf16[512,2048]{1,0:T(8,128)(2,1)}, u32[]{:S(2)}, u32[]{:S(2)}) %collective-permute-start.32) | collective-permute-done | bytes 2097184 | tf_op jit(solution)/shard_map/ppermute | solution.py:291
  528.8 43.9 %collective-permute-done.31 = bf16[512,2048]{1,0:T(8,128)(2,1)} collective-permute-done((bf16[512,2048]{1,0:T(8,128)(2,1)}, bf16[512,2048]{1,0:T(8,128)(2,1)}, u32[]{:S(2)}, u32[]{:S(2)}) %collective-permute-start.31) | collective-permute-done | bytes 2097184 | tf_op jit(solution)/shard_map/ppermute | solution.py:291
  572.8 13.2 %attend_back.1 = bf16[1024,768]{1,0:T(8,128)(2,1)S(1)} custom-call(s32[8]{0:T(128)S(1)} %bitcast.111, bf16[1024,768]{1,0:T(8,128)(2,1)S(1)} %copy-done.8, bf16[1024,768]{1,0:T(8,128)(2,1)S(1)} %copy-done.8, bf16[1024,768]{1,0:T(8,128)(2,1)S(1)} %copy-done.8, bf16[1024,256]{1,0:T(8,128)(2,1)S(1)} %convolution_convert_fusion.3.g_ref, ...), custom_call_target="tpu_custom_call" | custom-call | flops 10737418240 | bytes 4194304 | tf_op jit(solution)/shard_map/attend_back/pallas_call | solution.py:231
  593.4 5.9 fusion.5
  618.4 17.5 %fusion.2 = (f32[2048]{0:T(1024)S(1)}, bf16[1024,2048]{1,0:T(8,128)(2,1)}) fusion(bf16[1024,2048]{1,0:T(8,128)(2,1)} %all-gather.5.cloned.1.call-done.x_ref, f32[1024]{0:T(1024)S(1)} %add_rsqrt_fusion, bf16[1024,768]{1,0:T(8,128)(2,1)} %copy-done.9, bf16[512,1024]{1,0:T(8,128)(2,1)} %collective-permute-done.10.refs_3_, ...), kind=kOutput, calls=%fused_computation.4 | convolution fusion | flops 3246389248 | bytes 14168064 | tf_op jit(solution)/shard_map/dot_general | solution.py:43
  645.0 4.8 collective-permute-start.54
  649.8 3.4 collective-permute-start.55
  658.6 3.5 fusion.45
  664.0 5.4 fusion.46
  683.1 16.0 %collective-permute-done.38 = f32[2,1024]{1,0:T(2,128)S(1)} collective-permute-done((f32[2,1024]{1,0:T(2,128)S(1)}, f32[2,1024]{1,0:T(2,128)S(1)}, u32[]{:S(2)}, u32[]{:S(2)}) %collective-permute-start.38) | collective-permute-done | bytes 8224 | tf_op jit(solution)/shard_map/ppermute | solution.py:291
  715.4 33.2 %collective-permute-done.47 = bf16[128,2048]{1,0:T(8,128)(2,1)S(1)} collective-permute-done((bf16[128,2048]{1,0:T(8,128)(2,1)S(1)}, bf16[128,2048]{1,0:T(8,128)(2,1)S(1)}, u32[]{:S(2)}, u32[]{:S(2)}) %collective-permute-start.47) | collective-permute-done | bytes 524320 | tf_op jit(solution)/shard_map/ppermute | solution.py:288
  777.2 15.4 %collective-permute-start.49 = (bf16[128,1024]{0,1:T(8,128)(2,1)}, bf16[128,1024]{0,1:T(8,128)(2,1)}, u32[]{:S(2)}, u32[]{:S(2)}) collective-permute-start(bf16[128,1024]{0,1:T(8,128)(2,1)} %get-tuple-element.157), channel_id=1, source_target_pairs={{0,2},{2,4},{4,6},{6,0},{1,3},{3,5},{5,7},{7,1},{8,10},{10,12},{12... | collective-permute-start | bytes 786440 | tf_op jit(solution)/shard_map/ppermute | solution.py:288
  792.6 3.5 collective-permute-start.50
  805.8 6.3 collective-permute-done.50
  (474 shorter events, 254.1 us)
Async XLA Ops:
  7.2 90.0 %all-gather.5.cloned.1.call-start = ((), (), s32[]{:S(2)}) async-start(), calls=%async_computation.4 | async-start | bytes 4718592 | tf_op jit(solution)/shard_map/all_gather | solution.py:369
  14.2 19.3 %collective-permute-start.1 = (bf16[128,1024]{0,1:T(8,128)(2,1)S(1)}, bf16[128,1024]{0,1:T(8,128)(2,1)S(1)}, u32[]{:S(2)}, u32[]{:S(2)}) collective-permute-start(bf16[128,1024]{0,1:T(8,128)(2,1)S(1)} %pad_maximum_fusion.28), channel_id=1, source_target_pairs={{0,4},{2,6},{4,0},{6,2},{1,5},{3,7},{5,1},{7,3},{8,12},{10,14},{12... | collective-permute-start | bytes 786440 | tf_op jit(solution)/shard_map/ppermute | solution.py:288
  17.3 16.4 %collective-permute-start.2 = (bf16[128,1024]{0,1:T(8,128)(2,1)S(1)}, bf16[128,1024]{0,1:T(8,128)(2,1)S(1)}, u32[]{:S(2)}, u32[]{:S(2)}) collective-permute-start(bf16[128,1024]{0,1:T(8,128)(2,1)S(1)} %pad_maximum_fusion.29), channel_id=1, source_target_pairs={{0,6},{2,0},{4,2},{6,4},{1,7},{3,1},{5,3},{7,5},{8,14},{10,8},{12,... | collective-permute-start | bytes 786440 | tf_op jit(solution)/shard_map/ppermute | solution.py:288
  34.0 192.7 %reduce-scatter.5.cloned.1.call-start = ((), (), s32[]{:S(2)}) async-start(), calls=%async_computation.5 | async-start | bytes 4718592 | tf_op jit(solution)/shard_map/reduce_scatter | solution.py:372
  47.3 46.2 %collective-permute-start.8 = (bf16[512,1024]{1,0:T(8,128)(2,1)S(1)}, bf16[512,1024]{1,0:T(8,128)(2,1)S(1)}, u32[]{:S(2)}, u32[]{:S(2)}) collective-permute-start(bf16[512,1024]{1,0:T(8,128)(2,1)S(1)} %bitcast.102), channel_id=1, source_target_pairs={{0,8},{8,0},{16,24},{24,16},{1,9},{9,1},{17,25},{25,17},{2,10},{10... | collective-permute-start | bytes 3145736 | tf_op jit(solution)/shard_map/ppermute | solution.py:291
  47.9 45.6 %collective-permute-start.9 = (bf16[512,1024]{1,0:T(8,128)(2,1)S(1)}, bf16[512,1024]{1,0:T(8,128)(2,1)S(1)}, u32[]{:S(2)}, u32[]{:S(2)}) collective-permute-start(bf16[512,1024]{1,0:T(8,128)(2,1)S(1)} %bitcast.103), channel_id=1, source_target_pairs={{0,16},{8,24},{16,0},{24,8},{1,17},{9,25},{17,1},{25,9},{2,18},{10... | collective-permute-start | bytes 3145736 | tf_op jit(solution)/shard_map/ppermute | solution.py:291
  49.4 45.7 %collective-permute-start.10 = (bf16[512,1024]{1,0:T(8,128)(2,1)S(1)}, bf16[512,1024]{1,0:T(8,128)(2,1)}, u32[]{:S(2)}, u32[]{:S(2)}) collective-permute-start(bf16[512,1024]{1,0:T(8,128)(2,1)S(1)} %bitcast.104), channel_id=1, source_target_pairs={{0,24},{8,16},{16,8},{24,0},{1,25},{9,17},{17,9},{25,1},{2,26},{10... | collective-permute-start | bytes 3145736 | tf_op jit(solution)/shard_map/ppermute | solution.py:291
  55.3 38.2 %collective-permute-start.7 = (bf16[2,1024]{1,0:T(2,128)(2,1)S(1)}, bf16[2,1024]{1,0:T(2,128)(2,1)S(1)}, u32[]{:S(2)}, u32[]{:S(2)}) collective-permute-start(bf16[2,1024]{1,0:T(2,128)(2,1)S(1)} %pad_maximum_fusion.33), channel_id=1, source_target_pairs={{0,16},{8,24},{16,0},{24,8},{1,17},{9,25},{17,1},{25,9},{2,18},{10... | collective-permute-start | bytes 12296 | tf_op jit(solution)/shard_map/ppermute | solution.py:291
  98.4 19.7 %collective-permute-start.12 = (bf16[128,1024]{1,0:T(8,128)(2,1)S(1)}, bf16[128,1024]{1,0:T(8,128)(2,1)S(1)}, u32[]{:S(2)}, u32[]{:S(2)}) collective-permute-start(bf16[128,1024]{1,0:T(8,128)(2,1)S(1)} %get-tuple-element.186), channel_id=1, source_target_pairs={{0,4},{2,6},{4,0},{6,2},{1,5},{3,7},{5,1},{7,3},{8,12},{10,14},{12... | collective-permute-start | bytes 786440 | tf_op jit(solution)/shard_map/ppermute | solution.py:288
  100.6 17.5 %collective-permute-start.13 = (bf16[128,1024]{1,0:T(8,128)(2,1)S(1)}, bf16[128,1024]{1,0:T(8,128)(2,1)S(1)}, u32[]{:S(2)}, u32[]{:S(2)}) collective-permute-start(bf16[128,1024]{1,0:T(8,128)(2,1)S(1)} %get-tuple-element.185), channel_id=1, source_target_pairs={{0,6},{2,0},{4,2},{6,4},{1,7},{3,1},{5,3},{7,5},{8,14},{10,8},{12,... | collective-permute-start | bytes 786440 | tf_op jit(solution)/shard_map/ppermute | solution.py:288
  118.2 51.9 %collective-permute-start.19 = (bf16[512,1024]{1,0:T(8,128)(2,1)S(1)}, bf16[512,1024]{1,0:T(8,128)(2,1)S(1)}, u32[]{:S(2)}, u32[]{:S(2)}) collective-permute-start(bf16[512,1024]{1,0:T(8,128)(2,1)S(1)} %bitcast.114), channel_id=1, source_target_pairs={{0,24},{8,16},{16,8},{24,0},{1,25},{9,17},{17,9},{25,1},{2,26},{10... | collective-permute-start | bytes 3145736 | tf_op jit(solution)/shard_map/ppermute | solution.py:291
  118.8 51.3 %collective-permute-start.18 = (bf16[512,1024]{1,0:T(8,128)(2,1)S(1)}, bf16[512,1024]{1,0:T(8,128)(2,1)S(1)}, u32[]{:S(2)}, u32[]{:S(2)}) collective-permute-start(bf16[512,1024]{1,0:T(8,128)(2,1)S(1)} %bitcast.115), channel_id=1, source_target_pairs={{0,16},{8,24},{16,0},{24,8},{1,17},{9,25},{17,1},{25,9},{2,18},{10... | collective-permute-start | bytes 3145736 | tf_op jit(solution)/shard_map/ppermute | solution.py:291
  120.3 49.9 %collective-permute-start.17 = (bf16[512,1024]{1,0:T(8,128)(2,1)S(1)}, bf16[512,1024]{1,0:T(8,128)(2,1)S(1)}, u32[]{:S(2)}, u32[]{:S(2)}) collective-permute-start(bf16[512,1024]{1,0:T(8,128)(2,1)S(1)} %bitcast.116), channel_id=1, source_target_pairs={{0,8},{8,0},{16,24},{24,16},{1,9},{9,1},{17,25},{25,17},{2,10},{10... | collective-permute-start | bytes 3145736 | tf_op jit(solution)/shard_map/ppermute | solution.py:291
  121.9 19.0 %collective-permute-start.14 = (bf16[128,2048]{1,0:T(8,128)(2,1)S(1)}, bf16[128,2048]{1,0:T(8,128)(2,1)S(1)}, u32[]{:S(2)}, u32[]{:S(2)}) collective-permute-start(bf16[128,2048]{1,0:T(8,128)(2,1)S(1)} %pad_maximum_fusion.22), channel_id=1, source_target_pairs={{0,2},{2,4},{4,6},{6,0},{1,3},{3,5},{5,7},{7,1},{8,10},{10,12},{12... | collective-permute-start | bytes 1572872 | tf_op jit(solution)/shard_map/ppermute | solution.py:288
  127.3 31.1 %collective-permute-start.15 = (bf16[128,2048]{1,0:T(8,128)(2,1)S(1)}, bf16[128,2048]{1,0:T(8,128)(2,1)S(1)}, u32[]{:S(2)}, u32[]{:S(2)}) collective-permute-start(bf16[128,2048]{1,0:T(8,128)(2,1)S(1)} %pad_maximum_fusion.23), channel_id=1, source_target_pairs={{0,4},{2,6},{4,0},{6,2},{1,5},{3,7},{5,1},{7,3},{8,12},{10,14},{12... | collective-permute-start | bytes 1572872 | tf_op jit(solution)/shard_map/ppermute | solution.py:288
  140.9 28.4 %collective-permute-start.16 = (bf16[128,2048]{1,0:T(8,128)(2,1)S(1)}, bf16[128,2048]{1,0:T(8,128)(2,1)S(1)}, u32[]{:S(2)}, u32[]{:S(2)}) collective-permute-start(bf16[128,2048]{1,0:T(8,128)(2,1)S(1)} %pad_maximum_fusion.24), channel_id=1, source_target_pairs={{0,6},{2,0},{4,2},{6,4},{1,7},{3,1},{5,3},{7,5},{8,14},{10,8},{12,... | collective-permute-start | bytes 1572872 | tf_op jit(solution)/shard_map/ppermute | solution.py:288
  175.4 101.3 %all-gather.7.cloned.1.call-start = ((), (), s32[]{:S(2)}) async-start(), calls=%async_computation.6 | async-start | bytes 4718592 | tf_op jit(solution)/shard_map/all_gather | solution.py:369
  176.7 27.1 %collective-permute-start.22 = (bf16[512,1024]{1,0:T(8,128)(2,1)S(1)}, bf16[512,1024]{1,0:T(8,128)(2,1)S(1)}, u32[]{:S(2)}, u32[]{:S(2)}) collective-permute-start(bf16[512,1024]{1,0:T(8,128)(2,1)S(1)} %slice.194), channel_id=1, source_target_pairs={{0,24},{8,16},{16,8},{24,0},{1,25},{9,17},{17,9},{25,1},{2,26},{10... | collective-permute-start | bytes 3145736 | tf_op jit(solution)/shard_map/ppermute | solution.py:291
  177.4 40.7 %collective-permute-start.21 = (bf16[512,1024]{1,0:T(8,128)(2,1)S(1)}, bf16[512,1024]{1,0:T(8,128)(2,1)S(1)}, u32[]{:S(2)}, u32[]{:S(2)}) collective-permute-start(bf16[512,1024]{1,0:T(8,128)(2,1)S(1)} %slice.194), channel_id=1, source_target_pairs={{0,16},{8,24},{16,0},{24,8},{1,17},{9,25},{17,1},{25,9},{2,18},{10... | collective-permute-start | bytes 3145736 | tf_op jit(solution)/shard_map/ppermute | solution.py:291
  178.8 40.2 %collective-permute-start.20 = (bf16[512,1024]{1,0:T(8,128)(2,1)S(1)}, bf16[512,1024]{1,0:T(8,128)(2,1)}, u32[]{:S(2)}, u32[]{:S(2)}) collective-permute-start(bf16[512,1024]{1,0:T(8,128)(2,1)S(1)} %slice.194), channel_id=1, source_target_pairs={{0,8},{8,0},{16,24},{24,16},{1,9},{9,1},{17,25},{25,17},{2,10},{10... | collective-permute-start | bytes 3145736 | tf_op jit(solution)/shard_map/ppermute | solution.py:291
  231.0 96.9 %all-gather.9.cloned.1.call-start = ((), (), s32[]{:S(2)}) async-start(), calls=%async_computation.7 | async-start | bytes 4718592 | tf_op jit(solution)/shard_map/all_gather | solution.py:369
  276.7 140.2 %reduce-scatter.7.cloned.1.call-start = ((), (), s32[]{:S(2)}) async-start(), calls=%async_computation.8 | async-start | bytes 4718592 | tf_op jit(solution)/shard_map/reduce_scatter | solution.py:372
  278.2 27.0 %collective-permute-start.25 = (bf16[512,1024]{1,0:T(8,128)(2,1)S(1)}, bf16[512,1024]{1,0:T(8,128)(2,1)S(1)}, u32[]{:S(2)}, u32[]{:S(2)}) collective-permute-start(bf16[512,1024]{1,0:T(8,128)(2,1)S(1)} %slice.196), channel_id=1, source_target_pairs={{0,24},{8,16},{16,8},{24,0},{1,25},{9,17},{17,9},{25,1},{2,26},{10... | collective-permute-start | bytes 3145736 | tf_op jit(solution)/shard_map/ppermute | solution.py:291
  280.7 46.3 %collective-permute-start.24 = (bf16[512,1024]{1,0:T(8,128)(2,1)S(1)}, bf16[512,1024]{1,0:T(8,128)(2,1)S(1)}, u32[]{:S(2)}, u32[]{:S(2)}) collective-permute-start(bf16[512,1024]{1,0:T(8,128)(2,1)S(1)} %slice.196), channel_id=1, source_target_pairs={{0,16},{8,24},{16,0},{24,8},{1,17},{9,25},{17,1},{25,9},{2,18},{10... | collective-permute-start | bytes 3145736 | tf_op jit(solution)/shard_map/ppermute | solution.py:291
  281.2 46.7 %collective-permute-start.23 = (bf16[512,1024]{1,0:T(8,128)(2,1)S(1)}, bf16[512,1024]{1,0:T(8,128)(2,1)}, u32[]{:S(2)}, u32[]{:S(2)}) collective-permute-start(bf16[512,1024]{1,0:T(8,128)(2,1)S(1)} %slice.196), channel_id=1, source_target_pairs={{0,8},{8,0},{16,24},{24,16},{1,9},{9,1},{17,25},{25,17},{2,10},{10... | collective-permute-start | bytes 3145736 | tf_op jit(solution)/shard_map/ppermute | solution.py:291
  368.7 120.0 %all-gather.11.cloned.1.call-start = ((), (), s32[]{:S(2)}) async-start(), calls=%async_computation.9 | async-start | bytes 4718592 | tf_op jit(solution)/shard_map/all_gather | solution.py:369
  422.2 419.5 %reduce-scatter.11.cloned.1.call-start = ((), (), s32[]{:S(2)}) async-start(), calls=%async_computation.11 | async-start | bytes 4718592 | tf_op jit(solution)/shard_map/reduce_scatter | solution.py:372
  425.9 27.3 %collective-permute-start.28 = (bf16[512,1024]{1,0:T(8,128)(2,1)}, bf16[512,1024]{1,0:T(8,128)(2,1)}, u32[]{:S(2)}, u32[]{:S(2)}) collective-permute-start(bf16[512,1024]{1,0:T(8,128)(2,1)} %get-tuple-element.140), channel_id=1, source_target_pairs={{0,24},{8,16},{16,8},{24,0},{1,25},{9,17},{17,9},{25,1},{2,26},{10... | collective-permute-start | bytes 3145736 | tf_op jit(solution)/shard_map/ppermute | solution.py:291
  428.3 44.0 %collective-permute-start.27 = (bf16[512,1024]{1,0:T(8,128)(2,1)}, bf16[512,1024]{1,0:T(8,128)(2,1)}, u32[]{:S(2)}, u32[]{:S(2)}) collective-permute-start(bf16[512,1024]{1,0:T(8,128)(2,1)} %get-tuple-element.141), channel_id=1, source_target_pairs={{0,16},{8,24},{16,0},{24,8},{1,17},{9,25},{17,1},{25,9},{2,18},{10... | collective-permute-start | bytes 3145736 | tf_op jit(solution)/shard_map/ppermute | solution.py:291
  428.8 43.6 %collective-permute-start.26 = (bf16[512,1024]{1,0:T(8,128)(2,1)}, bf16[512,1024]{1,0:T(8,128)(2,1)}, u32[]{:S(2)}, u32[]{:S(2)}) collective-permute-start(bf16[512,1024]{1,0:T(8,128)(2,1)} %get-tuple-element.139), channel_id=1, source_target_pairs={{0,8},{8,0},{16,24},{24,16},{1,9},{9,1},{17,25},{25,17},{2,10},{10... | collective-permute-start | bytes 3145736 | tf_op jit(solution)/shard_map/ppermute | solution.py:291
  479.1 49.8 %collective-permute-start.32 = (bf16[512,2048]{1,0:T(8,128)(2,1)}, bf16[512,2048]{1,0:T(8,128)(2,1)}, u32[]{:S(2)}, u32[]{:S(2)}) collective-permute-start(bf16[512,2048]{1,0:T(8,128)(2,1)} %pad_maximum_fusion.11), channel_id=1, source_target_pairs={{0,24},{8,16},{16,8},{24,0},{1,25},{9,17},{17,9},{25,1},{2,26},{10... | collective-permute-start | bytes 6291464 | tf_op jit(solution)/shard_map/ppermute | solution.py:291
  482.3 90.5 %collective-permute-start.31 = (bf16[512,2048]{1,0:T(8,128)(2,1)}, bf16[512,2048]{1,0:T(8,128)(2,1)}, u32[]{:S(2)}, u32[]{:S(2)}) collective-permute-start(bf16[512,2048]{1,0:T(8,128)(2,1)} %pad_maximum_fusion.10), channel_id=1, source_target_pairs={{0,16},{8,24},{16,0},{24,8},{1,17},{9,25},{17,1},{25,9},{2,18},{10... | collective-permute-start | bytes 6291464 | tf_op jit(solution)/shard_map/ppermute | solution.py:291
  485.0 101.0 %collective-permute-start.30 = (bf16[512,2048]{1,0:T(8,128)(2,1)}, bf16[512,2048]{1,0:T(8,128)(2,1)}, u32[]{:S(2)}, u32[]{:S(2)}) collective-permute-start(bf16[512,2048]{1,0:T(8,128)(2,1)} %pad_maximum_fusion.9), channel_id=1, source_target_pairs={{0,8},{8,0},{16,24},{24,16},{1,9},{9,1},{17,25},{25,17},{2,10},{10... | collective-permute-start | bytes 6291464 | tf_op jit(solution)/shard_map/ppermute | solution.py:291
  587.3 17.3 %collective-permute-start.33 = (bf16[128,1024]{1,0:T(8,128)(2,1)}, bf16[128,1024]{1,0:T(8,128)(2,1)}, u32[]{:S(2)}, u32[]{:S(2)}) collective-permute-start(bf16[128,1024]{1,0:T(8,128)(2,1)} %get-tuple-element.169), channel_id=1, source_target_pairs={{0,2},{2,4},{4,6},{6,0},{1,3},{3,5},{5,7},{7,1},{8,10},{10,12},{12... | collective-permute-start | bytes 786440 | tf_op jit(solution)/shard_map/ppermute | solution.py:288
  588.5 20.5 %collective-permute-start.34 = (bf16[128,1024]{1,0:T(8,128)(2,1)}, bf16[128,1024]{1,0:T(8,128)(2,1)}, u32[]{:S(2)}, u32[]{:S(2)}) collective-permute-start(bf16[128,1024]{1,0:T(8,128)(2,1)} %get-tuple-element.168), channel_id=1, source_target_pairs={{0,4},{2,6},{4,0},{6,2},{1,5},{3,7},{5,1},{7,3},{8,12},{10,14},{12... | collective-permute-start | bytes 786440 | tf_op jit(solution)/shard_map/ppermute | solution.py:288
  590.8 23.8 %collective-permute-start.35 = (bf16[128,1024]{1,0:T(8,128)(2,1)}, bf16[128,1024]{1,0:T(8,128)(2,1)}, u32[]{:S(2)}, u32[]{:S(2)}) collective-permute-start(bf16[128,1024]{1,0:T(8,128)(2,1)} %get-tuple-element.167), channel_id=1, source_target_pairs={{0,6},{2,0},{4,2},{6,4},{1,7},{3,1},{5,3},{7,5},{8,14},{10,8},{12,... | collective-permute-start | bytes 786440 | tf_op jit(solution)/shard_map/ppermute | solution.py:288
  635.9 207.3 %reduce-scatter.9.cloned.1.call-start = ((), (), s32[]{:S(2)}) async-start(), calls=%async_computation.10 | async-start | bytes 4718592 | tf_op jit(solution)/shard_map/reduce_scatter | solution.py:372
  663.9 17.3 %collective-permute-start.37 = (f32[2,2048]{1,0:T(2,128)S(1)}, f32[2,2048]{1,0:T(2,128)S(1)}, u32[]{:S(2)}, u32[]{:S(2)}) collective-permute-start(f32[2,2048]{1,0:T(2,128)S(1)} %pad_maximum_fusion.30), channel_id=1, source_target_pairs={{0,1},{1,0},{2,3},{3,2},{4,5},{5,4},{6,7},{7,6},{8,9},{9,8},{10,11... | collective-permute-start | bytes 49160 | tf_op jit(solution)/shard_map/ppermute | solution.py:294
  672.9 100.6 %collective-permute-start.45 = (bf16[512,1024]{0,1:T(8,128)(2,1)}, bf16[512,1024]{0,1:T(8,128)(2,1)}, u32[]{:S(2)}, u32[]{:S(2)}) collective-permute-start(bf16[512,1024]{0,1:T(8,128)(2,1)} %pad_maximum_fusion.16), channel_id=1, source_target_pairs={{0,24},{8,16},{16,8},{24,0},{1,25},{9,17},{17,9},{25,1},{2,26},{10... | collective-permute-start | bytes 3145736 | tf_op jit(solution)/shard_map/ppermute | solution.py:291
  678.8 33.6 %collective-permute-start.46 = (bf16[128,2048]{1,0:T(8,128)(2,1)}, bf16[128,2048]{1,0:T(8,128)(2,1)}, u32[]{:S(2)}, u32[]{:S(2)}) collective-permute-start(bf16[128,2048]{1,0:T(8,128)(2,1)} %get-tuple-element.149), channel_id=1, source_target_pairs={{0,2},{2,4},{4,6},{6,0},{1,3},{3,5},{5,7},{7,1},{8,10},{10,12},{12... | collective-permute-start | bytes 1572872 | tf_op jit(solution)/shard_map/ppermute | solution.py:288
  681.3 17.8 %collective-permute-start.38 = (f32[2,1024]{1,0:T(2,128)S(1)}, f32[2,1024]{1,0:T(2,128)S(1)}, u32[]{:S(2)}, u32[]{:S(2)}) collective-permute-start(f32[2,1024]{1,0:T(2,128)S(1)} %pad_maximum_fusion.32), channel_id=1, source_target_pairs={{0,8},{8,0},{16,24},{24,16},{1,9},{9,1},{17,25},{25,17},{2,10},{10... | collective-permute-start | bytes 24584 | tf_op jit(solution)/shard_map/ppermute | solution.py:291
  706.5 67.0 %collective-permute-start.44 = (bf16[512,1024]{0,1:T(8,128)(2,1)}, bf16[512,1024]{0,1:T(8,128)(2,1)}, u32[]{:S(2)}, u32[]{:S(2)}) collective-permute-start(bf16[512,1024]{0,1:T(8,128)(2,1)} %pad_maximum_fusion.15), channel_id=1, source_target_pairs={{0,16},{8,24},{16,0},{24,8},{1,17},{9,25},{17,1},{25,9},{2,18},{10... | collective-permute-start | bytes 3145736 | tf_op jit(solution)/shard_map/ppermute | solution.py:291
  709.2 39.4 %collective-permute-start.47 = (bf16[128,2048]{1,0:T(8,128)(2,1)S(1)}, bf16[128,2048]{1,0:T(8,128)(2,1)S(1)}, u32[]{:S(2)}, u32[]{:S(2)}) collective-permute-start(bf16[128,2048]{1,0:T(8,128)(2,1)S(1)} %copy-done.47), channel_id=1, source_target_pairs={{0,4},{2,6},{4,0},{6,2},{1,5},{3,7},{5,1},{7,3},{8,12},{10,14},{12... | collective-permute-start | bytes 1572872 | tf_op jit(solution)/shard_map/ppermute | solution.py:288
  710.1 43.6 %collective-permute-start.48 = (bf16[128,2048]{1,0:T(8,128)(2,1)}, bf16[128,2048]{1,0:T(8,128)(2,1)}, u32[]{:S(2)}, u32[]{:S(2)}) collective-permute-start(bf16[128,2048]{1,0:T(8,128)(2,1)} %get-tuple-element.147), channel_id=1, source_target_pairs={{0,6},{2,0},{4,2},{6,4},{1,7},{3,1},{5,3},{7,5},{8,14},{10,8},{12,... | collective-permute-start | bytes 1572872 | tf_op jit(solution)/shard_map/ppermute | solution.py:288
  712.5 61.0 %collective-permute-start.43 = (bf16[512,1024]{0,1:T(8,128)(2,1)}, bf16[512,1024]{0,1:T(8,128)(2,1)}, u32[]{:S(2)}, u32[]{:S(2)}) collective-permute-start(bf16[512,1024]{0,1:T(8,128)(2,1)} %pad_maximum_fusion.14), channel_id=1, source_target_pairs={{0,8},{8,0},{16,24},{24,16},{1,9},{9,1},{17,25},{25,17},{2,10},{10... | collective-permute-start | bytes 3145736 | tf_op jit(solution)/shard_map/ppermute | solution.py:291
  777.2 26.0 %collective-permute-start.49 = (bf16[128,1024]{0,1:T(8,128)(2,1)}, bf16[128,1024]{0,1:T(8,128)(2,1)}, u32[]{:S(2)}, u32[]{:S(2)}) collective-permute-start(bf16[128,1024]{0,1:T(8,128)(2,1)} %get-tuple-element.157), channel_id=1, source_target_pairs={{0,2},{2,4},{4,6},{6,0},{1,3},{3,5},{5,7},{7,1},{8,10},{10,12},{12... | collective-permute-start | bytes 786440 | tf_op jit(solution)/shard_map/ppermute | solution.py:288
  792.6 19.5 %collective-permute-start.50 = (bf16[128,1024]{0,1:T(8,128)(2,1)}, bf16[128,1024]{0,1:T(8,128)(2,1)}, u32[]{:S(2)}, u32[]{:S(2)}) collective-permute-start(bf16[128,1024]{0,1:T(8,128)(2,1)} %get-tuple-element.156), channel_id=1, source_target_pairs={{0,4},{2,6},{4,0},{6,2},{1,5},{3,7},{5,1},{7,3},{8,12},{10,14},{12... | collective-permute-start | bytes 786440 | tf_op jit(solution)/shard_map/ppermute | solution.py:288
  796.1 19.3 %collective-permute-start.51 = (bf16[128,1024]{0,1:T(8,128)(2,1)}, bf16[128,1024]{0,1:T(8,128)(2,1)}, u32[]{:S(2)}, u32[]{:S(2)}) collective-permute-start(bf16[128,1024]{0,1:T(8,128)(2,1)} %get-tuple-element.155), channel_id=1, source_target_pairs={{0,6},{2,0},{4,2},{6,4},{1,7},{3,1},{5,3},{7,5},{8,14},{10,8},{12,... | collective-permute-start | bytes 786440 | tf_op jit(solution)/shard_map/ppermute | solution.py:288
  (98 other events, 1479.4 us)
Sparse Core Ops, SparseCore 0:
  34.1 51.9 all-gather.4
  175.5 51.0 reduce-scatter.4
  231.1 45.4 all-gather.6
  278.7 45.8 all-gather.8
  368.8 48.0 reduce-scatter.6
  422.4 45.2 all-gather.10
  636.0 60.0 reduce-scatter.10
  698.4 78.5 reduce-scatter.8

commit v3 on v2

--- a/solution.py
+++ b/solution.py
@@ -41,6 +41,47 @@
 
 def dot_rt(left, right):
     return lax.dot_general(left, right, (((1,), (1,)), ((), ())), preferred_element_type=f32)
+
+
+def place_kernel(count, ways, at_ref, *refs):
+    pieces = len(refs) - count
+    slot = lax.rem(at_ref[0] + pieces - pl.program_id(0), pieces)
+    for at in range(pieces):
+
+        @pl.when(slot == at)
+        def _(source=refs[at]):
+            columns = source.shape[1] // count
+            for which in range(count):
+                part = source[:, which * columns : (which + 1) * columns]
+                target = refs[pieces + which]
+                part = part.astype(target.dtype)
+                target[...] = part.T if ways[which] == "turned" else part
+
+
+def place(at, pieces, count, ways, dtype):
+    slots = len(pieces)
+    rows, columns = pieces[0].shape
+    columns = columns // count
+    shapes = {
+        "down": ((slots * rows, columns), (rows, columns), lambda b, at: (b, 0)),
+        "side": ((rows, slots * columns), (rows, columns), lambda b, at: (0, b)),
+        "turned": ((slots * columns, rows), (columns, rows), lambda b, at: (b, 0)),
+    }
+    return pl.pallas_call(
+        functools.partial(place_kernel, count, ways),
+        grid_spec=pltpu.PrefetchScalarGridSpec(
+            num_scalar_prefetch=1,
+            grid=(slots,),
+            in_specs=[pl.BlockSpec(piece.shape, lambda b, at: (0, 0)) for piece in pieces],
+            out_specs=[pl.BlockSpec(shapes[way][1], shapes[way][2]) for way in ways],
+        ),
+        out_shape=[jax.ShapeDtypeStruct(shapes[way][0], dtype) for way in ways],
+        compiler_params=pltpu.CompilerParams(vmem_limit_bytes=VMEM_LIMIT),
+        cost_estimate=pl.CostEstimate(
+            flops=0, bytes_accessed=6 * slots * rows * columns * count, transcendentals=0
+        ),
+        name="place",
+    )(at.astype(jnp.int32)[None], *pieces)
 
 
 def turn(pair, cosine, sine):
@@ -88,7 +129,7 @@
         out_specs=(rows(width), rows(3 * heads_width)),
         compiler_params=pltpu.CompilerParams(vmem_limit_bytes=VMEM_LIMIT),
         cost_estimate=pl.CostEstimate(
-            flops=6 * length * width * heads_width,
+            flops=length * width * heads_width,
             bytes_accessed=4 * length * width + 8 * width * heads_width,
             transcendentals=length,
         ),
@@ -170,9 +211,9 @@
         ),
         compiler_params=pltpu.CompilerParams(vmem_limit_bytes=VMEM_LIMIT),
         cost_estimate=pl.CostEstimate(
-            flops=16 * pairs * length * length * PAIR,
+            flops=2 * pairs * length * length * PAIR,
             bytes_accessed=8 * pairs * length * PAIR,
-            transcendentals=2 * pairs * length * length,
+            transcendentals=pairs * length,
         ),
         name="attend",
     )(order, qkv, qkv, qkv)
@@ -249,9 +290,9 @@
         out_shape=jax.ShapeDtypeStruct(qkv.shape, bf16),
         compiler_params=pltpu.CompilerParams(vmem_limit_bytes=VMEM_LIMIT),
         cost_estimate=pl.CostEstimate(
-            flops=40 * pairs * length * length * PAIR,
+            flops=2 * pairs * length * length * PAIR,
             bytes_accessed=16 * pairs * length * PAIR,
-            transcendentals=2 * pairs * length * length,
+            transcendentals=pairs * length,
         ),
         name="attend_back",
     )(order, qkv, qkv, qkv, grad, logs, cosine, sine)
@@ -305,73 +346,52 @@
             -1,
         )
 
-    def swap_ctx(tensor):
+    def swap_columns(*tensors, late=()):
+        piece = tensors[0].shape[1] // n_ctx
+        came = []
+        for shift in range(n_ctx):
+            start = ((c_at + shift) % n_ctx) * piece
+            sent = [lax.dynamic_slice_in_dim(tensor, start, piece, 1) for tensor in tensors]
+            came.append(after(along(jnp.concatenate(sent, 1), shift), *late))
+        return place(c_at, came, 1, ("down",), bf16)[0]
+
+    def swap_rows(tensor, ways, late=()):
         piece = tensor.shape[0] // n_ctx
-        columns = tensor.shape[1]
-        placed = jnp.zeros((piece, n_ctx * columns), f32)
+        came = []
         for shift in range(n_ctx):
             sent = lax.dynamic_slice_in_dim(tensor, ((c_at + shift) % n_ctx) * piece, piece, 0)
-            placed = lax.dynamic_update_slice_in_dim(
-                placed, along(sent, shift).astype(f32), ((c_at - shift) % n_ctx) * columns, 1
-            )
-        return placed
-
-    def swap_columns(*tensors):
-        rows, columns = tensors[0].shape
-        piece = columns // n_ctx
-        width_here = piece * len(tensors)
-        placed = jnp.zeros((n_ctx, rows, width_here), tensors[0].dtype)
-        for shift in range(n_ctx):
-            start = ((c_at + shift) % n_ctx) * piece
-            sent = jnp.concatenate(
-                [lax.dynamic_slice_in_dim(tensor, start, piece, 1) for tensor in tensors], 1
-            )
-            placed = lax.dynamic_update_slice_in_dim(
-                placed, along(sent, shift)[None], (c_at - shift) % n_ctx, 0
-            )
-        return placed.reshape(n_ctx * rows, width_here)
-
-    def swap_side(tensor, count, turn_last):
-        piece = tensor.shape[0] // n_ctx
-        columns = tensor.shape[1] // count
-        placed = [jnp.zeros((piece, n_ctx * columns), f32)] * count
-        if turn_last:
-            placed[-1] = placed[-1].T
-        for shift in range(n_ctx):
-            sent = lax.dynamic_slice_in_dim(tensor, ((c_at + shift) % n_ctx) * piece, piece, 0)
-            came = along(sent, shift)
-            start = ((c_at - shift) % n_ctx) * columns
-            for at in range(count):
-                part = came[:, at * columns : (at + 1) * columns].astype(f32)
-                turned_here = turn_last and at == count - 1
-                placed[at] = lax.dynamic_update_slice_in_dim(
-                    placed[at], part.T if turned_here else part, start, 0 if turned_here else 1
-                )
-        return placed
-
-    def plane_pieces(tensor):
-        return [tensor] + [across(tensor, m) for m in range(1, n_fsdp)]
-
-    def gather_plane(tensor):
-        return jnp.concatenate(plane_pieces(tensor), 0)
+            came.append(after(along(sent, shift), *late))
+        return place(c_at, came, len(ways), ways, f32)
+
+    def plane_pieces(tensor, late=()):
+        if n_fsdp != 4:
+            return [tensor] + [after(across(tensor, m), *late) for m in range(1, n_fsdp)]
+        half = tensor.shape[0] // 2
+        near_x, near_y = across(tensor, 1), across(tensor, 2)
+        far = [across(near_x[:half], 2), across(near_y[half:], 1)]
+        pieces = [tensor, near_x, near_y, jnp.concatenate(far, 0)]
+        return [after(piece, *late) for piece in pieces]
+
+    def gather_plane(tensor, late=()):
+        return jnp.concatenate(plane_pieces(tensor, late), 0)
 
     def scatter_plane(*tensors, late=()):
         size = tensors[0].shape[0] // n_fsdp
-        total = jnp.concatenate([tensor[:size] for tensor in tensors], 1)
+
+        def block(m):
+            parts = [tensor[m * size : (m + 1) * size] for tensor in tensors]
+            return jnp.concatenate(parts, 1) if len(parts) > 1 else parts[0]
+
+        total = block(0).astype(f32)
         for m in range(1, n_fsdp):
-            sent = jnp.concatenate(
-                [tensor[m * size : (m + 1) * size].astype(bf16) for tensor in tensors], 1
-            )
-            total = total + after(across(sent, m), *late).astype(f32)
+            total = total + after(across(block(m), m), *late).astype(f32)
         return total.astype(bf16)
 
     def gather_tokens(own):
         return lax.all_gather(own, ("ctx", "tp"), axis=0, tiled=True)
 
     def scatter_tokens(partial):
-        return lax.psum_scatter(
-            partial.astype(bf16), ("ctx", "tp"), scatter_dimension=0, tiled=True
-        ).astype(f32)
+        return lax.psum_scatter(partial.astype(bf16), ("ctx", "tp"), scatter_dimension=0, tiled=True)
 
     order_row = span_order[0]
     positions = (
@@ -388,19 +408,15 @@
 
     gains = jnp.stack([attn_gain, mlp_gain])
     gains = gather_plane_small(swap_small(gains, along, c_at, n_ctx), across, n_bits)
-    gain_one, gain_two = gains[0].astype(f32), gains[1].astype(f32)
+    gains_wide = gains.astype(f32)
+    gain_one, gain_two = gains_wide[0], gains_wide[1]
 
     heads_width = w_query.shape[1] // n_ctx
-    attn_part = swap_columns(w_query, w_key, w_value, w_out.T)
-    inputs_low = gather_tokens(after(inputs_own, attn_part))
+    attn_part = after(swap_columns(w_query, w_key, w_value, w_out.T), gains)
     attn_pieces = plane_pieces(attn_part)
     attn_full = jnp.concatenate(attn_pieces, 0)
-    gate_part = swap_columns(after(w_gate, inputs_low))
-    late_part = swap_columns(after(w_up, gate_part), w_down.T)
-    gate_full = gather_plane(gate_part)
-    hidden_here = gate_full.shape[1]
-    up_full = gather_plane(after(late_part, gate_full)[:, :hidden_here])
-    down_full = gather_plane(after(late_part, up_full)[:, hidden_here:])
+    gate_part = swap_columns(after(w_gate, attn_part))
+    inputs_low = after(gather_tokens(after(inputs_own, attn_part)), gate_part, attn_full)
     qkv_full = attn_full[:, : 3 * heads_width]
     out_full = attn_full[:, 3 * heads_width :]
 
@@ -408,45 +424,45 @@
     normed_one, qkv = project(
         inputs_low, gain_one[None], cosine, sine, attn_pieces, heads_width, row_count
     )
-    qkv = after(qkv, gate_part)
+    up_part = swap_columns(after(w_up, inputs_low), late=(qkv,))
     attn_low, log_total, peaks = attend(order_row, qkv)
+    down_part = swap_columns(after(w_down.T, up_part))
+    gate_full = gather_plane(after(gate_part, attn_full, inputs_low), late=(attn_low,))
+    up_full = gather_plane(after(up_part, gate_full))
+    down_full = gather_plane(after(down_part, up_full))
+    attn_low = after(attn_low, up_part, gate_full)
     head_max = peaks[:, 0, ::HEAD_DIM].reshape(-1)
-    attn_low = after(attn_low, late_part, gate_full)
     attn_sum = scatter_tokens(dot_rt(attn_low, out_full))
-    attn_sum = after(attn_sum, up_full)
-
-    peak = head_max
-    for step in range(n_bits):
-        peak = jnp.maximum(peak, across(peak, 1 << step))
-    head_peak = jnp.zeros((n_ctx * heads_here,), f32)
-    for shift in range(n_ctx):
-        head_peak = lax.dynamic_update_slice_in_dim(
-            head_peak, along(peak, shift), ((c_at - shift) % n_ctx) * heads_here, 0
-        )
+    attn_sum = after(attn_sum, down_part, up_full)
 
     inputs_mine = inputs_own.astype(f32)
-    resid = inputs_mine + attn_sum
+    resid = inputs_mine + attn_sum.astype(f32)
     inv_two = lax.rsqrt(jnp.mean(resid * resid, -1, keepdims=True) + NORM_EPS)
     scaled_two = resid * inv_two
-    normed_two = gather_tokens((scaled_two * gain_two).astype(bf16))
-    cot_all = gather_tokens(after(cot_own, normed_two))
+    normed_mine = (scaled_two * gain_two).astype(bf16)
+    normed_two = gather_tokens(normed_mine)
+    cot_all = gather_tokens(after(cot_own, normed_mine))
+    normed_two = after(normed_two, down_full)
     gate_act = dot(normed_two, gate_full)
     up_act = dot(normed_two, up_full)
     sig_gate = jax.nn.sigmoid(gate_act)
     silu_gate = gate_act * sig_gate
     hidden = (silu_gate * up_act).astype(bf16)
-    grad_hidden = dot(cot_all, down_full)
+    mlp_partial = dot_rt(hidden, down_full).astype(bf16)
+    mlp_sum = scatter_tokens(mlp_partial)
+    grad_hidden = dot(after(cot_all, mlp_partial), down_full)
     silu_slope = sig_gate * (1.0 + gate_act * (1.0 - sig_gate))
     grad_gate = (grad_hidden * up_act * silu_slope).astype(bf16)
     grad_up = (grad_hidden * silu_gate).astype(bf16)
     back_two = (dot_rt(grad_gate, gate_full) + dot_rt(grad_up, up_full)).astype(bf16)
+    hidden_late, gate_late, up_late = (after(g, back_two) for g in (hidden, grad_gate, grad_up))
+    grad_w_down = dot_lt(cot_all, hidden_late).astype(bf16)
+    back_two, mlp_sum = lax.optimization_barrier((back_two, mlp_sum))
     grad_normed_two = scatter_tokens(back_two)
-    hidden_late, gate_late, up_late = (after(g, back_two) for g in (hidden, grad_gate, grad_up))
-    grad_w_down = dot_lt(cot_all, hidden_late)
-    grad_w_gate = dot_lt(normed_two, gate_late)
-    grad_w_up = dot_lt(normed_two, up_late)
-    mlp_partial = dot_rt(hidden_late, down_full).astype(bf16)
-    grad_normed_two = after(grad_normed_two, grad_w_down, grad_w_gate, grad_w_up, mlp_partial)
+    grad_w_gate = dot_lt(normed_two, gate_late).astype(bf16)
+    grad_w_up = dot_lt(normed_two, up_late).astype(bf16)
+    down_sum = scatter_plane(grad_w_down)
+    grad_normed_two = after(grad_normed_two, down_sum, grad_w_gate, grad_w_up).astype(f32)
 
     grad_gain_two = jnp.sum(grad_normed_two * scaled_two, axis=0)
     weighted_two = grad_normed_two * gain_two
@@ -454,26 +470,30 @@
         weighted_two - scaled_two * jnp.mean(weighted_two * scaled_two, -1, keepdims=True)
     )
     grad_low = gather_tokens(grad_resid.astype(bf16))
-    down_sum = scatter_plane(grad_w_down, late=(grad_normed_two,))
-    grad_low = after(grad_low, down_sum)
-    mlp_sum = scatter_tokens(after(mlp_partial, grad_low))
-    block_out_mine = (resid + mlp_sum).astype(bf16)
+    gate_sum = scatter_plane(after(grad_w_gate, down_sum))
+    (down_out,) = swap_rows(down_sum, ("turned",))
+    grad_low = after(grad_low, gate_sum, down_out)
+    block_out_mine = (resid + mlp_sum.astype(f32)).astype(bf16)
 
     grad_attended = dot(grad_low, out_full).astype(bf16)
-    down_out = swap_ctx(after(down_sum, grad_low)).T
-    late_sum = scatter_plane(after(grad_w_gate, down_sum), grad_w_up, late=(grad_attended,))
-
     grad_proj = attend_back(order_row, qkv, grad_attended, log_total, cosine, sine)
-    grad_proj = after(grad_proj, late_sum, down_out)
-    back_one = dot_rt(grad_proj, qkv_full).astype(bf16)
+    up_sum = scatter_plane(after(grad_w_up, gate_sum), late=(grad_proj,))
+    (gate_out,) = swap_rows(after(gate_sum, grad_low), ("side",), late=(grad_proj,))
+    back_one = dot_rt(after(grad_proj, up_sum, gate_out), qkv_full).astype(bf16)
     grad_normed_one = scatter_tokens(back_one)
-    proj_late = after(grad_proj, back_one)
-    attn_sum_grad = scatter_plane(dot_lt(normed_one, proj_late), dot_lt(grad_low, attn_low))
-    gate_out, up_out = swap_side(after(late_sum, back_one), 2, False)
-    query_out, key_out, value_out, out_proj_out = swap_side(after(attn_sum_grad, up_out), 4, True)
+    proj_late, attn_late, back_late = (after(g, back_one) for g in (grad_proj, attn_low, back_one))
+    grad_w_qkv = dot_lt(normed_one, proj_late).astype(bf16)
+    grad_w_out = dot_lt(grad_low, attn_late).astype(bf16)
+    (up_out,) = swap_rows(after(up_sum, back_one), ("side",))
+    attn_weight_sum = scatter_plane(grad_w_qkv, grad_w_out, late=(up_out,))
+    query_out, key_out, value_out, out_proj_out = swap_rows(
+        attn_weight_sum, ("side", "side", "side", "turned")
+    )
     inputs = inputs_low.astype(f32)
     inv_one = lax.rsqrt(jnp.mean(inputs * inputs, -1, keepdims=True) + NORM_EPS)
-    grad_gain_one = jnp.sum(back_one.astype(f32) * (inputs * inv_one), axis=0)
+    back_late = after(back_late, grad_w_qkv, grad_w_out)
+    grad_gain_one = jnp.sum(back_late.astype(f32) * (inputs * inv_one), axis=0)
+    grad_normed_one = after(grad_normed_one, grad_w_qkv, grad_w_out).astype(f32)
 
     inv_mine = lax.rsqrt(jnp.mean(inputs_mine * inputs_mine, -1, keepdims=True) + NORM_EPS)
     scaled_one = inputs_mine * inv_mine
@@ -482,23 +502,31 @@
         weighted_one - scaled_one * jnp.mean(weighted_one * scaled_one, -1, keepdims=True)
     )
 
-    gain_grads = jnp.stack([grad_gain_one, grad_gain_two])
+    gain_grads = after(jnp.stack([grad_gain_one, grad_gain_two]), attn_weight_sum)
     gain_grads = gain_grads + twin(gain_grads)
+    peak = head_max[None]
     held = {m: gain_grads[:, m * feature_block : (m + 1) * feature_block] for m in range(n_fsdp)}
     for bit in [1 << step for step in range(n_bits)]:
         kept = [m for m in sorted(held) if not m & bit]
-        came = across(jnp.concatenate([held[m | bit] for m in kept], 1), bit)
+        sent = [held[m | bit].reshape(1, -1) for m in kept]
+        came = across(jnp.concatenate(sent + [peak], 1), bit)
+        size = 2 * feature_block
         held = {
-            m: held[m] + came[:, at * feature_block : (at + 1) * feature_block]
+            m: held[m] + came[:, at * size : (at + 1) * size].reshape(2, feature_block)
             for at, m in enumerate(kept)
         }
+        peak = jnp.maximum(peak, came[:, len(kept) * size :])
     piece = feature_block // n_ctx
     gain_total = None
+    head_peak = jnp.zeros((n_ctx * heads_here,), f32)
     for shift in range(n_ctx):
-        came = along(
-            lax.dynamic_slice_in_dim(held[0], ((c_at + shift) % n_ctx) * piece, piece, 1), shift
+        sent = lax.dynamic_slice_in_dim(held[0], ((c_at + shift) % n_ctx) * piece, piece, 1)
+        came = along(jnp.concatenate([sent.reshape(1, -1), peak], 1), shift)
+        part = came[:, : 2 * piece].reshape(2, piece)
+        gain_total = part if gain_total is None else gain_total + part
+        head_peak = lax.dynamic_update_slice_in_dim(
+            head_peak, came[0, 2 * piece :], ((c_at - shift) % n_ctx) * heads_here, 0
         )
-        gain_total = came if gain_total is None else gain_total + came
 
     def both_cores(mine):
         mine = reorder(mine)

time: 868 us -> 688 us (0.79)
  local copies, waits for them, and re-layouts: 130 us -> 38.8 us
  waiting for transfers between devices: 385 us -> 351 us
  other arithmetic: 77.8 us -> 49.9 us
  matrix products: 118 us -> 92.1 us
    ppermute x27 -> x32, waiting for transfers between devices: 232 us -> 176 us  [across(): return lax.ppermute(tensor, 'fsdp', [(i, i ^ mask) for i in range(n_fsdp)])]
    ppermute x27 -> x30, waiting for transfers between devices: 88.8 us -> 125 us  [along(): lax.ppermute(tensor, 'ctx', [(i, (i + shift) % n_ctx) for i in range(n_ct...]
    convert_element_type x24 -> x0, local copies, waits for them, and re-layouts: 33.2 us -> none  [the longest x20 25.5 us: swap_side(): part = came[:, at * columns:(at + 1) * columns].astype(f32)]
    dynamic_update_slice x38 -> x3, local copies, waits for them, and re-layouts: 32.5 us -> 0.44 us  [on_device(): lax.dynamic_update_slice_in_dim(head_peak, came[0, 2 * piece:], (c_at - s...]
    all_gather x4, waiting for transfers between devices: 42.6 us -> 28.1 us  [gather_tokens(): return lax.all_gather(own, ('ctx', 'tp'), axis=0, tiled=True)]
    dot_general x5, matrix products: 49.9 us -> 36.7 us  [dot_rt(): lax.dot_general(left, right, (((1,), (1,)), ((), ())), preferred_element_...]
    ppermute x27 -> x30, starting transfers between devices: 65.7 us -> 53 us  [along(): lax.ppermute(tensor, 'ctx', [(i, (i + shift) % n_ctx) for i in range(n_ct...]
    convert_element_type x11 -> x1, other arithmetic: 14.3 us -> 2.05 us  [on_device(): normed_mine = (scaled_two * gain_two).astype(bf16)]
  transfers between devices with their start and end apart: 65 -> 73, of which waited for: 32 -> 30; matrix products, arithmetic and copies ran while one was open for 27% -> 22% of each run, Pallas kernels for 4% -> 6%
where the time goes in v3:
time: 688 us; the launch traced here: 681 us
  waiting for transfers between devices  351 us (51%)
  starting transfers between devices  93.9 us (14%)
  matrix products  92.1 us (13%)
  other arithmetic  49.9 us (7%)
  Pallas kernels  39.6 us (6%)
  local copies, waits for them, and re-layouts  38.8 us (6%)
  between operations  15.5 us (2%)
    ppermute x32, waiting for transfers between devices, across(): return lax.ppermute(tensor, 'fsdp', [(i, i ^ mask) for i in range(n_fsdp)])  176 us
    ppermute x30, waiting for transfers between devices, along(): lax.ppermute(tensor, 'ctx', [(i, (i + shift) % n_ctx) for i in range(n_ct...  125 us
    ppermute x30, starting transfers between devices, along(): lax.ppermute(tensor, 'ctx', [(i, (i + shift) % n_ctx) for i in range(n_ct...  53 us
    ppermute x32, starting transfers between devices, across(): return lax.ppermute(tensor, 'fsdp', [(i, i ^ mask) for i in range(n_fsdp)])  38.7 us
    dot_general x5, matrix products, dot_rt(): lax.dot_general(left, right, (((1,), (1,)), ((), ())), preferred_element_...  36.7 us
    dot_general x4, matrix products, dot(): return jnp.dot(left, right, preferred_element_type=f32)  28.1 us
    all_gather x4, waiting for transfers between devices, gather_tokens(): return lax.all_gather(own, ('ctx', 'tp'), axis=0, tiled=True)  28.1 us
    dot_general x5, matrix products, dot_lt(): lax.dot_general(left, right, (((0,), (0,)), ((), ())), preferred_element_...  27.3 us
  transfers between devices with their start and end apart: 73, of which 30 were waited for; matrix products, arithmetic and copies ran while one was open for 22% of the time, Pallas kernels for 6%

profile of v3, /device:TPU:0, one launch (start us, length us, event | category | flops | bytes accessed | tf_op | source)
XLA Modules:
  0.0 681.2 jit_solution(14799894308747489143)
XLA Ops:
  7.9 4.1 collective-permute-start.4
  22.2 3.3 collective-permute-start.2
  33.6 4.8 collective-permute-done.1.refs_2_
  44.5 20.6 %collective-permute-done.12.refs_2_ = bf16[512,1024]{1,0:T(8,128)(2,1)S(1)} collective-permute-done((bf16[512,1024]{1,0:T(8,128)(2,1)S(1)}, bf16[512,1024]{1,0:T(8,128)(2,1)S(1)}, u32[]{:S(2)}, u32[]{:S(2)}) %collective-permute-start.12) | collective-permute-done | bytes 1048608 | tf_op jit(solution)/shard_map/ppermute | solution.py:332
  71.0 6.2 collective-permute-start.9
  77.2 14.1 %collective-permute-done.10.refs_3_ = bf16[128,1024]{1,0:T(8,128)(2,1)S(1)} collective-permute-done((bf16[128,1024]{1,0:T(8,128)(2,1)S(1)}, bf16[128,1024]{1,0:T(8,128)(2,1)S(1)}, u32[]{:S(2)}, u32[]{:S(2)}) %collective-permute-start.10) | collective-permute-done | bytes 262176 | tf_op jit(solution)/shard_map/ppermute | solution.py:329
  91.3 19.2 %collective-permute-done.9.refs_2_ = bf16[128,1024]{1,0:T(8,128)(2,1)S(1)} collective-permute-done((bf16[128,1024]{1,0:T(8,128)(2,1)S(1)}, bf16[128,1024]{1,0:T(8,128)(2,1)S(1)}, u32[]{:S(2)}, u32[]{:S(2)}) %collective-permute-start.9) | collective-permute-done | bytes 262176 | tf_op jit(solution)/shard_map/ppermute | solution.py:329
  123.8 16.2 %collective-permute-done.19 = bf16[512,1024]{1,0:T(8,128)(2,1)S(1)} collective-permute-done((bf16[512,1024]{1,0:T(8,128)(2,1)}, bf16[512,1024]{1,0:T(8,128)(2,1)S(1)}, u32[]{:S(2)}, u32[]{:S(2)}) %collective-permute-start.19) | collective-permute-done | bytes 1048608 | tf_op jit(solution)/shard_map/ppermute | solution.py:332
  143.9 8.3 %project.1 = (bf16[1024,2048]{1,0:T(8,128)(2,1)}, bf16[1024,768]{1,0:T(8,128)(2,1)}) custom-call(bf16[1024,2048]{1,0:T(8,128)(2,1)} %all-gather.5.cloned.1.call-done.x_ref, f32[1,2048]{1,0:T(1,128)S(1)} %get-tuple-element.229.gain_ref, f32[1024,128]{1,0:T(8,128)S(1)} %get-tuple-element.249.cosine_ref, f32[1024,128]{1,0:T(8,128)S(1)} %get-tuple-element.250.sine_ref, ...), custom_call_target="tpu_custom_call" | custom-call | flops 536870912 | bytes 12582912 | tf_op jit(solution)/shard_map/project/pallas_call | solution.py:121
  153.6 9.7 %attend.1 = (bf16[1024,256]{1,0:T(8,128)(2,1)S(1)}, f32[2,1024,128]{2,1,0:T(8,128)S(1)}, f32[2,8,128]{2,1,0:T(8,128)S(1)}) custom-call(s32[8]{0:T(128)S(1)} %bitcast.95, bf16[1024,768]{1,0:T(8,128)(2,1)S(1)} %copy-done, bf16[1024,768]{1,0:T(8,128)(2,1)S(1)} %copy-done, bf16[1024,768]{1,0:T(8,128)(2,1)S(1)} %copy-done), custom_call_target="tpu_custom_call" | custom-call | flops 536870912 | bytes 2097152 | tf_op jit(solution)/shard_map/attend/pallas_call | solution.py:194
  167.9 4.6 convolution_convert_fusion
  174.2 21.5 %collective-permute-done.26 = bf16[512,1024]{1,0:T(8,128)(2,1)S(1)} collective-permute-done((bf16[512,1024]{1,0:T(8,128)(2,1)S(1)}, bf16[512,1024]{1,0:T(8,128)(2,1)S(1)}, u32[]{:S(2)}, u32[]{:S(2)}) %collective-permute-start.26) | collective-permute-done | bytes 1048608 | tf_op jit(solution)/shard_map/ppermute | solution.py:332
  205.8 11.7 %collective-permute-done.24.refs_3_ = bf16[128,1024]{1,0:T(8,128)(2,1)S(1)} collective-permute-done((bf16[128,1024]{1,0:T(8,128)(2,1)S(1)}, bf16[128,1024]{1,0:T(8,128)(2,1)S(1)}, u32[]{:S(2)}, u32[]{:S(2)}) %collective-permute-start.24) | collective-permute-done | bytes 262176 | tf_op jit(solution)/shard_map/ppermute | solution.py:329
  217.4 21.9 %collective-permute-done.23.refs_2_ = bf16[128,1024]{1,0:T(8,128)(2,1)S(1)} collective-permute-done((bf16[128,1024]{1,0:T(8,128)(2,1)S(1)}, bf16[128,1024]{1,0:T(8,128)(2,1)S(1)}, u32[]{:S(2)}, u32[]{:S(2)}) %collective-permute-start.23) | collective-permute-done | bytes 262176 | tf_op jit(solution)/shard_map/ppermute | solution.py:329
  252.3 20.7 %collective-permute-done.30 = bf16[512,1024]{1,0:T(8,128)(2,1)S(1)} collective-permute-done((bf16[512,1024]{1,0:T(8,128)(2,1)}, bf16[512,1024]{1,0:T(8,128)(2,1)S(1)}, u32[]{:S(2)}, u32[]{:S(2)}) %collective-permute-start.30) | collective-permute-done | bytes 1048608 | tf_op jit(solution)/shard_map/ppermute | solution.py:332
  275.6 9.8 %collective-permute-done.32 = bf16[256,1024]{1,0:T(8,128)(2,1)S(1)} collective-permute-done((bf16[256,1024]{1,0:T(8,128)(2,1)S(1)}, bf16[256,1024]{1,0:T(8,128)(2,1)S(1)}, u32[]{:S(2)}, u32[]{:S(2)}) %collective-permute-start.32) | collective-permute-done | bytes 524320 | tf_op jit(solution)/shard_map/ppermute | solution.py:332
  286.5 5.5 all-gather.9.cloned.1.call-done
  292.0 7.6 %fusion.40 = f32[1024,1024]{1,0:T(8,128)S(1)} fusion(bf16[1024,2048]{1,0:T(8,128)(2,1)} %all-gather.9.cloned.1.call-done, bf16[2048,1024]{1,0:T(8,128)(2,1)} %constant_dynamic-update-slice_fusion.4), kind=kOutput, calls=%fused_computation.204 | convolution fusion | flops 4294967296 | bytes 12582912 | tf_op jit(solution)/shard_map/dot_general | solution.py:35
  299.7 6.5 multiply_convert_fusion.2
  307.5 9.1 %convolution_convert_fusion.5 = bf16[1024,2048]{1,0:T(8,128)(2,1)} fusion(bf16[1024,1024]{1,0:T(8,128)(2,1)S(1)} %get-tuple-element.99, bf16[512,1024]{1,0:T(8,128)(2,1)S(1)} %copy-done.37, bf16[512,1024]{1,0:T(8,128)(2,1)S(1)} %copy-done.47, bf16[512,1024]{1,0:T(8,128)(2,1)S(1)} %copy-done.49, bf16[512,1024]{1,0:T(8,128)(2,1)S(1)} %copy-done.12), kind=kOutput, calls=%fused_computation.19 | convolution fusion | flops 4313841664 | bytes 10485760 | tf_op jit(solution)/shard_map/dot_general | solution.py:43
  317.3 22.6 %all-gather.7.cloned.1.call-done = bf16[1024,2048]{1,0:T(8,128)(2,1)} async-done(((bf16[128,2048]{1,0:T(8,128)(2,1)}), bf16[1024,2048]{1,0:T(8,128)(2,1)}) %all-gather.7.cloned.1.call-update) | async-done | bytes 4194320 | tf_op jit(solution)/shard_map/all_gather | solution.py:391
  339.9 10.2 %multiply_convert_fusion = (bf16[1024,1024]{1,0:T(8,128)(2,1)S(1)}, bf16[1024,1024]{1,0:T(8,128)(2,1)S(1)}) fusion(f32[1024,1024]{1,0:T(8,128)} %copy-done.63, f32[1024,1024]{1,0:T(8,128)} %get-tuple-element.244, bf16[1024,2048]{1,0:T(8,128)(2,1)} %all-gather.7.cloned.1.call-done, bf16[512,1024]{1,0:T(8,128)(2,1)} %pad_maximum_fusion.6, ...), kind=kOutput, calls=%fused_computation.9 | convolution fusion | flops 4325376000 | bytes 20971520 | tf_op jit(solution)/shard_map/dot_general | solution.py:35
  350.2 6.9 %fusion.41 = f32[1024,2048]{1,0:T(8,128)} fusion(bf16[1024,1024]{1,0:T(8,128)(2,1)S(1)} %get-tuple-element.100, bf16[2048,1024]{1,0:T(8,128)(2,1)S(1)} %copy-done.39), kind=kOutput, calls=%fused_computation.205 | convolution fusion | flops 4294967296 | bytes 14680064 | tf_op jit(solution)/shard_map/dot_general | solution.py:43
  357.1 11.2 %add_convert_fusion = bf16[1024,2048]{1,0:T(8,128)(2,1)} fusion(f32[1024,2048]{1,0:T(8,128)} %fusion.41, bf16[1024,1024]{1,0:T(8,128)(2,1)S(1)} %get-tuple-element.101, bf16[512,1024]{1,0:T(8,128)(2,1)S(1)} %copy-done.36, bf16[512,1024]{1,0:T(8,128)(2,1)S(1)} %copy-done.42, bf16[512,1024]{1,0:T(8,128)(2,1)S(1)} %copy-done.45, bf16[512,1024]{1,0:T(8,128)(2,1)S(1)} %place.10), kind=kOutput, calls=%fused_computation.5 | convolution fusion | flops 4315938816 | bytes 18874368 | tf_op jit(solution)/shard_map/dot_general | solution.py:43
  368.3 22.4 %reduce-scatter.7.cloned.1.call-done = bf16[128,2048]{1,0:T(8,128)(2,1)} async-done(((bf16[1024,2048]{1,0:T(8,128)(2,1)}), bf16[128,2048]{1,0:T(8,128)(2,1)}) %reduce-scatter.7.cloned.1.call-update) | async-done | bytes 524304 | tf_op jit(solution)/shard_map/reduce_scatter | solution.py:394
  391.0 7.4 %convolution_convert_fusion.4 = bf16[2048,1024]{1,0:T(8,128)(2,1)S(1)} fusion(bf16[1024,2048]{1,0:T(8,128)(2,1)} %all-gather.7.cloned.1.call-done, bf16[1024,1024]{1,0:T(8,128)(2,1)} %copy-done.68), kind=kOutput, calls=%fused_computation.18 | convolution fusion | flops 4297064448 | bytes 10485760 | tf_op jit(solution)/shard_map/dot_general | solution.py:39
  402.3 6.3 convolution_convert_fusion.3
  408.6 6.3 convolution_convert_fusion.2
  414.9 10.0 %collective-permute-done.34 = bf16[512,1024]{1,0:T(8,128)(2,1)S(1)} collective-permute-done((bf16[512,1024]{1,0:T(8,128)(2,1)S(1)}, bf16[512,1024]{1,0:T(8,128)(2,1)S(1)}, u32[]{:S(2)}, u32[]{:S(2)}) %collective-permute-start.34) | collective-permute-done | bytes 1048608 | tf_op jit(solution)/shard_map/ppermute | solution.py:332
  424.9 20.1 %collective-permute-done.36 = bf16[512,1024]{1,0:T(8,128)(2,1)S(1)} collective-permute-done((bf16[512,1024]{1,0:T(8,128)(2,1)S(1)}, bf16[512,1024]{1,0:T(8,128)(2,1)S(1)}, u32[]{:S(2)}, u32[]{:S(2)}) %collective-permute-start.36) | collective-permute-done | bytes 1048608 | tf_op jit(solution)/shard_map/ppermute | solution.py:332
  453.6 3.6 fusion.35
  460.9 3.0 collective-permute-start.42
  463.8 19.8 %collective-permute-done.37 = bf16[512,1024]{1,0:T(8,128)(2,1)} collective-permute-done((bf16[512,1024]{1,0:T(8,128)(2,1)}, bf16[512,1024]{1,0:T(8,128)(2,1)}, u32[]{:S(2)}, u32[]{:S(2)}) %collective-permute-start.37) | collective-permute-done | bytes 1048608 | tf_op jit(solution)/shard_map/ppermute | solution.py:332
  483.7 16.9 %collective-permute-done.39 = bf16[512,1024]{1,0:T(8,128)(2,1)} collective-permute-done((bf16[512,1024]{1,0:T(8,128)(2,1)}, bf16[512,1024]{1,0:T(8,128)(2,1)}, u32[]{:S(2)}, u32[]{:S(2)}) %collective-permute-start.39) | collective-permute-done | bytes 1048608 | tf_op jit(solution)/shard_map/ppermute | solution.py:332
  501.9 3.1 add_convert_fusion.3
  510.2 7.4 %collective-permute-start.41 = (bf16[128,1024]{1,0:T(8,128)(2,1)S(1)}, bf16[128,1024]{1,0:T(8,128)(2,1)S(1)}, u32[]{:S(2)}, u32[]{:S(2)}) collective-permute-start(bf16[128,1024]{1,0:T(8,128)(2,1)S(1)} %get-tuple-element.181), channel_id=1, source_target_pairs={{0,4},{2,6},{4,0},{6,2},{1,5},{3,7},{5,1},{7,3},{8,12},{10,14},{12... | collective-permute-start | bytes 786440 | tf_op jit(solution)/shard_map/ppermute | solution.py:329
  517.6 14.7 %collective-permute-done.41.refs_2_ = bf16[128,1024]{1,0:T(8,128)(2,1)S(1)} collective-permute-done((bf16[128,1024]{1,0:T(8,128)(2,1)S(1)}, bf16[128,1024]{1,0:T(8,128)(2,1)S(1)}, u32[]{:S(2)}, u32[]{:S(2)}) %collective-permute-start.41) | collective-permute-done | bytes 262176 | tf_op jit(solution)/shard_map/ppermute | solution.py:329
  536.2 3.7 convolution_convert_fusion.8.g_ref
  539.9 13.1 %attend_back.1 = bf16[1024,768]{1,0:T(8,128)(2,1)S(1)} custom-call(s32[8]{0:T(128)S(1)} %bitcast.96, bf16[1024,768]{1,0:T(8,128)(2,1)S(1)} %copy-done.1, bf16[1024,768]{1,0:T(8,128)(2,1)S(1)} %copy-done.1, bf16[1024,768]{1,0:T(8,128)(2,1)S(1)} %copy-done.1, bf16[1024,256]{1,0:T(8,128)(2,1)S(1)} %convolution_convert_fusion.8.g_ref, ...), custom_call_target="tpu_custom_call" | custom-call | flops 536870912 | bytes 4194304 | tf_op jit(solution)/shard_map/attend_back/pallas_call | solution.py:272
  555.4 4.0 add_convert_fusion.2
  564.0 5.0 convolution_convert_fusion.1
  573.2 3.5 convolution_convert_fusion.7
  576.8 3.8 convolution_convert_fusion.6
  593.6 23.7 %collective-permute-done.52.refs_2_ = bf16[128,1024]{1,0:T(8,128)(2,1)S(1)} collective-permute-done((bf16[128,1024]{1,0:T(8,128)(2,1)S(1)}, bf16[128,1024]{1,0:T(8,128)(2,1)S(1)}, u32[]{:S(2)}, u32[]{:S(2)}) %collective-permute-start.52) | collective-permute-done | bytes 262176 | tf_op jit(solution)/shard_map/ppermute | solution.py:329
  619.1 8.3 %collective-permute-done.54 = bf16[512,1024]{1,0:T(8,128)(2,1)S(1)} collective-permute-done((bf16[512,1024]{1,0:T(8,128)(2,1)}, bf16[512,1024]{1,0:T(8,128)(2,1)S(1)}, u32[]{:S(2)}, u32[]{:S(2)}) %collective-permute-start.54) | collective-permute-done | bytes 1048608 | tf_op jit(solution)/shard_map/ppermute | solution.py:332
  631.0 3.4 collective-permute-done.57
  639.0 3.2 collective-permute-start.61
  658.7 9.4 %collective-permute-done.63.refs_2_ = bf16[128,1024]{1,0:T(8,128)(2,1)S(1)} collective-permute-done((bf16[128,1024]{1,0:T(8,128)(2,1)}, bf16[128,1024]{1,0:T(8,128)(2,1)S(1)}, u32[]{:S(2)}, u32[]{:S(2)}) %collective-permute-start.63) | collective-permute-done | bytes 262176 | tf_op jit(solution)/shard_map/ppermute | solution.py:329
  (391 shorter events, 167.1 us)
Async XLA Ops:
  7.2 108.1 %all-gather.5.cloned.1.call-start = ((), (), s32[]{:S(2)}) async-start(), calls=%async_computation.4 | async-start | bytes 4718592 | tf_op jit(solution)/shard_map/all_gather | solution.py:391
  41.4 201.4 %reduce-scatter.5.cloned.1.call-start = ((), (), s32[]{:S(2)}) async-start(), calls=%async_computation.5 | async-start | bytes 4718592 | tf_op jit(solution)/shard_map/reduce_scatter | solution.py:394
  41.5 23.7 %collective-permute-start.12 = (bf16[512,1024]{1,0:T(8,128)(2,1)S(1)}, bf16[512,1024]{1,0:T(8,128)(2,1)S(1)}, u32[]{:S(2)}, u32[]{:S(2)}) collective-permute-start(bf16[512,1024]{1,0:T(8,128)(2,1)S(1)} %place.8.refs_0_), channel_id=1, source_target_pairs={{0,16},{8,24},{16,0},{24,8},{1,17},{9,25},{17,1},{25,9},{2,18},{10... | collective-permute-start | bytes 3145736 | tf_op jit(solution)/shard_map/ppermute | solution.py:332
  43.0 24.5 %collective-permute-start.11 = (bf16[512,1024]{1,0:T(8,128)(2,1)S(1)}, bf16[512,1024]{1,0:T(8,128)(2,1)S(1)}, u32[]{:S(2)}, u32[]{:S(2)}) collective-permute-start(bf16[512,1024]{1,0:T(8,128)(2,1)S(1)} %place.8.refs_0_), channel_id=1, source_target_pairs={{0,8},{8,0},{16,24},{24,16},{1,9},{9,1},{17,25},{25,17},{2,10},{10... | collective-permute-start | bytes 3145736 | tf_op jit(solution)/shard_map/ppermute | solution.py:332
  66.0 45.7 %collective-permute-start.14 = (bf16[256,1024]{1,0:T(8,128)(2,1)}, bf16[256,1024]{1,0:T(8,128)(2,1)}, u32[]{:S(2)}, u32[]{:S(2)}) collective-permute-start(bf16[256,1024]{1,0:T(8,128)(2,1)} %slice.201), channel_id=1, source_target_pairs={{0,8},{8,0},{16,24},{24,16},{1,9},{9,1},{17,25},{25,17},{2,10},{10... | collective-permute-start | bytes 1572872 | tf_op jit(solution)/shard_map/ppermute | solution.py:332
  69.3 42.4 %collective-permute-start.13 = (bf16[256,1024]{1,0:T(8,128)(2,1)}, bf16[256,1024]{1,0:T(8,128)(2,1)}, u32[]{:S(2)}, u32[]{:S(2)}) collective-permute-start(bf16[256,1024]{1,0:T(8,128)(2,1)} %slice.200), channel_id=1, source_target_pairs={{0,16},{8,24},{16,0},{24,8},{1,17},{9,25},{17,1},{25,9},{2,18},{10... | collective-permute-start | bytes 1572872 | tf_op jit(solution)/shard_map/ppermute | solution.py:332
  71.0 39.5 %collective-permute-start.9 = (bf16[128,1024]{1,0:T(8,128)(2,1)S(1)}, bf16[128,1024]{1,0:T(8,128)(2,1)S(1)}, u32[]{:S(2)}, u32[]{:S(2)}) collective-permute-start(bf16[128,1024]{1,0:T(8,128)(2,1)S(1)} %get-tuple-element.199), channel_id=1, source_target_pairs={{0,4},{2,6},{4,0},{6,2},{1,5},{3,7},{5,1},{7,3},{8,12},{10,14},{12... | collective-permute-start | bytes 786440 | tf_op jit(solution)/shard_map/ppermute | solution.py:329
  77.2 33.3 %collective-permute-start.8 = (bf16[128,1024]{1,0:T(8,128)(2,1)S(1)}, bf16[128,1024]{1,0:T(8,128)(2,1)S(1)}, u32[]{:S(2)}, u32[]{:S(2)}) collective-permute-start(bf16[128,1024]{1,0:T(8,128)(2,1)S(1)} %get-tuple-element.200), channel_id=1, source_target_pairs={{0,2},{2,4},{4,6},{6,0},{1,3},{3,5},{5,7},{7,1},{8,10},{10,12},{12... | collective-permute-start | bytes 786440 | tf_op jit(solution)/shard_map/ppermute | solution.py:329
  115.3 24.7 %collective-permute-start.19 = (bf16[512,1024]{1,0:T(8,128)(2,1)}, bf16[512,1024]{1,0:T(8,128)(2,1)S(1)}, u32[]{:S(2)}, u32[]{:S(2)}) collective-permute-start(bf16[512,1024]{1,0:T(8,128)(2,1)} %copy-done.9), channel_id=1, source_target_pairs={{0,16},{8,24},{16,0},{24,8},{1,17},{9,25},{17,1},{25,9},{2,18},{10... | collective-permute-start | bytes 3145736 | tf_op jit(solution)/shard_map/ppermute | solution.py:332
  116.8 25.1 %collective-permute-start.18 = (bf16[512,1024]{1,0:T(8,128)(2,1)}, bf16[512,1024]{1,0:T(8,128)(2,1)S(1)}, u32[]{:S(2)}, u32[]{:S(2)}) collective-permute-start(bf16[512,1024]{1,0:T(8,128)(2,1)} %copy-done.9), channel_id=1, source_target_pairs={{0,8},{8,0},{16,24},{24,16},{1,9},{9,1},{17,25},{25,17},{2,10},{10... | collective-permute-start | bytes 3145736 | tf_op jit(solution)/shard_map/ppermute | solution.py:332
  121.2 43.2 %collective-permute-start.17 = (bf16[128,1024]{1,0:T(8,128)(2,1)S(1)}, bf16[128,1024]{1,0:T(8,128)(2,1)S(1)}, u32[]{:S(2)}, u32[]{:S(2)}) collective-permute-start(bf16[128,1024]{1,0:T(8,128)(2,1)S(1)} %get-tuple-element.194), channel_id=1, source_target_pairs={{0,6},{2,0},{4,2},{6,4},{1,7},{3,1},{5,3},{7,5},{8,14},{10,8},{12,... | collective-permute-start | bytes 786440 | tf_op jit(solution)/shard_map/ppermute | solution.py:329
  121.3 43.1 %collective-permute-start.16 = (bf16[128,1024]{1,0:T(8,128)(2,1)S(1)}, bf16[128,1024]{1,0:T(8,128)(2,1)S(1)}, u32[]{:S(2)}, u32[]{:S(2)}) collective-permute-start(bf16[128,1024]{1,0:T(8,128)(2,1)S(1)} %get-tuple-element.195), channel_id=1, source_target_pairs={{0,4},{2,6},{4,0},{6,2},{1,5},{3,7},{5,1},{7,3},{8,12},{10,14},{12... | collective-permute-start | bytes 786440 | tf_op jit(solution)/shard_map/ppermute | solution.py:329
  121.6 42.9 %collective-permute-start.15 = (bf16[128,1024]{1,0:T(8,128)(2,1)S(1)}, bf16[128,1024]{1,0:T(8,128)(2,1)S(1)}, u32[]{:S(2)}, u32[]{:S(2)}) collective-permute-start(bf16[128,1024]{1,0:T(8,128)(2,1)S(1)} %get-tuple-element.196), channel_id=1, source_target_pairs={{0,2},{2,4},{4,6},{6,0},{1,3},{3,5},{5,7},{7,1},{8,10},{10,12},{12... | collective-permute-start | bytes 786440 | tf_op jit(solution)/shard_map/ppermute | solution.py:329
  140.1 26.7 %collective-permute-start.21 = (bf16[256,1024]{1,0:T(8,128)(2,1)S(1)}, bf16[256,1024]{1,0:T(8,128)(2,1)S(1)}, u32[]{:S(2)}, u32[]{:S(2)}) collective-permute-start(bf16[256,1024]{1,0:T(8,128)(2,1)S(1)} %slice.204), channel_id=1, source_target_pairs={{0,8},{8,0},{16,24},{24,16},{1,9},{9,1},{17,25},{25,17},{2,10},{10... | collective-permute-start | bytes 1572872 | tf_op jit(solution)/shard_map/ppermute | solution.py:332
  141.9 24.9 %collective-permute-start.20 = (bf16[256,1024]{1,0:T(8,128)(2,1)S(1)}, bf16[256,1024]{1,0:T(8,128)(2,1)S(1)}, u32[]{:S(2)}, u32[]{:S(2)}) collective-permute-start(bf16[256,1024]{1,0:T(8,128)(2,1)S(1)} %slice.203), channel_id=1, source_target_pairs={{0,16},{8,24},{16,0},{24,8},{1,17},{9,25},{17,1},{25,9},{2,18},{10... | collective-permute-start | bytes 1572872 | tf_op jit(solution)/shard_map/ppermute | solution.py:332
  172.5 119.5 %all-gather.9.cloned.1.call-start = ((), (), s32[]{:S(2)}) async-start(), calls=%async_computation.7 | async-start | bytes 4718592 | tf_op jit(solution)/shard_map/all_gather | solution.py:391
  172.5 23.2 %collective-permute-start.26 = (bf16[512,1024]{1,0:T(8,128)(2,1)S(1)}, bf16[512,1024]{1,0:T(8,128)(2,1)S(1)}, u32[]{:S(2)}, u32[]{:S(2)}) collective-permute-start(bf16[512,1024]{1,0:T(8,128)(2,1)S(1)} %place.10), channel_id=1, source_target_pairs={{0,16},{8,24},{16,0},{24,8},{1,17},{9,25},{17,1},{25,9},{2,18},{10... | collective-permute-start | bytes 3145736 | tf_op jit(solution)/shard_map/ppermute | solution.py:332
  173.3 24.2 %collective-permute-start.25 = (bf16[512,1024]{1,0:T(8,128)(2,1)S(1)}, bf16[512,1024]{1,0:T(8,128)(2,1)S(1)}, u32[]{:S(2)}, u32[]{:S(2)}) collective-permute-start(bf16[512,1024]{1,0:T(8,128)(2,1)S(1)} %place.10), channel_id=1, source_target_pairs={{0,8},{8,0},{16,24},{24,16},{1,9},{9,1},{17,25},{25,17},{2,10},{10... | collective-permute-start | bytes 3145736 | tf_op jit(solution)/shard_map/ppermute | solution.py:332
  196.7 43.9 %collective-permute-start.28 = (bf16[256,1024]{1,0:T(8,128)(2,1)}, bf16[256,1024]{1,0:T(8,128)(2,1)}, u32[]{:S(2)}, u32[]{:S(2)}) collective-permute-start(bf16[256,1024]{1,0:T(8,128)(2,1)} %slice.207), channel_id=1, source_target_pairs={{0,8},{8,0},{16,24},{24,16},{1,9},{9,1},{17,25},{25,17},{2,10},{10... | collective-permute-start | bytes 1572872 | tf_op jit(solution)/shard_map/ppermute | solution.py:332
  198.8 41.8 %collective-permute-start.27 = (bf16[256,1024]{1,0:T(8,128)(2,1)}, bf16[256,1024]{1,0:T(8,128)(2,1)}, u32[]{:S(2)}, u32[]{:S(2)}) collective-permute-start(bf16[256,1024]{1,0:T(8,128)(2,1)} %slice.206), channel_id=1, source_target_pairs={{0,16},{8,24},{16,0},{24,8},{1,17},{9,25},{17,1},{25,9},{2,18},{10... | collective-permute-start | bytes 1572872 | tf_op jit(solution)/shard_map/ppermute | solution.py:332
  203.2 36.2 %collective-permute-start.23 = (bf16[128,1024]{1,0:T(8,128)(2,1)S(1)}, bf16[128,1024]{1,0:T(8,128)(2,1)S(1)}, u32[]{:S(2)}, u32[]{:S(2)}) collective-permute-start(bf16[128,1024]{1,0:T(8,128)(2,1)S(1)} %get-tuple-element.191), channel_id=1, source_target_pairs={{0,4},{2,6},{4,0},{6,2},{1,5},{3,7},{5,1},{7,3},{8,12},{10,14},{12... | collective-permute-start | bytes 786440 | tf_op jit(solution)/shard_map/ppermute | solution.py:329
  203.8 35.6 %collective-permute-start.22 = (bf16[128,1024]{1,0:T(8,128)(2,1)S(1)}, bf16[128,1024]{1,0:T(8,128)(2,1)S(1)}, u32[]{:S(2)}, u32[]{:S(2)}) collective-permute-start(bf16[128,1024]{1,0:T(8,128)(2,1)S(1)} %get-tuple-element.192), channel_id=1, source_target_pairs={{0,2},{2,4},{4,6},{6,0},{1,3},{3,5},{5,7},{7,1},{8,10},{10,12},{12... | collective-permute-start | bytes 786440 | tf_op jit(solution)/shard_map/ppermute | solution.py:329
  246.2 93.7 %all-gather.7.cloned.1.call-start = ((), (), s32[]{:S(2)}) async-start(), calls=%async_computation.6 | async-start | bytes 4718592 | tf_op jit(solution)/shard_map/all_gather | solution.py:391
  249.3 141.5 %reduce-scatter.7.cloned.1.call-start = ((), (), s32[]{:S(2)}) async-start(), calls=%async_computation.8 | async-start | bytes 4718592 | tf_op jit(solution)/shard_map/reduce_scatter | solution.py:394
  249.6 23.4 %collective-permute-start.30 = (bf16[512,1024]{1,0:T(8,128)(2,1)}, bf16[512,1024]{1,0:T(8,128)(2,1)S(1)}, u32[]{:S(2)}, u32[]{:S(2)}) collective-permute-start(bf16[512,1024]{1,0:T(8,128)(2,1)} %copy-done.11), channel_id=1, source_target_pairs={{0,16},{8,24},{16,0},{24,8},{1,17},{9,25},{17,1},{25,9},{2,18},{10... | collective-permute-start | bytes 3145736 | tf_op jit(solution)/shard_map/ppermute | solution.py:332
  251.2 24.1 %collective-permute-start.29 = (bf16[512,1024]{1,0:T(8,128)(2,1)}, bf16[512,1024]{1,0:T(8,128)(2,1)S(1)}, u32[]{:S(2)}, u32[]{:S(2)}) collective-permute-start(bf16[512,1024]{1,0:T(8,128)(2,1)} %copy-done.11), channel_id=1, source_target_pairs={{0,8},{8,0},{16,24},{24,16},{1,9},{9,1},{17,25},{25,17},{2,10},{10... | collective-permute-start | bytes 3145736 | tf_op jit(solution)/shard_map/ppermute | solution.py:332
  316.6 131.7 %reduce-scatter.9.cloned.1.call-start = ((), (), s32[]{:S(2)}) async-start(), calls=%async_computation.9 | async-start | bytes 4718592 | tf_op jit(solution)/shard_map/reduce_scatter | solution.py:394
  390.8 143.6 %all-gather.11.cloned.1.call-start = ((), (), s32[]{:S(2)}) async-start(), calls=%async_computation.10 | async-start | bytes 4718592 | tf_op jit(solution)/shard_map/all_gather | solution.py:391
  398.8 26.2 %collective-permute-start.34 = (bf16[512,1024]{1,0:T(8,128)(2,1)S(1)}, bf16[512,1024]{1,0:T(8,128)(2,1)S(1)}, u32[]{:S(2)}, u32[]{:S(2)}) collective-permute-start(bf16[512,1024]{1,0:T(8,128)(2,1)S(1)} %get-tuple-element.149), channel_id=1, source_target_pairs={{0,8},{8,0},{16,24},{24,16},{1,9},{9,1},{17,25},{25,17},{2,10},{10... | collective-permute-start | bytes 3145736 | tf_op jit(solution)/shard_map/ppermute | solution.py:332
  400.3 44.8 %collective-permute-start.36 = (bf16[512,1024]{1,0:T(8,128)(2,1)S(1)}, bf16[512,1024]{1,0:T(8,128)(2,1)S(1)}, u32[]{:S(2)}, u32[]{:S(2)}) collective-permute-start(bf16[512,1024]{1,0:T(8,128)(2,1)S(1)} %get-tuple-element.150), channel_id=1, source_target_pairs={{0,24},{8,16},{16,8},{24,0},{1,25},{9,17},{17,9},{25,1},{2,26},{10... | collective-permute-start | bytes 3145736 | tf_op jit(solution)/shard_map/ppermute | solution.py:332
  401.8 44.7 %collective-permute-start.35 = (bf16[512,1024]{1,0:T(8,128)(2,1)S(1)}, bf16[512,1024]{1,0:T(8,128)(2,1)S(1)}, u32[]{:S(2)}, u32[]{:S(2)}) collective-permute-start(bf16[512,1024]{1,0:T(8,128)(2,1)S(1)} %get-tuple-element.151), channel_id=1, source_target_pairs={{0,16},{8,24},{16,0},{24,8},{1,17},{9,25},{17,1},{25,9},{2,18},{10... | collective-permute-start | bytes 3145736 | tf_op jit(solution)/shard_map/ppermute | solution.py:332
  453.4 196.8 %reduce-scatter.11.cloned.1.call-start = ((), (), s32[]{:S(2)}) async-start(), calls=%async_computation.11 | async-start | bytes 4718592 | tf_op jit(solution)/shard_map/reduce_scatter | solution.py:394
  457.3 26.4 %collective-permute-start.37 = (bf16[512,1024]{1,0:T(8,128)(2,1)}, bf16[512,1024]{1,0:T(8,128)(2,1)}, u32[]{:S(2)}, u32[]{:S(2)}) collective-permute-start(bf16[512,1024]{1,0:T(8,128)(2,1)} %get-tuple-element.146), channel_id=1, source_target_pairs={{0,8},{8,0},{16,24},{24,16},{1,9},{9,1},{17,25},{25,17},{2,10},{10... | collective-permute-start | bytes 3145736 | tf_op jit(solution)/shard_map/ppermute | solution.py:332
  458.7 41.8 %collective-permute-start.39 = (bf16[512,1024]{1,0:T(8,128)(2,1)}, bf16[512,1024]{1,0:T(8,128)(2,1)}, u32[]{:S(2)}, u32[]{:S(2)}) collective-permute-start(bf16[512,1024]{1,0:T(8,128)(2,1)} %get-tuple-element.147), channel_id=1, source_target_pairs={{0,24},{8,16},{16,8},{24,0},{1,25},{9,17},{17,9},{25,1},{2,26},{10... | collective-permute-start | bytes 3145736 | tf_op jit(solution)/shard_map/ppermute | solution.py:332
  459.3 42.6 %collective-permute-start.38 = (bf16[512,1024]{1,0:T(8,128)(2,1)}, bf16[512,1024]{1,0:T(8,128)(2,1)}, u32[]{:S(2)}, u32[]{:S(2)}) collective-permute-start(bf16[512,1024]{1,0:T(8,128)(2,1)} %get-tuple-element.148), channel_id=1, source_target_pairs={{0,16},{8,24},{16,0},{24,8},{1,17},{9,25},{17,1},{25,9},{2,18},{10... | collective-permute-start | bytes 3145736 | tf_op jit(solution)/shard_map/ppermute | solution.py:332
  460.9 56.7 %collective-permute-start.42 = (bf16[128,1024]{1,0:T(8,128)(2,1)S(1)}, bf16[128,1024]{1,0:T(8,128)(2,1)S(1)}, u32[]{:S(2)}, u32[]{:S(2)}) collective-permute-start(bf16[128,1024]{1,0:T(8,128)(2,1)S(1)} %get-tuple-element.180), channel_id=1, source_target_pairs={{0,6},{2,0},{4,2},{6,4},{1,7},{3,1},{5,3},{7,5},{8,14},{10,8},{12,... | collective-permute-start | bytes 786440 | tf_op jit(solution)/shard_map/ppermute | solution.py:329
  506.7 46.3 %collective-permute-start.43 = (bf16[512,1024]{1,0:T(8,128)(2,1)}, bf16[512,1024]{1,0:T(8,128)(2,1)}, u32[]{:S(2)}, u32[]{:S(2)}) collective-permute-start(bf16[512,1024]{1,0:T(8,128)(2,1)} %get-tuple-element.143), channel_id=1, source_target_pairs={{0,8},{8,0},{16,24},{24,16},{1,9},{9,1},{17,25},{25,17},{2,10},{10... | collective-permute-start | bytes 3145736 | tf_op jit(solution)/shard_map/ppermute | solution.py:332
  508.2 47.2 %collective-permute-start.45 = (bf16[512,1024]{1,0:T(8,128)(2,1)}, bf16[512,1024]{1,0:T(8,128)(2,1)}, u32[]{:S(2)}, u32[]{:S(2)}) collective-permute-start(bf16[512,1024]{1,0:T(8,128)(2,1)} %get-tuple-element.144), channel_id=1, source_target_pairs={{0,24},{8,16},{16,8},{24,0},{1,25},{9,17},{17,9},{25,1},{2,26},{10... | collective-permute-start | bytes 3145736 | tf_op jit(solution)/shard_map/ppermute | solution.py:332
  509.7 45.8 %collective-permute-start.44 = (bf16[512,1024]{1,0:T(8,128)(2,1)}, bf16[512,1024]{1,0:T(8,128)(2,1)}, u32[]{:S(2)}, u32[]{:S(2)}) collective-permute-start(bf16[512,1024]{1,0:T(8,128)(2,1)} %get-tuple-element.145), channel_id=1, source_target_pairs={{0,16},{8,24},{16,0},{24,8},{1,17},{9,25},{17,1},{25,9},{2,18},{10... | collective-permute-start | bytes 3145736 | tf_op jit(solution)/shard_map/ppermute | solution.py:332
  510.2 22.1 %collective-permute-start.41 = (bf16[128,1024]{1,0:T(8,128)(2,1)S(1)}, bf16[128,1024]{1,0:T(8,128)(2,1)S(1)}, u32[]{:S(2)}, u32[]{:S(2)}) collective-permute-start(bf16[128,1024]{1,0:T(8,128)(2,1)S(1)} %get-tuple-element.181), channel_id=1, source_target_pairs={{0,4},{2,6},{4,0},{6,2},{1,5},{3,7},{5,1},{7,3},{8,12},{10,14},{12... | collective-permute-start | bytes 786440 | tf_op jit(solution)/shard_map/ppermute | solution.py:329
  534.5 25.0 %collective-permute-start.48 = (bf16[128,1024]{1,0:T(8,128)(2,1)S(1)}, bf16[128,1024]{1,0:T(8,128)(2,1)S(1)}, u32[]{:S(2)}, u32[]{:S(2)}) collective-permute-start(bf16[128,1024]{1,0:T(8,128)(2,1)S(1)} %get-tuple-element.176), channel_id=1, source_target_pairs={{0,6},{2,0},{4,2},{6,4},{1,7},{3,1},{5,3},{7,5},{8,14},{10,8},{12,... | collective-permute-start | bytes 786440 | tf_op jit(solution)/shard_map/ppermute | solution.py:329
  534.5 25.0 %collective-permute-start.47 = (bf16[128,1024]{1,0:T(8,128)(2,1)S(1)}, bf16[128,1024]{1,0:T(8,128)(2,1)S(1)}, u32[]{:S(2)}, u32[]{:S(2)}) collective-permute-start(bf16[128,1024]{1,0:T(8,128)(2,1)S(1)} %get-tuple-element.177), channel_id=1, source_target_pairs={{0,4},{2,6},{4,0},{6,2},{1,5},{3,7},{5,1},{7,3},{8,12},{10,14},{12... | collective-permute-start | bytes 786440 | tf_op jit(solution)/shard_map/ppermute | solution.py:329
  581.9 37.2 %collective-permute-start.50 = (bf16[512,1024]{1,0:T(8,128)(2,1)}, bf16[512,1024]{1,0:T(8,128)(2,1)S(1)}, u32[]{:S(2)}, u32[]{:S(2)}) collective-permute-start(bf16[512,1024]{1,0:T(8,128)(2,1)} %pad_maximum_fusion.8), channel_id=1, source_target_pairs={{0,8},{8,0},{16,24},{24,16},{1,9},{9,1},{17,25},{25,17},{2,10},{10... | collective-permute-start | bytes 3145736 | tf_op jit(solution)/shard_map/ppermute | solution.py:332
  584.5 42.9 %collective-permute-start.54 = (bf16[512,1024]{1,0:T(8,128)(2,1)}, bf16[512,1024]{1,0:T(8,128)(2,1)S(1)}, u32[]{:S(2)}, u32[]{:S(2)}) collective-permute-start(bf16[512,1024]{1,0:T(8,128)(2,1)} %pad_maximum_fusion.9), channel_id=1, source_target_pairs={{0,16},{8,24},{16,0},{24,8},{1,17},{9,25},{17,1},{25,9},{2,18},{10... | collective-permute-start | bytes 3145736 | tf_op jit(solution)/shard_map/ppermute | solution.py:332
  585.9 41.5 %collective-permute-start.55 = (bf16[512,1024]{1,0:T(8,128)(2,1)}, bf16[512,1024]{1,0:T(8,128)(2,1)S(1)}, u32[]{:S(2)}, u32[]{:S(2)}) collective-permute-start(bf16[512,1024]{1,0:T(8,128)(2,1)} %pad_maximum_fusion.10), channel_id=1, source_target_pairs={{0,24},{8,16},{16,8},{24,0},{1,25},{9,17},{17,9},{25,1},{2,26},{10... | collective-permute-start | bytes 3145736 | tf_op jit(solution)/shard_map/ppermute | solution.py:332
  588.6 28.7 %collective-permute-start.52 = (bf16[128,1024]{1,0:T(8,128)(2,1)S(1)}, bf16[128,1024]{1,0:T(8,128)(2,1)S(1)}, u32[]{:S(2)}, u32[]{:S(2)}) collective-permute-start(bf16[128,1024]{1,0:T(8,128)(2,1)S(1)} %get-tuple-element.167), channel_id=1, source_target_pairs={{0,4},{2,6},{4,0},{6,2},{1,5},{3,7},{5,1},{7,3},{8,12},{10,14},{12... | collective-permute-start | bytes 786440 | tf_op jit(solution)/shard_map/ppermute | solution.py:329
  590.7 26.6 %collective-permute-start.51 = (bf16[128,1024]{1,0:T(8,128)(2,1)S(1)}, bf16[128,1024]{1,0:T(8,128)(2,1)S(1)}, u32[]{:S(2)}, u32[]{:S(2)}) collective-permute-start(bf16[128,1024]{1,0:T(8,128)(2,1)S(1)} %get-tuple-element.168), channel_id=1, source_target_pairs={{0,2},{2,4},{4,6},{6,0},{1,3},{3,5},{5,7},{7,1},{8,10},{10,12},{12... | collective-permute-start | bytes 786440 | tf_op jit(solution)/shard_map/ppermute | solution.py:329
  645.5 22.6 %collective-permute-start.63 = (bf16[128,1024]{1,0:T(8,128)(2,1)}, bf16[128,1024]{1,0:T(8,128)(2,1)S(1)}, u32[]{:S(2)}, u32[]{:S(2)}) collective-permute-start(bf16[128,1024]{1,0:T(8,128)(2,1)} %get-tuple-element.159), channel_id=1, source_target_pairs={{0,4},{2,6},{4,0},{6,2},{1,5},{3,7},{5,1},{7,3},{8,12},{10,14},{12... | collective-permute-start | bytes 786440 | tf_op jit(solution)/shard_map/ppermute | solution.py:329
  (94 other events, 1811.1 us)
Sparse Core Ops, SparseCore 0:
  41.5 60.0 all-gather.4
  172.6 59.5 reduce-scatter.4
  246.3 45.6 all-gather.8
  294.0 45.8 all-gather.6
  342.0 48.6 reduce-scatter.6
  392.9 48.1 reduce-scatter.8
  453.5 51.4 all-gather.10
  569.2 62.5 reduce-scatter.10

commit v4 on v3

--- a/solution.py
+++ b/solution.py
@@ -415,8 +415,7 @@
     attn_part = after(swap_columns(w_query, w_key, w_value, w_out.T), gains)
     attn_pieces = plane_pieces(attn_part)
     attn_full = jnp.concatenate(attn_pieces, 0)
-    gate_part = swap_columns(after(w_gate, attn_part))
-    inputs_low = after(gather_tokens(after(inputs_own, attn_part)), gate_part, attn_full)
+    inputs_low = after(gather_tokens(after(inputs_own, attn_part)), attn_full)
     qkv_full = attn_full[:, : 3 * heads_width]
     out_full = attn_full[:, 3 * heads_width :]
 
@@ -424,10 +423,12 @@
     normed_one, qkv = project(
         inputs_low, gain_one[None], cosine, sine, attn_pieces, heads_width, row_count
     )
+    gate_part = swap_columns(after(w_gate, inputs_low), late=(qkv,))
     up_part = swap_columns(after(w_up, inputs_low), late=(qkv,))
+    qkv = after(qkv, gate_part)
     attn_low, log_total, peaks = attend(order_row, qkv)
     down_part = swap_columns(after(w_down.T, up_part))
-    gate_full = gather_plane(after(gate_part, attn_full, inputs_low), late=(attn_low,))
+    gate_full = gather_plane(gate_part, late=(attn_low,))
     up_full = gather_plane(after(up_part, gate_full))
     down_full = gather_plane(after(down_part, up_full))
     attn_low = after(attn_low, up_part, gate_full)

time: 688 us -> 681 us (0.990)
  waiting for transfers between devices: 351 us -> 342 us
    ppermute x30, waiting for transfers between devices: 125 us -> 104 us  [along(): lax.ppermute(tensor, 'ctx', [(i, (i + shift) % n_ctx) for i in range(n_ct...]
    all_gather x4, waiting for transfers between devices: 28.1 us -> 35.1 us  [gather_tokens(): return lax.all_gather(own, ('ctx', 'tp'), axis=0, tiled=True)]
    unnamed x150 -> x140, local copies, waits for them, and re-layouts: 14.5 us -> 15.7 us
  transfers between devices with their start and end apart: 73 -> 73, of which waited for: 30 -> 33; matrix products, arithmetic and copies ran while one was open for 22% -> 22% of each run, Pallas kernels for 6% -> 6%
where the time goes in v4:
time: 681 us; the launch traced here: 674 us
  waiting for transfers between devices  342 us (50%)
  matrix products  94.3 us (14%)
  starting transfers between devices  94.2 us (14%)
  other arithmetic  47.8 us (7%)
  local copies, waits for them, and re-layouts  40.4 us (6%)
  Pallas kernels  39.6 us (6%)
  between operations  15.5 us (2%)
    ppermute x32, waiting for transfers between devices, across(): return lax.ppermute(tensor, 'fsdp', [(i, i ^ mask) for i in range(n_fsdp)])  181 us
    ppermute x30, waiting for transfers between devices, along(): lax.ppermute(tensor, 'ctx', [(i, (i + shift) % n_ctx) for i in range(n_ct...  104 us
    ppermute x30, starting transfers between devices, along(): lax.ppermute(tensor, 'ctx', [(i, (i + shift) % n_ctx) for i in range(n_ct...  52.1 us
    ppermute x32, starting transfers between devices, across(): return lax.ppermute(tensor, 'fsdp', [(i, i ^ mask) for i in range(n_fsdp)])  39.9 us
    dot_general x5, matrix products, dot_rt(): lax.dot_general(left, right, (((1,), (1,)), ((), ())), preferred_element_...  37.5 us
    all_gather x4, waiting for transfers between devices, gather_tokens(): return lax.all_gather(own, ('ctx', 'tp'), axis=0, tiled=True)  35.1 us
    dot_general x4, matrix products, dot(): return jnp.dot(left, right, preferred_element_type=f32)  29.2 us
    dot_general x5, matrix products, dot_lt(): lax.dot_general(left, right, (((0,), (0,)), ((), ())), preferred_element_...  27.6 us
  transfers between devices with their start and end apart: 73, of which 33 were waited for; matrix products, arithmetic and copies ran while one was open for 22% of the time, Pallas kernels for 6%

profile of v4, /device:TPU:0, one launch (start us, length us, event | category | flops | bytes accessed | tf_op | source)
XLA Modules:
  0.0 673.6 jit_solution(2486183438803920692)
XLA Ops:
  8.0 4.1 collective-permute-start.4
  20.5 3.3 collective-permute-start.2
  31.2 6.7 collective-permute-done.1.refs_2_
  42.9 20.4 %collective-permute-done.9.refs_2_ = bf16[512,1024]{1,0:T(8,128)(2,1)S(1)} collective-permute-done((bf16[512,1024]{1,0:T(8,128)(2,1)S(1)}, bf16[512,1024]{1,0:T(8,128)(2,1)S(1)}, u32[]{:S(2)}, u32[]{:S(2)}) %collective-permute-start.9) | collective-permute-done | bytes 1048608 | tf_op jit(solution)/shard_map/ppermute | solution.py:332
  72.8 3.1 collective-permute-done.11
  75.9 2.9 collective-permute-done.10
  82.4 6.8 %all-gather.5.cloned.1.call-done.x_ref = bf16[1024,2048]{1,0:T(8,128)(2,1)} async-done(((bf16[128,2048]{1,0:T(8,128)(2,1)}), bf16[1024,2048]{1,0:T(8,128)(2,1)}) %all-gather.5.cloned.1.call-update) | async-done | bytes 4194320 | tf_op jit(solution)/shard_map/all_gather | solution.py:391
  97.5 8.3 %project.1 = (bf16[1024,2048]{1,0:T(8,128)(2,1)}, bf16[1024,768]{1,0:T(8,128)(2,1)}) custom-call(bf16[1024,2048]{1,0:T(8,128)(2,1)} %all-gather.5.cloned.1.call-done.x_ref, f32[1,2048]{1,0:T(1,128)S(1)} %get-tuple-element.237.gain_ref, f32[1024,128]{1,0:T(8,128)S(1)} %copy-done.4, f32[1024,128]{1,0:T(8,128)S(1)} %copy-done.6, ...), custom_call_target="tpu_custom_call" | custom-call | flops 536870912 | bytes 12582912 | tf_op jit(solution)/shard_map/project/pallas_call | solution.py:121
  105.8 9.4 %collective-permute-done.13.refs_2_ = bf16[128,1024]{1,0:T(8,128)(2,1)S(1)} collective-permute-done((bf16[128,1024]{1,0:T(8,128)(2,1)S(1)}, bf16[128,1024]{1,0:T(8,128)(2,1)S(1)}, u32[]{:S(2)}, u32[]{:S(2)}) %collective-permute-start.13) | collective-permute-done | bytes 262176 | tf_op jit(solution)/shard_map/ppermute | solution.py:329
  123.5 15.3 %collective-permute-done.19 = bf16[512,1024]{1,0:T(8,128)(2,1)S(1)} collective-permute-done((bf16[512,1024]{1,0:T(8,128)(2,1)S(1)}, bf16[512,1024]{1,0:T(8,128)(2,1)S(1)}, u32[]{:S(2)}, u32[]{:S(2)}) %collective-permute-start.19) | collective-permute-done | bytes 1048608 | tf_op jit(solution)/shard_map/ppermute | solution.py:332
  144.0 9.7 %attend.1 = (bf16[1024,256]{1,0:T(8,128)(2,1)S(1)}, f32[2,1024,128]{2,1,0:T(8,128)S(1)}, f32[2,8,128]{2,1,0:T(8,128)S(1)}) custom-call(s32[8]{0:T(128)S(1)} %bitcast.95, bf16[1024,768]{1,0:T(8,128)(2,1)S(1)} %copy-done, bf16[1024,768]{1,0:T(8,128)(2,1)S(1)} %copy-done, bf16[1024,768]{1,0:T(8,128)(2,1)S(1)} %copy-done), custom_call_target="tpu_custom_call" | custom-call | flops 536870912 | bytes 2097152 | tf_op jit(solution)/shard_map/attend/pallas_call | solution.py:194
  157.0 4.6 convolution_convert_fusion
  162.8 23.0 %collective-permute-done.26 = bf16[512,1024]{1,0:T(8,128)(2,1)S(1)} collective-permute-done((bf16[512,1024]{1,0:T(8,128)(2,1)}, bf16[512,1024]{1,0:T(8,128)(2,1)S(1)}, u32[]{:S(2)}, u32[]{:S(2)}) %collective-permute-start.26) | collective-permute-done | bytes 1048608 | tf_op jit(solution)/shard_map/ppermute | solution.py:332
  199.1 9.9 %collective-permute-done.24.refs_3_ = bf16[128,1024]{1,0:T(8,128)(2,1)S(1)} collective-permute-done((bf16[128,1024]{1,0:T(8,128)(2,1)S(1)}, bf16[128,1024]{1,0:T(8,128)(2,1)S(1)}, u32[]{:S(2)}, u32[]{:S(2)}) %collective-permute-start.24) | collective-permute-done | bytes 262176 | tf_op jit(solution)/shard_map/ppermute | solution.py:329
  209.0 22.8 %collective-permute-done.23.refs_2_ = bf16[128,1024]{1,0:T(8,128)(2,1)S(1)} collective-permute-done((bf16[128,1024]{1,0:T(8,128)(2,1)S(1)}, bf16[128,1024]{1,0:T(8,128)(2,1)S(1)}, u32[]{:S(2)}, u32[]{:S(2)}) %collective-permute-start.23) | collective-permute-done | bytes 262176 | tf_op jit(solution)/shard_map/ppermute | solution.py:329
  244.9 20.2 %collective-permute-done.30 = bf16[512,1024]{1,0:T(8,128)(2,1)S(1)} collective-permute-done((bf16[512,1024]{1,0:T(8,128)(2,1)}, bf16[512,1024]{1,0:T(8,128)(2,1)S(1)}, u32[]{:S(2)}, u32[]{:S(2)}) %collective-permute-start.30) | collective-permute-done | bytes 1048608 | tf_op jit(solution)/shard_map/ppermute | solution.py:332
  268.1 9.1 %collective-permute-done.32 = bf16[256,1024]{1,0:T(8,128)(2,1)S(1)} collective-permute-done((bf16[256,1024]{1,0:T(8,128)(2,1)S(1)}, bf16[256,1024]{1,0:T(8,128)(2,1)S(1)}, u32[]{:S(2)}, u32[]{:S(2)}) %collective-permute-start.32) | collective-permute-done | bytes 524320 | tf_op jit(solution)/shard_map/ppermute | solution.py:332
  278.3 5.9 all-gather.9.cloned.1.call-done
  284.2 7.7 %fusion.40 = f32[1024,1024]{1,0:T(8,128)S(1)} fusion(bf16[1024,2048]{1,0:T(8,128)(2,1)} %all-gather.9.cloned.1.call-done, bf16[2048,1024]{1,0:T(8,128)(2,1)} %copy-done.35), kind=kOutput, calls=%fused_computation.204 | convolution fusion | flops 4294967296 | bytes 12582912 | tf_op jit(solution)/shard_map/dot_general | solution.py:35
  292.0 6.6 multiply_convert_fusion.2
  299.9 9.1 %convolution_convert_fusion.5 = bf16[1024,2048]{1,0:T(8,128)(2,1)} fusion(bf16[1024,1024]{1,0:T(8,128)(2,1)S(1)} %get-tuple-element.107, bf16[512,1024]{1,0:T(8,128)(2,1)S(1)} %copy-done.33, bf16[512,1024]{1,0:T(8,128)(2,1)S(1)} %copy-done.44, bf16[512,1024]{1,0:T(8,128)(2,1)S(1)} %copy-done.46, bf16[512,1024]{1,0:T(8,128)(2,1)S(1)} %copy-done.14), kind=kOutput, calls=%fused_computation.19 | convolution fusion | flops 4313841664 | bytes 10485760 | tf_op jit(solution)/shard_map/dot_general | solution.py:43
  309.6 22.5 %all-gather.7.cloned.1.call-done = bf16[1024,2048]{1,0:T(8,128)(2,1)} async-done(((bf16[128,2048]{1,0:T(8,128)(2,1)}), bf16[1024,2048]{1,0:T(8,128)(2,1)}) %all-gather.7.cloned.1.call-update) | async-done | bytes 4194320 | tf_op jit(solution)/shard_map/all_gather | solution.py:391
  332.1 11.2 %multiply_convert_fusion = (bf16[1024,1024]{1,0:T(8,128)(2,1)}, bf16[1024,1024]{1,0:T(8,128)(2,1)S(1)}) fusion(f32[1024,1024]{1,0:T(8,128)} %copy-done.59, f32[1024,1024]{1,0:T(8,128)} %get-tuple-element.252, bf16[1024,2048]{1,0:T(8,128)(2,1)} %all-gather.7.cloned.1.call-done, bf16[512,1024]{1,0:T(8,128)(2,1)} %pad_maximum_fusion.6, ...), kind=kOutput, calls=%fused_computation.9 | convolution fusion | flops 4325376000 | bytes 20971520 | tf_op jit(solution)/shard_map/dot_general | solution.py:35
  343.4 6.8 %fusion.41 = f32[1024,2048]{1,0:T(8,128)} fusion(bf16[1024,1024]{1,0:T(8,128)(2,1)S(1)} %get-tuple-element.108, bf16[2048,1024]{1,0:T(8,128)(2,1)S(1)} %copy-done.36), kind=kOutput, calls=%fused_computation.205 | convolution fusion | flops 4294967296 | bytes 14680064 | tf_op jit(solution)/shard_map/dot_general | solution.py:43
  350.2 12.0 %add_convert_fusion = bf16[1024,2048]{1,0:T(8,128)(2,1)} fusion(f32[1024,2048]{1,0:T(8,128)} %fusion.41, bf16[1024,1024]{1,0:T(8,128)(2,1)} %get-tuple-element.109, bf16[512,1024]{1,0:T(8,128)(2,1)S(1)} %copy-done.32, bf16[512,1024]{1,0:T(8,128)(2,1)S(1)} %copy-done.39, bf16[512,1024]{1,0:T(8,128)(2,1)S(1)} %copy-done.42, bf16[512,1024]{1,0:T(8,128)(2,1)S(1)} %copy-done.12), kind=kOutput, calls=%fused_computation.5 | convolution fusion | flops 4315938816 | bytes 18874368 | tf_op jit(solution)/shard_map/dot_general | solution.py:43
  362.1 20.9 %reduce-scatter.7.cloned.1.call-done = bf16[128,2048]{1,0:T(8,128)(2,1)} async-done(((bf16[1024,2048]{1,0:T(8,128)(2,1)}), bf16[128,2048]{1,0:T(8,128)(2,1)}) %reduce-scatter.7.cloned.1.call-update) | async-done | bytes 524304 | tf_op jit(solution)/shard_map/reduce_scatter | solution.py:394
  383.3 7.4 %convolution_convert_fusion.4 = bf16[2048,1024]{1,0:T(8,128)(2,1)S(1)} fusion(bf16[1024,2048]{1,0:T(8,128)(2,1)} %all-gather.7.cloned.1.call-done, bf16[1024,1024]{1,0:T(8,128)(2,1)} %copy-done.63), kind=kOutput, calls=%fused_computation.18 | convolution fusion | flops 4297064448 | bytes 10485760 | tf_op jit(solution)/shard_map/dot_general | solution.py:39
  394.6 6.3 convolution_convert_fusion.3
  400.9 6.3 convolution_convert_fusion.2
  407.2 10.0 %collective-permute-done.34 = bf16[512,1024]{1,0:T(8,128)(2,1)S(1)} collective-permute-done((bf16[512,1024]{1,0:T(8,128)(2,1)S(1)}, bf16[512,1024]{1,0:T(8,128)(2,1)S(1)}, u32[]{:S(2)}, u32[]{:S(2)}) %collective-permute-start.34) | collective-permute-done | bytes 1048608 | tf_op jit(solution)/shard_map/ppermute | solution.py:332
  417.2 20.1 %collective-permute-done.36 = bf16[512,1024]{1,0:T(8,128)(2,1)S(1)} collective-permute-done((bf16[512,1024]{1,0:T(8,128)(2,1)S(1)}, bf16[512,1024]{1,0:T(8,128)(2,1)S(1)}, u32[]{:S(2)}, u32[]{:S(2)}) %collective-permute-start.36) | collective-permute-done | bytes 1048608 | tf_op jit(solution)/shard_map/ppermute | solution.py:332
  446.5 3.6 fusion.35
  458.0 18.5 %collective-permute-done.37 = bf16[512,1024]{1,0:T(8,128)(2,1)} collective-permute-done((bf16[512,1024]{1,0:T(8,128)(2,1)}, bf16[512,1024]{1,0:T(8,128)(2,1)}, u32[]{:S(2)}, u32[]{:S(2)}) %collective-permute-start.37) | collective-permute-done | bytes 1048608 | tf_op jit(solution)/shard_map/ppermute | solution.py:332
  476.5 16.9 %collective-permute-done.39 = bf16[512,1024]{1,0:T(8,128)(2,1)} collective-permute-done((bf16[512,1024]{1,0:T(8,128)(2,1)}, bf16[512,1024]{1,0:T(8,128)(2,1)}, u32[]{:S(2)}, u32[]{:S(2)}) %collective-permute-start.39) | collective-permute-done | bytes 1048608 | tf_op jit(solution)/shard_map/ppermute | solution.py:332
  494.7 4.1 add_convert_fusion.3
  504.0 7.4 %collective-permute-start.41 = (bf16[128,1024]{1,0:T(8,128)(2,1)S(1)}, bf16[128,1024]{1,0:T(8,128)(2,1)S(1)}, u32[]{:S(2)}, u32[]{:S(2)}) collective-permute-start(bf16[128,1024]{1,0:T(8,128)(2,1)S(1)} %get-tuple-element.189), channel_id=1, source_target_pairs={{0,4},{2,6},{4,0},{6,2},{1,5},{3,7},{5,1},{7,3},{8,12},{10,14},{12... | collective-permute-start | bytes 786440 | tf_op jit(solution)/shard_map/ppermute | solution.py:329
  511.4 14.7 %collective-permute-done.41.refs_2_ = bf16[128,1024]{1,0:T(8,128)(2,1)S(1)} collective-permute-done((bf16[128,1024]{1,0:T(8,128)(2,1)S(1)}, bf16[128,1024]{1,0:T(8,128)(2,1)S(1)}, u32[]{:S(2)}, u32[]{:S(2)}) %collective-permute-start.41) | collective-permute-done | bytes 262176 | tf_op jit(solution)/shard_map/ppermute | solution.py:329
  531.1 3.7 convolution_convert_fusion.8.g_ref
  534.9 13.1 %attend_back.1 = bf16[1024,768]{1,0:T(8,128)(2,1)S(1)} custom-call(s32[8]{0:T(128)S(1)} %bitcast.96, bf16[1024,768]{1,0:T(8,128)(2,1)S(1)} %copy-done, bf16[1024,768]{1,0:T(8,128)(2,1)S(1)} %copy-done, bf16[1024,768]{1,0:T(8,128)(2,1)S(1)} %copy-done, bf16[1024,256]{1,0:T(8,128)(2,1)S(1)} %convolution_convert_fusion.8.g_ref, ...), custom_call_target="tpu_custom_call" | custom-call | flops 536870912 | bytes 4194304 | tf_op jit(solution)/shard_map/attend_back/pallas_call | solution.py:272
  550.5 3.1 add_convert_fusion.2
  553.6 3.6 collective-permute-done.46.refs_1_
  559.0 5.1 convolution_convert_fusion.1
  564.8 3.8 convolution_convert_fusion.7
  568.6 3.8 convolution_convert_fusion.6
  582.8 25.0 %collective-permute-done.52.refs_2_ = bf16[128,1024]{1,0:T(8,128)(2,1)S(1)} collective-permute-done((bf16[128,1024]{1,0:T(8,128)(2,1)S(1)}, bf16[128,1024]{1,0:T(8,128)(2,1)S(1)}, u32[]{:S(2)}, u32[]{:S(2)}) %collective-permute-start.52) | collective-permute-done | bytes 262176 | tf_op jit(solution)/shard_map/ppermute | solution.py:329
  609.7 10.1 %collective-permute-done.54 = bf16[512,1024]{1,0:T(8,128)(2,1)S(1)} collective-permute-done((bf16[512,1024]{1,0:T(8,128)(2,1)S(1)}, bf16[512,1024]{1,0:T(8,128)(2,1)S(1)}, u32[]{:S(2)}, u32[]{:S(2)}) %collective-permute-start.54) | collective-permute-done | bytes 1048608 | tf_op jit(solution)/shard_map/ppermute | solution.py:332
  630.8 3.7 collective-permute-start.61
  651.0 9.4 %collective-permute-done.63.refs_2_ = bf16[128,1024]{1,0:T(8,128)(2,1)S(1)} collective-permute-done((bf16[128,1024]{1,0:T(8,128)(2,1)}, bf16[128,1024]{1,0:T(8,128)(2,1)S(1)}, u32[]{:S(2)}, u32[]{:S(2)}) %collective-permute-start.63) | collective-permute-done | bytes 262176 | tf_op jit(solution)/shard_map/ppermute | solution.py:329
  (381 shorter events, 176.4 us)
Async XLA Ops:
  7.2 82.0 %all-gather.5.cloned.1.call-start = ((), (), s32[]{:S(2)}) async-start(), calls=%async_computation.4 | async-start | bytes 4718592 | tf_op jit(solution)/shard_map/all_gather | solution.py:391
  19.1 18.8 %collective-permute-start.1 = (bf16[128,1024]{1,0:T(8,128)(2,1)S(1)}, bf16[128,1024]{1,0:T(8,128)(2,1)S(1)}, u32[]{:S(2)}, u32[]{:S(2)}) collective-permute-start(bf16[128,1024]{1,0:T(8,128)(2,1)S(1)} %pad_maximum_fusion.18), channel_id=1, source_target_pairs={{0,4},{2,6},{4,0},{6,2},{1,5},{3,7},{5,1},{7,3},{8,12},{10,14},{12... | collective-permute-start | bytes 786440 | tf_op jit(solution)/shard_map/ppermute | solution.py:329
  19.4 18.5 %collective-permute-start = (bf16[128,1024]{1,0:T(8,128)(2,1)S(1)}, bf16[128,1024]{1,0:T(8,128)(2,1)S(1)}, u32[]{:S(2)}, u32[]{:S(2)}) collective-permute-start(bf16[128,1024]{1,0:T(8,128)(2,1)S(1)} %pad_maximum_fusion.17), channel_id=1, source_target_pairs={{0,2},{2,4},{4,6},{6,0},{1,3},{3,5},{5,7},{7,1},{8,10},{10,12},{12... | collective-permute-start | bytes 786440 | tf_op jit(solution)/shard_map/ppermute | solution.py:329
  20.5 19.0 %collective-permute-start.2 = (bf16[128,1024]{1,0:T(8,128)(2,1)S(1)}, bf16[128,1024]{1,0:T(8,128)(2,1)S(1)}, u32[]{:S(2)}, u32[]{:S(2)}) collective-permute-start(bf16[128,1024]{1,0:T(8,128)(2,1)S(1)} %pad_maximum_fusion.19), channel_id=1, source_target_pairs={{0,6},{2,0},{4,2},{6,4},{1,7},{3,1},{5,3},{7,5},{8,14},{10,8},{12,... | collective-permute-start | bytes 786440 | tf_op jit(solution)/shard_map/ppermute | solution.py:329
  39.8 195.4 %reduce-scatter.5.cloned.1.call-start = ((), (), s32[]{:S(2)}) async-start(), calls=%async_computation.5 | async-start | bytes 4718592 | tf_op jit(solution)/shard_map/reduce_scatter | solution.py:394
  39.8 23.5 %collective-permute-start.9 = (bf16[512,1024]{1,0:T(8,128)(2,1)S(1)}, bf16[512,1024]{1,0:T(8,128)(2,1)S(1)}, u32[]{:S(2)}, u32[]{:S(2)}) collective-permute-start(bf16[512,1024]{1,0:T(8,128)(2,1)S(1)} %place.8.refs_0_), channel_id=1, source_target_pairs={{0,16},{8,24},{16,0},{24,8},{1,17},{9,25},{17,1},{25,9},{2,18},{10... | collective-permute-start | bytes 3145736 | tf_op jit(solution)/shard_map/ppermute | solution.py:332
  41.4 24.2 %collective-permute-start.8 = (bf16[512,1024]{1,0:T(8,128)(2,1)S(1)}, bf16[512,1024]{1,0:T(8,128)(2,1)S(1)}, u32[]{:S(2)}, u32[]{:S(2)}) collective-permute-start(bf16[512,1024]{1,0:T(8,128)(2,1)S(1)} %place.8.refs_0_), channel_id=1, source_target_pairs={{0,8},{8,0},{16,24},{24,16},{1,9},{9,1},{17,25},{25,17},{2,10},{10... | collective-permute-start | bytes 3145736 | tf_op jit(solution)/shard_map/ppermute | solution.py:332
  91.6 23.6 %collective-permute-start.13 = (bf16[128,1024]{1,0:T(8,128)(2,1)S(1)}, bf16[128,1024]{1,0:T(8,128)(2,1)S(1)}, u32[]{:S(2)}, u32[]{:S(2)}) collective-permute-start(bf16[128,1024]{1,0:T(8,128)(2,1)S(1)} %get-tuple-element.207), channel_id=1, source_target_pairs={{0,4},{2,6},{4,0},{6,2},{1,5},{3,7},{5,1},{7,3},{8,12},{10,14},{12... | collective-permute-start | bytes 786440 | tf_op jit(solution)/shard_map/ppermute | solution.py:329
  92.9 22.2 %collective-permute-start.12 = (bf16[128,1024]{1,0:T(8,128)(2,1)S(1)}, bf16[128,1024]{1,0:T(8,128)(2,1)S(1)}, u32[]{:S(2)}, u32[]{:S(2)}) collective-permute-start(bf16[128,1024]{1,0:T(8,128)(2,1)S(1)} %get-tuple-element.208), channel_id=1, source_target_pairs={{0,2},{2,4},{4,6},{6,0},{1,3},{3,5},{5,7},{7,1},{8,10},{10,12},{12... | collective-permute-start | bytes 786440 | tf_op jit(solution)/shard_map/ppermute | solution.py:329
  115.4 23.4 %collective-permute-start.19 = (bf16[512,1024]{1,0:T(8,128)(2,1)S(1)}, bf16[512,1024]{1,0:T(8,128)(2,1)S(1)}, u32[]{:S(2)}, u32[]{:S(2)}) collective-permute-start(bf16[512,1024]{1,0:T(8,128)(2,1)S(1)} %place.9), channel_id=1, source_target_pairs={{0,16},{8,24},{16,0},{24,8},{1,17},{9,25},{17,1},{25,9},{2,18},{10... | collective-permute-start | bytes 3145736 | tf_op jit(solution)/shard_map/ppermute | solution.py:332
  116.9 24.4 %collective-permute-start.18 = (bf16[512,1024]{1,0:T(8,128)(2,1)S(1)}, bf16[512,1024]{1,0:T(8,128)(2,1)S(1)}, u32[]{:S(2)}, u32[]{:S(2)}) collective-permute-start(bf16[512,1024]{1,0:T(8,128)(2,1)S(1)} %place.9), channel_id=1, source_target_pairs={{0,8},{8,0},{16,24},{24,16},{1,9},{9,1},{17,25},{25,17},{2,10},{10... | collective-permute-start | bytes 3145736 | tf_op jit(solution)/shard_map/ppermute | solution.py:332
  118.5 24.4 %collective-permute-start.17 = (bf16[128,1024]{1,0:T(8,128)(2,1)S(1)}, bf16[128,1024]{1,0:T(8,128)(2,1)S(1)}, u32[]{:S(2)}, u32[]{:S(2)}) collective-permute-start(bf16[128,1024]{1,0:T(8,128)(2,1)S(1)} %get-tuple-element.202), channel_id=1, source_target_pairs={{0,6},{2,0},{4,2},{6,4},{1,7},{3,1},{5,3},{7,5},{8,14},{10,8},{12,... | collective-permute-start | bytes 786440 | tf_op jit(solution)/shard_map/ppermute | solution.py:329
  118.5 25.4 %collective-permute-start.16 = (bf16[128,1024]{1,0:T(8,128)(2,1)S(1)}, bf16[128,1024]{1,0:T(8,128)(2,1)S(1)}, u32[]{:S(2)}, u32[]{:S(2)}) collective-permute-start(bf16[128,1024]{1,0:T(8,128)(2,1)S(1)} %get-tuple-element.203), channel_id=1, source_target_pairs={{0,4},{2,6},{4,0},{6,2},{1,5},{3,7},{5,1},{7,3},{8,12},{10,14},{12... | collective-permute-start | bytes 786440 | tf_op jit(solution)/shard_map/ppermute | solution.py:329
  121.3 22.7 %collective-permute-start.15 = (bf16[128,1024]{1,0:T(8,128)(2,1)S(1)}, bf16[128,1024]{1,0:T(8,128)(2,1)S(1)}, u32[]{:S(2)}, u32[]{:S(2)}) collective-permute-start(bf16[128,1024]{1,0:T(8,128)(2,1)S(1)} %get-tuple-element.204), channel_id=1, source_target_pairs={{0,2},{2,4},{4,6},{6,0},{1,3},{3,5},{5,7},{7,1},{8,10},{10,12},{12... | collective-permute-start | bytes 786440 | tf_op jit(solution)/shard_map/ppermute | solution.py:329
  161.6 122.6 %all-gather.9.cloned.1.call-start = ((), (), s32[]{:S(2)}) async-start(), calls=%async_computation.7 | async-start | bytes 4718592 | tf_op jit(solution)/shard_map/all_gather | solution.py:391
  161.6 24.2 %collective-permute-start.26 = (bf16[512,1024]{1,0:T(8,128)(2,1)}, bf16[512,1024]{1,0:T(8,128)(2,1)S(1)}, u32[]{:S(2)}, u32[]{:S(2)}) collective-permute-start(bf16[512,1024]{1,0:T(8,128)(2,1)} %copy-done.10), channel_id=1, source_target_pairs={{0,16},{8,24},{16,0},{24,8},{1,17},{9,25},{17,1},{25,9},{2,18},{10... | collective-permute-start | bytes 3145736 | tf_op jit(solution)/shard_map/ppermute | solution.py:332
  162.3 25.9 %collective-permute-start.25 = (bf16[512,1024]{1,0:T(8,128)(2,1)}, bf16[512,1024]{1,0:T(8,128)(2,1)S(1)}, u32[]{:S(2)}, u32[]{:S(2)}) collective-permute-start(bf16[512,1024]{1,0:T(8,128)(2,1)} %copy-done.10), channel_id=1, source_target_pairs={{0,8},{8,0},{16,24},{24,16},{1,9},{9,1},{17,25},{25,17},{2,10},{10... | collective-permute-start | bytes 3145736 | tf_op jit(solution)/shard_map/ppermute | solution.py:332
  187.6 45.3 %collective-permute-start.28 = (bf16[256,1024]{1,0:T(8,128)(2,1)}, bf16[256,1024]{1,0:T(8,128)(2,1)}, u32[]{:S(2)}, u32[]{:S(2)}) collective-permute-start(bf16[256,1024]{1,0:T(8,128)(2,1)} %slice.207), channel_id=1, source_target_pairs={{0,8},{8,0},{16,24},{24,16},{1,9},{9,1},{17,25},{25,17},{2,10},{10... | collective-permute-start | bytes 1572872 | tf_op jit(solution)/shard_map/ppermute | solution.py:332
  190.1 42.9 %collective-permute-start.27 = (bf16[256,1024]{1,0:T(8,128)(2,1)}, bf16[256,1024]{1,0:T(8,128)(2,1)}, u32[]{:S(2)}, u32[]{:S(2)}) collective-permute-start(bf16[256,1024]{1,0:T(8,128)(2,1)} %slice.206), channel_id=1, source_target_pairs={{0,16},{8,24},{16,0},{24,8},{1,17},{9,25},{17,1},{25,9},{2,18},{10... | collective-permute-start | bytes 1572872 | tf_op jit(solution)/shard_map/ppermute | solution.py:332
  194.2 37.5 %collective-permute-start.23 = (bf16[128,1024]{1,0:T(8,128)(2,1)S(1)}, bf16[128,1024]{1,0:T(8,128)(2,1)S(1)}, u32[]{:S(2)}, u32[]{:S(2)}) collective-permute-start(bf16[128,1024]{1,0:T(8,128)(2,1)S(1)} %get-tuple-element.199), channel_id=1, source_target_pairs={{0,4},{2,6},{4,0},{6,2},{1,5},{3,7},{5,1},{7,3},{8,12},{10,14},{12... | collective-permute-start | bytes 786440 | tf_op jit(solution)/shard_map/ppermute | solution.py:329
  197.1 34.6 %collective-permute-start.22 = (bf16[128,1024]{1,0:T(8,128)(2,1)S(1)}, bf16[128,1024]{1,0:T(8,128)(2,1)S(1)}, u32[]{:S(2)}, u32[]{:S(2)}) collective-permute-start(bf16[128,1024]{1,0:T(8,128)(2,1)S(1)} %get-tuple-element.200), channel_id=1, source_target_pairs={{0,2},{2,4},{4,6},{6,0},{1,3},{3,5},{5,7},{7,1},{8,10},{10,12},{12... | collective-permute-start | bytes 786440 | tf_op jit(solution)/shard_map/ppermute | solution.py:329
  238.6 93.5 %all-gather.7.cloned.1.call-start = ((), (), s32[]{:S(2)}) async-start(), calls=%async_computation.6 | async-start | bytes 4718592 | tf_op jit(solution)/shard_map/all_gather | solution.py:391
  241.8 141.2 %reduce-scatter.7.cloned.1.call-start = ((), (), s32[]{:S(2)}) async-start(), calls=%async_computation.8 | async-start | bytes 4718592 | tf_op jit(solution)/shard_map/reduce_scatter | solution.py:394
  242.2 22.9 %collective-permute-start.30 = (bf16[512,1024]{1,0:T(8,128)(2,1)}, bf16[512,1024]{1,0:T(8,128)(2,1)S(1)}, u32[]{:S(2)}, u32[]{:S(2)}) collective-permute-start(bf16[512,1024]{1,0:T(8,128)(2,1)} %copy-done.13), channel_id=1, source_target_pairs={{0,16},{8,24},{16,0},{24,8},{1,17},{9,25},{17,1},{25,9},{2,18},{10... | collective-permute-start | bytes 3145736 | tf_op jit(solution)/shard_map/ppermute | solution.py:332
  243.5 24.0 %collective-permute-start.29 = (bf16[512,1024]{1,0:T(8,128)(2,1)}, bf16[512,1024]{1,0:T(8,128)(2,1)S(1)}, u32[]{:S(2)}, u32[]{:S(2)}) collective-permute-start(bf16[512,1024]{1,0:T(8,128)(2,1)} %copy-done.13), channel_id=1, source_target_pairs={{0,8},{8,0},{16,24},{24,16},{1,9},{9,1},{17,25},{25,17},{2,10},{10... | collective-permute-start | bytes 3145736 | tf_op jit(solution)/shard_map/ppermute | solution.py:332
  309.0 131.6 %reduce-scatter.9.cloned.1.call-start = ((), (), s32[]{:S(2)}) async-start(), calls=%async_computation.9 | async-start | bytes 4718592 | tf_op jit(solution)/shard_map/reduce_scatter | solution.py:394
  383.0 145.1 %all-gather.11.cloned.1.call-start = ((), (), s32[]{:S(2)}) async-start(), calls=%async_computation.10 | async-start | bytes 4718592 | tf_op jit(solution)/shard_map/all_gather | solution.py:391
  391.0 26.2 %collective-permute-start.34 = (bf16[512,1024]{1,0:T(8,128)(2,1)S(1)}, bf16[512,1024]{1,0:T(8,128)(2,1)S(1)}, u32[]{:S(2)}, u32[]{:S(2)}) collective-permute-start(bf16[512,1024]{1,0:T(8,128)(2,1)S(1)} %get-tuple-element.157), channel_id=1, source_target_pairs={{0,8},{8,0},{16,24},{24,16},{1,9},{9,1},{17,25},{25,17},{2,10},{10... | collective-permute-start | bytes 3145736 | tf_op jit(solution)/shard_map/ppermute | solution.py:332
  392.6 44.8 %collective-permute-start.36 = (bf16[512,1024]{1,0:T(8,128)(2,1)S(1)}, bf16[512,1024]{1,0:T(8,128)(2,1)S(1)}, u32[]{:S(2)}, u32[]{:S(2)}) collective-permute-start(bf16[512,1024]{1,0:T(8,128)(2,1)S(1)} %get-tuple-element.158), channel_id=1, source_target_pairs={{0,24},{8,16},{16,8},{24,0},{1,25},{9,17},{17,9},{25,1},{2,26},{10... | collective-permute-start | bytes 3145736 | tf_op jit(solution)/shard_map/ppermute | solution.py:332
  394.0 44.7 %collective-permute-start.35 = (bf16[512,1024]{1,0:T(8,128)(2,1)S(1)}, bf16[512,1024]{1,0:T(8,128)(2,1)S(1)}, u32[]{:S(2)}, u32[]{:S(2)}) collective-permute-start(bf16[512,1024]{1,0:T(8,128)(2,1)S(1)} %get-tuple-element.159), channel_id=1, source_target_pairs={{0,16},{8,24},{16,0},{24,8},{1,17},{9,25},{17,1},{25,9},{2,18},{10... | collective-permute-start | bytes 3145736 | tf_op jit(solution)/shard_map/ppermute | solution.py:332
  446.2 196.3 %reduce-scatter.11.cloned.1.call-start = ((), (), s32[]{:S(2)}) async-start(), calls=%async_computation.11 | async-start | bytes 4718592 | tf_op jit(solution)/shard_map/reduce_scatter | solution.py:394
  450.0 26.4 %collective-permute-start.37 = (bf16[512,1024]{1,0:T(8,128)(2,1)}, bf16[512,1024]{1,0:T(8,128)(2,1)}, u32[]{:S(2)}, u32[]{:S(2)}) collective-permute-start(bf16[512,1024]{1,0:T(8,128)(2,1)} %get-tuple-element.154), channel_id=1, source_target_pairs={{0,8},{8,0},{16,24},{24,16},{1,9},{9,1},{17,25},{25,17},{2,10},{10... | collective-permute-start | bytes 3145736 | tf_op jit(solution)/shard_map/ppermute | solution.py:332
  451.5 41.8 %collective-permute-start.39 = (bf16[512,1024]{1,0:T(8,128)(2,1)}, bf16[512,1024]{1,0:T(8,128)(2,1)}, u32[]{:S(2)}, u32[]{:S(2)}) collective-permute-start(bf16[512,1024]{1,0:T(8,128)(2,1)} %get-tuple-element.155), channel_id=1, source_target_pairs={{0,24},{8,16},{16,8},{24,0},{1,25},{9,17},{17,9},{25,1},{2,26},{10... | collective-permute-start | bytes 3145736 | tf_op jit(solution)/shard_map/ppermute | solution.py:332
  452.1 42.6 %collective-permute-start.38 = (bf16[512,1024]{1,0:T(8,128)(2,1)}, bf16[512,1024]{1,0:T(8,128)(2,1)}, u32[]{:S(2)}, u32[]{:S(2)}) collective-permute-start(bf16[512,1024]{1,0:T(8,128)(2,1)} %get-tuple-element.156), channel_id=1, source_target_pairs={{0,16},{8,24},{16,0},{24,8},{1,17},{9,25},{17,1},{25,9},{2,18},{10... | collective-permute-start | bytes 3145736 | tf_op jit(solution)/shard_map/ppermute | solution.py:332
  455.2 56.2 %collective-permute-start.42 = (bf16[128,1024]{1,0:T(8,128)(2,1)S(1)}, bf16[128,1024]{1,0:T(8,128)(2,1)S(1)}, u32[]{:S(2)}, u32[]{:S(2)}) collective-permute-start(bf16[128,1024]{1,0:T(8,128)(2,1)S(1)} %get-tuple-element.188), channel_id=1, source_target_pairs={{0,6},{2,0},{4,2},{6,4},{1,7},{3,1},{5,3},{7,5},{8,14},{10,8},{12,... | collective-permute-start | bytes 786440 | tf_op jit(solution)/shard_map/ppermute | solution.py:329
  500.5 47.5 %collective-permute-start.43 = (bf16[512,1024]{1,0:T(8,128)(2,1)}, bf16[512,1024]{1,0:T(8,128)(2,1)}, u32[]{:S(2)}, u32[]{:S(2)}) collective-permute-start(bf16[512,1024]{1,0:T(8,128)(2,1)} %get-tuple-element.151), channel_id=1, source_target_pairs={{0,8},{8,0},{16,24},{24,16},{1,9},{9,1},{17,25},{25,17},{2,10},{10... | collective-permute-start | bytes 3145736 | tf_op jit(solution)/shard_map/ppermute | solution.py:332
  502.0 48.4 %collective-permute-start.45 = (bf16[512,1024]{1,0:T(8,128)(2,1)}, bf16[512,1024]{1,0:T(8,128)(2,1)}, u32[]{:S(2)}, u32[]{:S(2)}) collective-permute-start(bf16[512,1024]{1,0:T(8,128)(2,1)} %get-tuple-element.152), channel_id=1, source_target_pairs={{0,24},{8,16},{16,8},{24,0},{1,25},{9,17},{17,9},{25,1},{2,26},{10... | collective-permute-start | bytes 3145736 | tf_op jit(solution)/shard_map/ppermute | solution.py:332
  503.4 47.0 %collective-permute-start.44 = (bf16[512,1024]{1,0:T(8,128)(2,1)}, bf16[512,1024]{1,0:T(8,128)(2,1)}, u32[]{:S(2)}, u32[]{:S(2)}) collective-permute-start(bf16[512,1024]{1,0:T(8,128)(2,1)} %get-tuple-element.153), channel_id=1, source_target_pairs={{0,16},{8,24},{16,0},{24,8},{1,17},{9,25},{17,1},{25,9},{2,18},{10... | collective-permute-start | bytes 3145736 | tf_op jit(solution)/shard_map/ppermute | solution.py:332
  504.0 22.1 %collective-permute-start.41 = (bf16[128,1024]{1,0:T(8,128)(2,1)S(1)}, bf16[128,1024]{1,0:T(8,128)(2,1)S(1)}, u32[]{:S(2)}, u32[]{:S(2)}) collective-permute-start(bf16[128,1024]{1,0:T(8,128)(2,1)S(1)} %get-tuple-element.189), channel_id=1, source_target_pairs={{0,4},{2,6},{4,0},{6,2},{1,5},{3,7},{5,1},{7,3},{8,12},{10,14},{12... | collective-permute-start | bytes 786440 | tf_op jit(solution)/shard_map/ppermute | solution.py:329
  529.5 24.1 %collective-permute-start.48 = (bf16[128,1024]{1,0:T(8,128)(2,1)S(1)}, bf16[128,1024]{1,0:T(8,128)(2,1)S(1)}, u32[]{:S(2)}, u32[]{:S(2)}) collective-permute-start(bf16[128,1024]{1,0:T(8,128)(2,1)S(1)} %get-tuple-element.184), channel_id=1, source_target_pairs={{0,6},{2,0},{4,2},{6,4},{1,7},{3,1},{5,3},{7,5},{8,14},{10,8},{12,... | collective-permute-start | bytes 786440 | tf_op jit(solution)/shard_map/ppermute | solution.py:329
  529.5 24.0 %collective-permute-start.47 = (bf16[128,1024]{1,0:T(8,128)(2,1)S(1)}, bf16[128,1024]{1,0:T(8,128)(2,1)S(1)}, u32[]{:S(2)}, u32[]{:S(2)}) collective-permute-start(bf16[128,1024]{1,0:T(8,128)(2,1)S(1)} %get-tuple-element.185), channel_id=1, source_target_pairs={{0,4},{2,6},{4,0},{6,2},{1,5},{3,7},{5,1},{7,3},{8,12},{10,14},{12... | collective-permute-start | bytes 786440 | tf_op jit(solution)/shard_map/ppermute | solution.py:329
  572.8 36.8 %collective-permute-start.50 = (bf16[512,1024]{1,0:T(8,128)(2,1)S(1)}, bf16[512,1024]{1,0:T(8,128)(2,1)S(1)}, u32[]{:S(2)}, u32[]{:S(2)}) collective-permute-start(bf16[512,1024]{1,0:T(8,128)(2,1)S(1)} %pad_maximum_fusion.8), channel_id=1, source_target_pairs={{0,8},{8,0},{16,24},{24,16},{1,9},{9,1},{17,25},{25,17},{2,10},{10... | collective-permute-start | bytes 3145736 | tf_op jit(solution)/shard_map/ppermute | solution.py:332
  574.8 45.0 %collective-permute-start.54 = (bf16[512,1024]{1,0:T(8,128)(2,1)S(1)}, bf16[512,1024]{1,0:T(8,128)(2,1)S(1)}, u32[]{:S(2)}, u32[]{:S(2)}) collective-permute-start(bf16[512,1024]{1,0:T(8,128)(2,1)S(1)} %pad_maximum_fusion.9), channel_id=1, source_target_pairs={{0,16},{8,24},{16,0},{24,8},{1,17},{9,25},{17,1},{25,9},{2,18},{10... | collective-permute-start | bytes 3145736 | tf_op jit(solution)/shard_map/ppermute | solution.py:332
  576.4 43.4 %collective-permute-start.55 = (bf16[512,1024]{1,0:T(8,128)(2,1)S(1)}, bf16[512,1024]{1,0:T(8,128)(2,1)S(1)}, u32[]{:S(2)}, u32[]{:S(2)}) collective-permute-start(bf16[512,1024]{1,0:T(8,128)(2,1)S(1)} %pad_maximum_fusion.10), channel_id=1, source_target_pairs={{0,24},{8,16},{16,8},{24,0},{1,25},{9,17},{17,9},{25,1},{2,26},{10... | collective-permute-start | bytes 3145736 | tf_op jit(solution)/shard_map/ppermute | solution.py:332
  577.7 30.1 %collective-permute-start.52 = (bf16[128,1024]{1,0:T(8,128)(2,1)S(1)}, bf16[128,1024]{1,0:T(8,128)(2,1)S(1)}, u32[]{:S(2)}, u32[]{:S(2)}) collective-permute-start(bf16[128,1024]{1,0:T(8,128)(2,1)S(1)} %get-tuple-element.175), channel_id=1, source_target_pairs={{0,4},{2,6},{4,0},{6,2},{1,5},{3,7},{5,1},{7,3},{8,12},{10,14},{12... | collective-permute-start | bytes 786440 | tf_op jit(solution)/shard_map/ppermute | solution.py:329
  579.8 28.0 %collective-permute-start.51 = (bf16[128,1024]{1,0:T(8,128)(2,1)S(1)}, bf16[128,1024]{1,0:T(8,128)(2,1)S(1)}, u32[]{:S(2)}, u32[]{:S(2)}) collective-permute-start(bf16[128,1024]{1,0:T(8,128)(2,1)S(1)} %get-tuple-element.176), channel_id=1, source_target_pairs={{0,2},{2,4},{4,6},{6,0},{1,3},{3,5},{5,7},{7,1},{8,10},{10,12},{12... | collective-permute-start | bytes 786440 | tf_op jit(solution)/shard_map/ppermute | solution.py:329
  637.3 23.2 %collective-permute-start.63 = (bf16[128,1024]{1,0:T(8,128)(2,1)}, bf16[128,1024]{1,0:T(8,128)(2,1)S(1)}, u32[]{:S(2)}, u32[]{:S(2)}) collective-permute-start(bf16[128,1024]{1,0:T(8,128)(2,1)} %get-tuple-element.167), channel_id=1, source_target_pairs={{0,4},{2,6},{4,0},{6,2},{1,5},{3,7},{5,1},{7,3},{8,12},{10,14},{12... | collective-permute-start | bytes 786440 | tf_op jit(solution)/shard_map/ppermute | solution.py:329
  639.5 20.9 %collective-permute-start.62 = (bf16[128,1024]{1,0:T(8,128)(2,1)}, bf16[128,1024]{1,0:T(8,128)(2,1)S(1)}, u32[]{:S(2)}, u32[]{:S(2)}) collective-permute-start(bf16[128,1024]{1,0:T(8,128)(2,1)} %get-tuple-element.168), channel_id=1, source_target_pairs={{0,2},{2,4},{4,6},{6,0},{1,3},{3,5},{5,7},{7,1},{8,10},{10,12},{12... | collective-permute-start | bytes 786440 | tf_op jit(solution)/shard_map/ppermute | solution.py:329
  (89 other events, 887.6 us)
Sparse Core Ops, SparseCore 0:
  39.9 49.2 all-gather.4
  161.7 61.0 reduce-scatter.4
  238.7 45.3 all-gather.8
  286.2 45.8 all-gather.6
  334.2 48.7 reduce-scatter.6
  385.2 48.1 reduce-scatter.8
  446.3 52.2 all-gather.10
  564.2 60.4 reduce-scatter.10

commit v5 on v4

--- a/solution.py
+++ b/solution.py
@@ -355,13 +355,16 @@
             came.append(after(along(jnp.concatenate(sent, 1), shift), *late))
         return place(c_at, came, 1, ("down",), bf16)[0]
 
-    def swap_rows(tensor, ways, late=()):
+    def swap_rows(tensor, ways, late=(), waiting=None):
         piece = tensor.shape[0] // n_ctx
         came = []
         for shift in range(n_ctx):
             sent = lax.dynamic_slice_in_dim(tensor, ((c_at + shift) % n_ctx) * piece, piece, 0)
             came.append(after(along(sent, shift), *late))
-        return place(c_at, came, len(ways), ways, f32)
+        if waiting is None:
+            return place(c_at, came, len(ways), ways, f32)
+        came[1], waiting = lax.optimization_barrier((came[1], waiting))
+        return place(c_at, came, len(ways), ways, f32), waiting
 
     def plane_pieces(tensor, late=()):
         if n_fsdp != 4:
@@ -487,9 +490,6 @@
     grad_w_out = dot_lt(grad_low, attn_late).astype(bf16)
     (up_out,) = swap_rows(after(up_sum, back_one), ("side",))
     attn_weight_sum = scatter_plane(grad_w_qkv, grad_w_out, late=(up_out,))
-    query_out, key_out, value_out, out_proj_out = swap_rows(
-        attn_weight_sum, ("side", "side", "side", "turned")
-    )
     inputs = inputs_low.astype(f32)
     inv_one = lax.rsqrt(jnp.mean(inputs * inputs, -1, keepdims=True) + NORM_EPS)
     back_late = after(back_late, grad_w_qkv, grad_w_out)
@@ -503,7 +503,11 @@
         weighted_one - scaled_one * jnp.mean(weighted_one * scaled_one, -1, keepdims=True)
     )
 
-    gain_grads = after(jnp.stack([grad_gain_one, grad_gain_two]), attn_weight_sum)
+    (query_out, key_out, value_out, out_proj_out), gain_grads = swap_rows(
+        attn_weight_sum,
+        ("side", "side", "side", "turned"),
+        waiting=jnp.stack([grad_gain_one, grad_gain_two]),
+    )
     gain_grads = gain_grads + twin(gain_grads)
     peak = head_max[None]
     held = {m: gain_grads[:, m * feature_block : (m + 1) * feature_block] for m in range(n_fsdp)}

time: 681 us -> 688 us (1.010)
    ppermute x30, waiting for transfers between devices: 104 us -> 121 us  [along(): lax.ppermute(tensor, 'ctx', [(i, (i + shift) % n_ctx) for i in range(n_ct...]
    ppermute x32, waiting for transfers between devices: 181 us -> 169 us  [across(): return lax.ppermute(tensor, 'fsdp', [(i, i ^ mask) for i in range(n_fsdp)])]
    unnamed x140 -> x146, local copies, waits for them, and re-layouts: 15.7 us -> 16.9 us
  transfers between devices with their start and end apart: 73 -> 73, of which waited for: 33 -> 35; matrix products, arithmetic and copies ran while one was open for 22% -> 21% of each run, Pallas kernels for 6% -> 5%
where the time goes in v5:
time: 688 us; the launch traced here: 681 us
  waiting for transfers between devices  347 us (50%)
  starting transfers between devices  98 us (14%)
  matrix products  93.9 us (14%)
  other arithmetic  47.6 us (7%)
  Pallas kernels  39.6 us (6%)
  local copies, waits for them, and re-layouts  39.5 us (6%)
  between operations  15.6 us (2%)
    ppermute x32, waiting for transfers between devices, across(): return lax.ppermute(tensor, 'fsdp', [(i, i ^ mask) for i in range(n_fsdp)])  169 us
    ppermute x30, waiting for transfers between devices, along(): lax.ppermute(tensor, 'ctx', [(i, (i + shift) % n_ctx) for i in range(n_ct...  121 us
    ppermute x30, starting transfers between devices, along(): lax.ppermute(tensor, 'ctx', [(i, (i + shift) % n_ctx) for i in range(n_ct...  55.2 us
    ppermute x32, starting transfers between devices, across(): return lax.ppermute(tensor, 'fsdp', [(i, i ^ mask) for i in range(n_fsdp)])  40.7 us
    dot_general x5, matrix products, dot_rt(): lax.dot_general(left, right, (((1,), (1,)), ((), ())), preferred_element_...  37.4 us
    all_gather x4, waiting for transfers between devices, gather_tokens(): return lax.all_gather(own, ('ctx', 'tp'), axis=0, tiled=True)  35.2 us
    dot_general x4, matrix products, dot(): return jnp.dot(left, right, preferred_element_type=f32)  29.1 us
    dot_general x5, matrix products, dot_lt(): lax.dot_general(left, right, (((0,), (0,)), ((), ())), preferred_element_...  27.4 us
  transfers between devices with their start and end apart: 73, of which 35 were waited for; matrix products, arithmetic and copies ran while one was open for 21% of the time, Pallas kernels for 5%

profile of v5, /device:TPU:0, one launch (start us, length us, event | category | flops | bytes accessed | tf_op | source)
XLA Modules:
  0.0 680.9 jit_solution(12955087202027040860)
XLA Ops:
  8.0 4.1 collective-permute-start.4
  20.5 3.3 collective-permute-start.2
  31.2 6.7 collective-permute-done.1.refs_2_
  42.9 20.4 %collective-permute-done.9.refs_2_ = bf16[512,1024]{1,0:T(8,128)(2,1)S(1)} collective-permute-done((bf16[512,1024]{1,0:T(8,128)(2,1)S(1)}, bf16[512,1024]{1,0:T(8,128)(2,1)S(1)}, u32[]{:S(2)}, u32[]{:S(2)}) %collective-permute-start.9) | collective-permute-done | bytes 1048608 | tf_op jit(solution)/shard_map/ppermute | solution.py:332
  72.8 3.1 collective-permute-done.11
  82.4 6.8 %all-gather.5.cloned.1.call-done.x_ref = bf16[1024,2048]{1,0:T(8,128)(2,1)} async-done(((bf16[128,2048]{1,0:T(8,128)(2,1)}), bf16[1024,2048]{1,0:T(8,128)(2,1)}) %all-gather.5.cloned.1.call-update) | async-done | bytes 4194320 | tf_op jit(solution)/shard_map/all_gather | solution.py:394
  97.5 8.3 %project.1 = (bf16[1024,2048]{1,0:T(8,128)(2,1)}, bf16[1024,768]{1,0:T(8,128)(2,1)}) custom-call(bf16[1024,2048]{1,0:T(8,128)(2,1)} %all-gather.5.cloned.1.call-done.x_ref, f32[1,2048]{1,0:T(1,128)S(1)} %get-tuple-element.239.gain_ref, f32[1024,128]{1,0:T(8,128)S(1)} %copy-done.4, f32[1024,128]{1,0:T(8,128)S(1)} %copy-done.6, ...), custom_call_target="tpu_custom_call" | custom-call | flops 536870912 | bytes 12582912 | tf_op jit(solution)/shard_map/project/pallas_call | solution.py:121
  105.8 9.4 %collective-permute-done.13.refs_2_ = bf16[128,1024]{1,0:T(8,128)(2,1)S(1)} collective-permute-done((bf16[128,1024]{1,0:T(8,128)(2,1)S(1)}, bf16[128,1024]{1,0:T(8,128)(2,1)S(1)}, u32[]{:S(2)}, u32[]{:S(2)}) %collective-permute-start.13) | collective-permute-done | bytes 262176 | tf_op jit(solution)/shard_map/ppermute | solution.py:329
  123.5 15.3 %collective-permute-done.19 = bf16[512,1024]{1,0:T(8,128)(2,1)S(1)} collective-permute-done((bf16[512,1024]{1,0:T(8,128)(2,1)S(1)}, bf16[512,1024]{1,0:T(8,128)(2,1)S(1)}, u32[]{:S(2)}, u32[]{:S(2)}) %collective-permute-start.19) | collective-permute-done | bytes 1048608 | tf_op jit(solution)/shard_map/ppermute | solution.py:332
  144.0 9.7 %attend.1 = (bf16[1024,256]{1,0:T(8,128)(2,1)S(1)}, f32[2,1024,128]{2,1,0:T(8,128)S(1)}, f32[2,8,128]{2,1,0:T(8,128)S(1)}) custom-call(s32[8]{0:T(128)S(1)} %bitcast.95, bf16[1024,768]{1,0:T(8,128)(2,1)S(1)} %copy-done, bf16[1024,768]{1,0:T(8,128)(2,1)S(1)} %copy-done, bf16[1024,768]{1,0:T(8,128)(2,1)S(1)} %copy-done), custom_call_target="tpu_custom_call" | custom-call | flops 536870912 | bytes 2097152 | tf_op jit(solution)/shard_map/attend/pallas_call | solution.py:194
  157.0 4.6 convolution_convert_fusion
  162.8 23.0 %collective-permute-done.26 = bf16[512,1024]{1,0:T(8,128)(2,1)S(1)} collective-permute-done((bf16[512,1024]{1,0:T(8,128)(2,1)}, bf16[512,1024]{1,0:T(8,128)(2,1)S(1)}, u32[]{:S(2)}, u32[]{:S(2)}) %collective-permute-start.26) | collective-permute-done | bytes 1048608 | tf_op jit(solution)/shard_map/ppermute | solution.py:332
  199.1 9.9 %collective-permute-done.24.refs_3_ = bf16[128,1024]{1,0:T(8,128)(2,1)S(1)} collective-permute-done((bf16[128,1024]{1,0:T(8,128)(2,1)S(1)}, bf16[128,1024]{1,0:T(8,128)(2,1)S(1)}, u32[]{:S(2)}, u32[]{:S(2)}) %collective-permute-start.24) | collective-permute-done | bytes 262176 | tf_op jit(solution)/shard_map/ppermute | solution.py:329
  209.0 22.8 %collective-permute-done.23.refs_2_ = bf16[128,1024]{1,0:T(8,128)(2,1)S(1)} collective-permute-done((bf16[128,1024]{1,0:T(8,128)(2,1)S(1)}, bf16[128,1024]{1,0:T(8,128)(2,1)S(1)}, u32[]{:S(2)}, u32[]{:S(2)}) %collective-permute-start.23) | collective-permute-done | bytes 262176 | tf_op jit(solution)/shard_map/ppermute | solution.py:329
  244.9 20.2 %collective-permute-done.30 = bf16[512,1024]{1,0:T(8,128)(2,1)S(1)} collective-permute-done((bf16[512,1024]{1,0:T(8,128)(2,1)}, bf16[512,1024]{1,0:T(8,128)(2,1)S(1)}, u32[]{:S(2)}, u32[]{:S(2)}) %collective-permute-start.30) | collective-permute-done | bytes 1048608 | tf_op jit(solution)/shard_map/ppermute | solution.py:332
  268.1 9.1 %collective-permute-done.32 = bf16[256,1024]{1,0:T(8,128)(2,1)S(1)} collective-permute-done((bf16[256,1024]{1,0:T(8,128)(2,1)S(1)}, bf16[256,1024]{1,0:T(8,128)(2,1)S(1)}, u32[]{:S(2)}, u32[]{:S(2)}) %collective-permute-start.32) | collective-permute-done | bytes 524320 | tf_op jit(solution)/shard_map/ppermute | solution.py:332
  278.3 5.8 all-gather.9.cloned.1.call-done
  284.2 7.7 %fusion.40 = f32[1024,1024]{1,0:T(8,128)S(1)} fusion(bf16[1024,2048]{1,0:T(8,128)(2,1)} %all-gather.9.cloned.1.call-done, bf16[2048,1024]{1,0:T(8,128)(2,1)} %copy-done.38), kind=kOutput, calls=%fused_computation.204 | convolution fusion | flops 4294967296 | bytes 12582912 | tf_op jit(solution)/shard_map/dot_general | solution.py:35
  292.0 6.5 multiply_convert_fusion.2
  299.8 9.1 %convolution_convert_fusion.5 = bf16[1024,2048]{1,0:T(8,128)(2,1)} fusion(bf16[1024,1024]{1,0:T(8,128)(2,1)S(1)} %get-tuple-element.108, bf16[512,1024]{1,0:T(8,128)(2,1)S(1)} %copy-done.35, bf16[512,1024]{1,0:T(8,128)(2,1)S(1)} %copy-done.47, bf16[512,1024]{1,0:T(8,128)(2,1)S(1)} %copy-done.49, bf16[512,1024]{1,0:T(8,128)(2,1)S(1)} %copy-done.14), kind=kOutput, calls=%fused_computation.19 | convolution fusion | flops 4313841664 | bytes 10485760 | tf_op jit(solution)/shard_map/dot_general | solution.py:43
  309.6 22.5 %all-gather.7.cloned.1.call-done = bf16[1024,2048]{1,0:T(8,128)(2,1)} async-done(((bf16[128,2048]{1,0:T(8,128)(2,1)}), bf16[1024,2048]{1,0:T(8,128)(2,1)}) %all-gather.7.cloned.1.call-update) | async-done | bytes 4194320 | tf_op jit(solution)/shard_map/all_gather | solution.py:394
  332.1 11.2 %multiply_convert_fusion = (bf16[1024,1024]{1,0:T(8,128)(2,1)}, bf16[1024,1024]{1,0:T(8,128)(2,1)S(1)}) fusion(f32[1024,1024]{1,0:T(8,128)} %copy-done.62, f32[1024,1024]{1,0:T(8,128)} %get-tuple-element.254, bf16[1024,2048]{1,0:T(8,128)(2,1)} %all-gather.7.cloned.1.call-done, bf16[512,1024]{1,0:T(8,128)(2,1)} %pad_maximum_fusion.6, ...), kind=kOutput, calls=%fused_computation.9 | convolution fusion | flops 4325376000 | bytes 20971520 | tf_op jit(solution)/shard_map/dot_general | solution.py:35
  343.4 6.8 %fusion.41 = f32[1024,2048]{1,0:T(8,128)} fusion(bf16[1024,1024]{1,0:T(8,128)(2,1)S(1)} %get-tuple-element.109, bf16[2048,1024]{1,0:T(8,128)(2,1)S(1)} %copy-done.39), kind=kOutput, calls=%fused_computation.205 | convolution fusion | flops 4294967296 | bytes 14680064 | tf_op jit(solution)/shard_map/dot_general | solution.py:43
  350.2 11.9 %add_convert_fusion = bf16[1024,2048]{1,0:T(8,128)(2,1)} fusion(f32[1024,2048]{1,0:T(8,128)} %fusion.41, bf16[1024,1024]{1,0:T(8,128)(2,1)} %get-tuple-element.110, bf16[512,1024]{1,0:T(8,128)(2,1)S(1)} %copy-done.34, bf16[512,1024]{1,0:T(8,128)(2,1)S(1)} %copy-done.42, bf16[512,1024]{1,0:T(8,128)(2,1)S(1)} %copy-done.45, bf16[512,1024]{1,0:T(8,128)(2,1)S(1)} %copy-done.12), kind=kOutput, calls=%fused_computation.5 | convolution fusion | flops 4315938816 | bytes 18874368 | tf_op jit(solution)/shard_map/dot_general | solution.py:43
  362.1 20.9 %reduce-scatter.7.cloned.1.call-done = bf16[128,2048]{1,0:T(8,128)(2,1)} async-done(((bf16[1024,2048]{1,0:T(8,128)(2,1)}), bf16[128,2048]{1,0:T(8,128)(2,1)}) %reduce-scatter.7.cloned.1.call-update) | async-done | bytes 524304 | tf_op jit(solution)/shard_map/reduce_scatter | solution.py:397
  383.2 7.4 %convolution_convert_fusion.4 = bf16[2048,1024]{1,0:T(8,128)(2,1)S(1)} fusion(bf16[1024,2048]{1,0:T(8,128)(2,1)} %all-gather.7.cloned.1.call-done, bf16[1024,1024]{1,0:T(8,128)(2,1)} %copy-done.66), kind=kOutput, calls=%fused_computation.18 | convolution fusion | flops 4297064448 | bytes 10485760 | tf_op jit(solution)/shard_map/dot_general | solution.py:39
  394.6 6.3 convolution_convert_fusion.3
  400.9 6.3 convolution_convert_fusion.2
  407.2 10.0 %collective-permute-done.34 = bf16[512,1024]{1,0:T(8,128)(2,1)S(1)} collective-permute-done((bf16[512,1024]{1,0:T(8,128)(2,1)S(1)}, bf16[512,1024]{1,0:T(8,128)(2,1)S(1)}, u32[]{:S(2)}, u32[]{:S(2)}) %collective-permute-start.34) | collective-permute-done | bytes 1048608 | tf_op jit(solution)/shard_map/ppermute | solution.py:332
  417.2 20.1 %collective-permute-done.36 = bf16[512,1024]{1,0:T(8,128)(2,1)S(1)} collective-permute-done((bf16[512,1024]{1,0:T(8,128)(2,1)S(1)}, bf16[512,1024]{1,0:T(8,128)(2,1)S(1)}, u32[]{:S(2)}, u32[]{:S(2)}) %collective-permute-start.36) | collective-permute-done | bytes 1048608 | tf_op jit(solution)/shard_map/ppermute | solution.py:332
  446.4 3.6 fusion.35
  457.9 18.5 %collective-permute-done.37 = bf16[512,1024]{1,0:T(8,128)(2,1)} collective-permute-done((bf16[512,1024]{1,0:T(8,128)(2,1)}, bf16[512,1024]{1,0:T(8,128)(2,1)}, u32[]{:S(2)}, u32[]{:S(2)}) %collective-permute-start.37) | collective-permute-done | bytes 1048608 | tf_op jit(solution)/shard_map/ppermute | solution.py:332
  476.4 16.9 %collective-permute-done.39 = bf16[512,1024]{1,0:T(8,128)(2,1)} collective-permute-done((bf16[512,1024]{1,0:T(8,128)(2,1)}, bf16[512,1024]{1,0:T(8,128)(2,1)}, u32[]{:S(2)}, u32[]{:S(2)}) %collective-permute-start.39) | collective-permute-done | bytes 1048608 | tf_op jit(solution)/shard_map/ppermute | solution.py:332
  494.6 4.1 add_convert_fusion.3
  504.0 7.2 %collective-permute-start.41 = (bf16[128,1024]{1,0:T(8,128)(2,1)S(1)}, bf16[128,1024]{1,0:T(8,128)(2,1)S(1)}, u32[]{:S(2)}, u32[]{:S(2)}) collective-permute-start(bf16[128,1024]{1,0:T(8,128)(2,1)S(1)} %get-tuple-element.191), channel_id=1, source_target_pairs={{0,4},{2,6},{4,0},{6,2},{1,5},{3,7},{5,1},{7,3},{8,12},{10,14},{12... | collective-permute-start | bytes 786440 | tf_op jit(solution)/shard_map/ppermute | solution.py:329
  511.2 14.7 %collective-permute-done.41.refs_2_ = bf16[128,1024]{1,0:T(8,128)(2,1)S(1)} collective-permute-done((bf16[128,1024]{1,0:T(8,128)(2,1)S(1)}, bf16[128,1024]{1,0:T(8,128)(2,1)S(1)}, u32[]{:S(2)}, u32[]{:S(2)}) %collective-permute-start.41) | collective-permute-done | bytes 262176 | tf_op jit(solution)/shard_map/ppermute | solution.py:329
  530.9 3.7 convolution_convert_fusion.8.g_ref
  534.6 13.1 %attend_back.1 = bf16[1024,768]{1,0:T(8,128)(2,1)S(1)} custom-call(s32[8]{0:T(128)S(1)} %bitcast.96, bf16[1024,768]{1,0:T(8,128)(2,1)S(1)} %copy-done, bf16[1024,768]{1,0:T(8,128)(2,1)S(1)} %copy-done, bf16[1024,768]{1,0:T(8,128)(2,1)S(1)} %copy-done, bf16[1024,256]{1,0:T(8,128)(2,1)S(1)} %convolution_convert_fusion.8.g_ref, ...), custom_call_target="tpu_custom_call" | custom-call | flops 536870912 | bytes 4194304 | tf_op jit(solution)/shard_map/attend_back/pallas_call | solution.py:272
  550.2 3.1 add_convert_fusion.2
  553.3 3.5 collective-permute-done.46.refs_1_
  558.6 5.0 convolution_convert_fusion.1
  563.7 3.7 convolution_convert_fusion.7
  567.6 3.7 convolution_convert_fusion.6
  580.4 12.0 %collective-permute-done.53.refs_3_ = bf16[128,1024]{1,0:T(8,128)(2,1)S(1)} collective-permute-done((bf16[128,1024]{1,0:T(8,128)(2,1)S(1)}, bf16[128,1024]{1,0:T(8,128)(2,1)S(1)}, u32[]{:S(2)}, u32[]{:S(2)}) %collective-permute-start.53) | collective-permute-done | bytes 262176 | tf_op jit(solution)/shard_map/ppermute | solution.py:329
  592.4 8.3 %collective-permute-start.51 = (bf16[128,1024]{1,0:T(8,128)(2,1)S(1)}, bf16[128,1024]{1,0:T(8,128)(2,1)S(1)}, u32[]{:S(2)}, u32[]{:S(2)}) collective-permute-start(bf16[128,1024]{1,0:T(8,128)(2,1)S(1)} %get-tuple-element.178), channel_id=1, source_target_pairs={{0,2},{2,4},{4,6},{6,0},{1,3},{3,5},{5,7},{7,1},{8,10},{10,12},{12... | collective-permute-start | bytes 786440 | tf_op jit(solution)/shard_map/ppermute | solution.py:329
  601.6 17.9 %collective-permute-done.52.refs_2_ = bf16[128,1024]{1,0:T(8,128)(2,1)S(1)} collective-permute-done((bf16[128,1024]{1,0:T(8,128)(2,1)S(1)}, bf16[128,1024]{1,0:T(8,128)(2,1)S(1)}, u32[]{:S(2)}, u32[]{:S(2)}) %collective-permute-start.52) | collective-permute-done | bytes 262176 | tf_op jit(solution)/shard_map/ppermute | solution.py:329
  625.0 9.3 %collective-permute-done.56.refs_1_ = bf16[128,1024]{1,0:T(8,128)(2,1)S(1)} collective-permute-done((bf16[128,1024]{1,0:T(8,128)(2,1)S(1)}, bf16[128,1024]{1,0:T(8,128)(2,1)S(1)}, u32[]{:S(2)}, u32[]{:S(2)}) %collective-permute-start.56) | collective-permute-done | bytes 262176 | tf_op jit(solution)/shard_map/ppermute | solution.py:329
  649.4 10.2 %collective-permute-done.63.refs_2_ = bf16[128,1024]{1,0:T(8,128)(2,1)S(1)} collective-permute-done((bf16[128,1024]{1,0:T(8,128)(2,1)S(1)}, bf16[128,1024]{1,0:T(8,128)(2,1)S(1)}, u32[]{:S(2)}, u32[]{:S(2)}) %collective-permute-start.63) | collective-permute-done | bytes 262176 | tf_op jit(solution)/shard_map/ppermute | solution.py:329
  (387 shorter events, 177.5 us)
Async XLA Ops:
  7.2 82.0 %all-gather.5.cloned.1.call-start = ((), (), s32[]{:S(2)}) async-start(), calls=%async_computation.4 | async-start | bytes 4718592 | tf_op jit(solution)/shard_map/all_gather | solution.py:394
  19.1 18.8 %collective-permute-start.1 = (bf16[128,1024]{1,0:T(8,128)(2,1)S(1)}, bf16[128,1024]{1,0:T(8,128)(2,1)S(1)}, u32[]{:S(2)}, u32[]{:S(2)}) collective-permute-start(bf16[128,1024]{1,0:T(8,128)(2,1)S(1)} %pad_maximum_fusion.18), channel_id=1, source_target_pairs={{0,4},{2,6},{4,0},{6,2},{1,5},{3,7},{5,1},{7,3},{8,12},{10,14},{12... | collective-permute-start | bytes 786440 | tf_op jit(solution)/shard_map/ppermute | solution.py:329
  19.4 18.5 %collective-permute-start = (bf16[128,1024]{1,0:T(8,128)(2,1)S(1)}, bf16[128,1024]{1,0:T(8,128)(2,1)S(1)}, u32[]{:S(2)}, u32[]{:S(2)}) collective-permute-start(bf16[128,1024]{1,0:T(8,128)(2,1)S(1)} %pad_maximum_fusion.17), channel_id=1, source_target_pairs={{0,2},{2,4},{4,6},{6,0},{1,3},{3,5},{5,7},{7,1},{8,10},{10,12},{12... | collective-permute-start | bytes 786440 | tf_op jit(solution)/shard_map/ppermute | solution.py:329
  20.5 19.0 %collective-permute-start.2 = (bf16[128,1024]{1,0:T(8,128)(2,1)S(1)}, bf16[128,1024]{1,0:T(8,128)(2,1)S(1)}, u32[]{:S(2)}, u32[]{:S(2)}) collective-permute-start(bf16[128,1024]{1,0:T(8,128)(2,1)S(1)} %pad_maximum_fusion.19), channel_id=1, source_target_pairs={{0,6},{2,0},{4,2},{6,4},{1,7},{3,1},{5,3},{7,5},{8,14},{10,8},{12,... | collective-permute-start | bytes 786440 | tf_op jit(solution)/shard_map/ppermute | solution.py:329
  39.8 195.4 %reduce-scatter.5.cloned.1.call-start = ((), (), s32[]{:S(2)}) async-start(), calls=%async_computation.5 | async-start | bytes 4718592 | tf_op jit(solution)/shard_map/reduce_scatter | solution.py:397
  39.8 23.5 %collective-permute-start.9 = (bf16[512,1024]{1,0:T(8,128)(2,1)S(1)}, bf16[512,1024]{1,0:T(8,128)(2,1)S(1)}, u32[]{:S(2)}, u32[]{:S(2)}) collective-permute-start(bf16[512,1024]{1,0:T(8,128)(2,1)S(1)} %place.8.refs_0_), channel_id=1, source_target_pairs={{0,16},{8,24},{16,0},{24,8},{1,17},{9,25},{17,1},{25,9},{2,18},{10... | collective-permute-start | bytes 3145736 | tf_op jit(solution)/shard_map/ppermute | solution.py:332
  41.4 24.2 %collective-permute-start.8 = (bf16[512,1024]{1,0:T(8,128)(2,1)S(1)}, bf16[512,1024]{1,0:T(8,128)(2,1)S(1)}, u32[]{:S(2)}, u32[]{:S(2)}) collective-permute-start(bf16[512,1024]{1,0:T(8,128)(2,1)S(1)} %place.8.refs_0_), channel_id=1, source_target_pairs={{0,8},{8,0},{16,24},{24,16},{1,9},{9,1},{17,25},{25,17},{2,10},{10... | collective-permute-start | bytes 3145736 | tf_op jit(solution)/shard_map/ppermute | solution.py:332
  91.6 23.6 %collective-permute-start.13 = (bf16[128,1024]{1,0:T(8,128)(2,1)S(1)}, bf16[128,1024]{1,0:T(8,128)(2,1)S(1)}, u32[]{:S(2)}, u32[]{:S(2)}) collective-permute-start(bf16[128,1024]{1,0:T(8,128)(2,1)S(1)} %get-tuple-element.209), channel_id=1, source_target_pairs={{0,4},{2,6},{4,0},{6,2},{1,5},{3,7},{5,1},{7,3},{8,12},{10,14},{12... | collective-permute-start | bytes 786440 | tf_op jit(solution)/shard_map/ppermute | solution.py:329
  92.9 22.3 %collective-permute-start.12 = (bf16[128,1024]{1,0:T(8,128)(2,1)S(1)}, bf16[128,1024]{1,0:T(8,128)(2,1)S(1)}, u32[]{:S(2)}, u32[]{:S(2)}) collective-permute-start(bf16[128,1024]{1,0:T(8,128)(2,1)S(1)} %get-tuple-element.210), channel_id=1, source_target_pairs={{0,2},{2,4},{4,6},{6,0},{1,3},{3,5},{5,7},{7,1},{8,10},{10,12},{12... | collective-permute-start | bytes 786440 | tf_op jit(solution)/shard_map/ppermute | solution.py:329
  115.4 23.4 %collective-permute-start.19 = (bf16[512,1024]{1,0:T(8,128)(2,1)S(1)}, bf16[512,1024]{1,0:T(8,128)(2,1)S(1)}, u32[]{:S(2)}, u32[]{:S(2)}) collective-permute-start(bf16[512,1024]{1,0:T(8,128)(2,1)S(1)} %place.9), channel_id=1, source_target_pairs={{0,16},{8,24},{16,0},{24,8},{1,17},{9,25},{17,1},{25,9},{2,18},{10... | collective-permute-start | bytes 3145736 | tf_op jit(solution)/shard_map/ppermute | solution.py:332
  116.9 24.4 %collective-permute-start.18 = (bf16[512,1024]{1,0:T(8,128)(2,1)S(1)}, bf16[512,1024]{1,0:T(8,128)(2,1)S(1)}, u32[]{:S(2)}, u32[]{:S(2)}) collective-permute-start(bf16[512,1024]{1,0:T(8,128)(2,1)S(1)} %place.9), channel_id=1, source_target_pairs={{0,8},{8,0},{16,24},{24,16},{1,9},{9,1},{17,25},{25,17},{2,10},{10... | collective-permute-start | bytes 3145736 | tf_op jit(solution)/shard_map/ppermute | solution.py:332
  118.5 24.4 %collective-permute-start.17 = (bf16[128,1024]{1,0:T(8,128)(2,1)S(1)}, bf16[128,1024]{1,0:T(8,128)(2,1)S(1)}, u32[]{:S(2)}, u32[]{:S(2)}) collective-permute-start(bf16[128,1024]{1,0:T(8,128)(2,1)S(1)} %get-tuple-element.204), channel_id=1, source_target_pairs={{0,6},{2,0},{4,2},{6,4},{1,7},{3,1},{5,3},{7,5},{8,14},{10,8},{12,... | collective-permute-start | bytes 786440 | tf_op jit(solution)/shard_map/ppermute | solution.py:329
  118.5 25.4 %collective-permute-start.16 = (bf16[128,1024]{1,0:T(8,128)(2,1)S(1)}, bf16[128,1024]{1,0:T(8,128)(2,1)S(1)}, u32[]{:S(2)}, u32[]{:S(2)}) collective-permute-start(bf16[128,1024]{1,0:T(8,128)(2,1)S(1)} %get-tuple-element.205), channel_id=1, source_target_pairs={{0,4},{2,6},{4,0},{6,2},{1,5},{3,7},{5,1},{7,3},{8,12},{10,14},{12... | collective-permute-start | bytes 786440 | tf_op jit(solution)/shard_map/ppermute | solution.py:329
  121.3 22.7 %collective-permute-start.15 = (bf16[128,1024]{1,0:T(8,128)(2,1)S(1)}, bf16[128,1024]{1,0:T(8,128)(2,1)S(1)}, u32[]{:S(2)}, u32[]{:S(2)}) collective-permute-start(bf16[128,1024]{1,0:T(8,128)(2,1)S(1)} %get-tuple-element.206), channel_id=1, source_target_pairs={{0,2},{2,4},{4,6},{6,0},{1,3},{3,5},{5,7},{7,1},{8,10},{10,12},{12... | collective-permute-start | bytes 786440 | tf_op jit(solution)/shard_map/ppermute | solution.py:329
  161.6 122.6 %all-gather.9.cloned.1.call-start = ((), (), s32[]{:S(2)}) async-start(), calls=%async_computation.7 | async-start | bytes 4718592 | tf_op jit(solution)/shard_map/all_gather | solution.py:394
  161.6 24.2 %collective-permute-start.26 = (bf16[512,1024]{1,0:T(8,128)(2,1)}, bf16[512,1024]{1,0:T(8,128)(2,1)S(1)}, u32[]{:S(2)}, u32[]{:S(2)}) collective-permute-start(bf16[512,1024]{1,0:T(8,128)(2,1)} %copy-done.10), channel_id=1, source_target_pairs={{0,16},{8,24},{16,0},{24,8},{1,17},{9,25},{17,1},{25,9},{2,18},{10... | collective-permute-start | bytes 3145736 | tf_op jit(solution)/shard_map/ppermute | solution.py:332
  162.2 26.0 %collective-permute-start.25 = (bf16[512,1024]{1,0:T(8,128)(2,1)}, bf16[512,1024]{1,0:T(8,128)(2,1)S(1)}, u32[]{:S(2)}, u32[]{:S(2)}) collective-permute-start(bf16[512,1024]{1,0:T(8,128)(2,1)} %copy-done.10), channel_id=1, source_target_pairs={{0,8},{8,0},{16,24},{24,16},{1,9},{9,1},{17,25},{25,17},{2,10},{10... | collective-permute-start | bytes 3145736 | tf_op jit(solution)/shard_map/ppermute | solution.py:332
  187.6 45.3 %collective-permute-start.28 = (bf16[256,1024]{1,0:T(8,128)(2,1)}, bf16[256,1024]{1,0:T(8,128)(2,1)}, u32[]{:S(2)}, u32[]{:S(2)}) collective-permute-start(bf16[256,1024]{1,0:T(8,128)(2,1)} %slice.207), channel_id=1, source_target_pairs={{0,8},{8,0},{16,24},{24,16},{1,9},{9,1},{17,25},{25,17},{2,10},{10... | collective-permute-start | bytes 1572872 | tf_op jit(solution)/shard_map/ppermute | solution.py:332
  190.1 42.9 %collective-permute-start.27 = (bf16[256,1024]{1,0:T(8,128)(2,1)}, bf16[256,1024]{1,0:T(8,128)(2,1)}, u32[]{:S(2)}, u32[]{:S(2)}) collective-permute-start(bf16[256,1024]{1,0:T(8,128)(2,1)} %slice.206), channel_id=1, source_target_pairs={{0,16},{8,24},{16,0},{24,8},{1,17},{9,25},{17,1},{25,9},{2,18},{10... | collective-permute-start | bytes 1572872 | tf_op jit(solution)/shard_map/ppermute | solution.py:332
  194.2 37.5 %collective-permute-start.23 = (bf16[128,1024]{1,0:T(8,128)(2,1)S(1)}, bf16[128,1024]{1,0:T(8,128)(2,1)S(1)}, u32[]{:S(2)}, u32[]{:S(2)}) collective-permute-start(bf16[128,1024]{1,0:T(8,128)(2,1)S(1)} %get-tuple-element.201), channel_id=1, source_target_pairs={{0,4},{2,6},{4,0},{6,2},{1,5},{3,7},{5,1},{7,3},{8,12},{10,14},{12... | collective-permute-start | bytes 786440 | tf_op jit(solution)/shard_map/ppermute | solution.py:329
  197.1 34.6 %collective-permute-start.22 = (bf16[128,1024]{1,0:T(8,128)(2,1)S(1)}, bf16[128,1024]{1,0:T(8,128)(2,1)S(1)}, u32[]{:S(2)}, u32[]{:S(2)}) collective-permute-start(bf16[128,1024]{1,0:T(8,128)(2,1)S(1)} %get-tuple-element.202), channel_id=1, source_target_pairs={{0,2},{2,4},{4,6},{6,0},{1,3},{3,5},{5,7},{7,1},{8,10},{10,12},{12... | collective-permute-start | bytes 786440 | tf_op jit(solution)/shard_map/ppermute | solution.py:329
  238.6 93.5 %all-gather.7.cloned.1.call-start = ((), (), s32[]{:S(2)}) async-start(), calls=%async_computation.6 | async-start | bytes 4718592 | tf_op jit(solution)/shard_map/all_gather | solution.py:394
  241.8 141.2 %reduce-scatter.7.cloned.1.call-start = ((), (), s32[]{:S(2)}) async-start(), calls=%async_computation.8 | async-start | bytes 4718592 | tf_op jit(solution)/shard_map/reduce_scatter | solution.py:397
  242.2 22.9 %collective-permute-start.30 = (bf16[512,1024]{1,0:T(8,128)(2,1)}, bf16[512,1024]{1,0:T(8,128)(2,1)S(1)}, u32[]{:S(2)}, u32[]{:S(2)}) collective-permute-start(bf16[512,1024]{1,0:T(8,128)(2,1)} %copy-done.13), channel_id=1, source_target_pairs={{0,16},{8,24},{16,0},{24,8},{1,17},{9,25},{17,1},{25,9},{2,18},{10... | collective-permute-start | bytes 3145736 | tf_op jit(solution)/shard_map/ppermute | solution.py:332
  243.5 24.0 %collective-permute-start.29 = (bf16[512,1024]{1,0:T(8,128)(2,1)}, bf16[512,1024]{1,0:T(8,128)(2,1)S(1)}, u32[]{:S(2)}, u32[]{:S(2)}) collective-permute-start(bf16[512,1024]{1,0:T(8,128)(2,1)} %copy-done.13), channel_id=1, source_target_pairs={{0,8},{8,0},{16,24},{24,16},{1,9},{9,1},{17,25},{25,17},{2,10},{10... | collective-permute-start | bytes 3145736 | tf_op jit(solution)/shard_map/ppermute | solution.py:332
  308.9 131.7 %reduce-scatter.9.cloned.1.call-start = ((), (), s32[]{:S(2)}) async-start(), calls=%async_computation.9 | async-start | bytes 4718592 | tf_op jit(solution)/shard_map/reduce_scatter | solution.py:397
  383.0 144.9 %all-gather.11.cloned.1.call-start = ((), (), s32[]{:S(2)}) async-start(), calls=%async_computation.10 | async-start | bytes 4718592 | tf_op jit(solution)/shard_map/all_gather | solution.py:394
  391.0 26.2 %collective-permute-start.34 = (bf16[512,1024]{1,0:T(8,128)(2,1)S(1)}, bf16[512,1024]{1,0:T(8,128)(2,1)S(1)}, u32[]{:S(2)}, u32[]{:S(2)}) collective-permute-start(bf16[512,1024]{1,0:T(8,128)(2,1)S(1)} %get-tuple-element.159), channel_id=1, source_target_pairs={{0,8},{8,0},{16,24},{24,16},{1,9},{9,1},{17,25},{25,17},{2,10},{10... | collective-permute-start | bytes 3145736 | tf_op jit(solution)/shard_map/ppermute | solution.py:332
  392.6 44.8 %collective-permute-start.36 = (bf16[512,1024]{1,0:T(8,128)(2,1)S(1)}, bf16[512,1024]{1,0:T(8,128)(2,1)S(1)}, u32[]{:S(2)}, u32[]{:S(2)}) collective-permute-start(bf16[512,1024]{1,0:T(8,128)(2,1)S(1)} %get-tuple-element.160), channel_id=1, source_target_pairs={{0,24},{8,16},{16,8},{24,0},{1,25},{9,17},{17,9},{25,1},{2,26},{10... | collective-permute-start | bytes 3145736 | tf_op jit(solution)/shard_map/ppermute | solution.py:332
  394.0 44.7 %collective-permute-start.35 = (bf16[512,1024]{1,0:T(8,128)(2,1)S(1)}, bf16[512,1024]{1,0:T(8,128)(2,1)S(1)}, u32[]{:S(2)}, u32[]{:S(2)}) collective-permute-start(bf16[512,1024]{1,0:T(8,128)(2,1)S(1)} %get-tuple-element.161), channel_id=1, source_target_pairs={{0,16},{8,24},{16,0},{24,8},{1,17},{9,25},{17,1},{25,9},{2,18},{10... | collective-permute-start | bytes 3145736 | tf_op jit(solution)/shard_map/ppermute | solution.py:332
  446.1 216.3 %reduce-scatter.11.cloned.1.call-start = ((), (), s32[]{:S(2)}) async-start(), calls=%async_computation.11 | async-start | bytes 4718592 | tf_op jit(solution)/shard_map/reduce_scatter | solution.py:397
  450.0 26.4 %collective-permute-start.37 = (bf16[512,1024]{1,0:T(8,128)(2,1)}, bf16[512,1024]{1,0:T(8,128)(2,1)}, u32[]{:S(2)}, u32[]{:S(2)}) collective-permute-start(bf16[512,1024]{1,0:T(8,128)(2,1)} %get-tuple-element.156), channel_id=1, source_target_pairs={{0,8},{8,0},{16,24},{24,16},{1,9},{9,1},{17,25},{25,17},{2,10},{10... | collective-permute-start | bytes 3145736 | tf_op jit(solution)/shard_map/ppermute | solution.py:332
  451.4 41.8 %collective-permute-start.39 = (bf16[512,1024]{1,0:T(8,128)(2,1)}, bf16[512,1024]{1,0:T(8,128)(2,1)}, u32[]{:S(2)}, u32[]{:S(2)}) collective-permute-start(bf16[512,1024]{1,0:T(8,128)(2,1)} %get-tuple-element.157), channel_id=1, source_target_pairs={{0,24},{8,16},{16,8},{24,0},{1,25},{9,17},{17,9},{25,1},{2,26},{10... | collective-permute-start | bytes 3145736 | tf_op jit(solution)/shard_map/ppermute | solution.py:332
  452.0 42.6 %collective-permute-start.38 = (bf16[512,1024]{1,0:T(8,128)(2,1)}, bf16[512,1024]{1,0:T(8,128)(2,1)}, u32[]{:S(2)}, u32[]{:S(2)}) collective-permute-start(bf16[512,1024]{1,0:T(8,128)(2,1)} %get-tuple-element.158), channel_id=1, source_target_pairs={{0,16},{8,24},{16,0},{24,8},{1,17},{9,25},{17,1},{25,9},{2,18},{10... | collective-permute-start | bytes 3145736 | tf_op jit(solution)/shard_map/ppermute | solution.py:332
  455.2 56.0 %collective-permute-start.42 = (bf16[128,1024]{1,0:T(8,128)(2,1)S(1)}, bf16[128,1024]{1,0:T(8,128)(2,1)S(1)}, u32[]{:S(2)}, u32[]{:S(2)}) collective-permute-start(bf16[128,1024]{1,0:T(8,128)(2,1)S(1)} %get-tuple-element.190), channel_id=1, source_target_pairs={{0,6},{2,0},{4,2},{6,4},{1,7},{3,1},{5,3},{7,5},{8,14},{10,8},{12,... | collective-permute-start | bytes 786440 | tf_op jit(solution)/shard_map/ppermute | solution.py:329
  500.5 47.3 %collective-permute-start.43 = (bf16[512,1024]{1,0:T(8,128)(2,1)}, bf16[512,1024]{1,0:T(8,128)(2,1)}, u32[]{:S(2)}, u32[]{:S(2)}) collective-permute-start(bf16[512,1024]{1,0:T(8,128)(2,1)} %get-tuple-element.153), channel_id=1, source_target_pairs={{0,8},{8,0},{16,24},{24,16},{1,9},{9,1},{17,25},{25,17},{2,10},{10... | collective-permute-start | bytes 3145736 | tf_op jit(solution)/shard_map/ppermute | solution.py:332
  501.9 48.2 %collective-permute-start.45 = (bf16[512,1024]{1,0:T(8,128)(2,1)}, bf16[512,1024]{1,0:T(8,128)(2,1)}, u32[]{:S(2)}, u32[]{:S(2)}) collective-permute-start(bf16[512,1024]{1,0:T(8,128)(2,1)} %get-tuple-element.154), channel_id=1, source_target_pairs={{0,24},{8,16},{16,8},{24,0},{1,25},{9,17},{17,9},{25,1},{2,26},{10... | collective-permute-start | bytes 3145736 | tf_op jit(solution)/shard_map/ppermute | solution.py:332
  503.4 46.8 %collective-permute-start.44 = (bf16[512,1024]{1,0:T(8,128)(2,1)}, bf16[512,1024]{1,0:T(8,128)(2,1)}, u32[]{:S(2)}, u32[]{:S(2)}) collective-permute-start(bf16[512,1024]{1,0:T(8,128)(2,1)} %get-tuple-element.155), channel_id=1, source_target_pairs={{0,16},{8,24},{16,0},{24,8},{1,17},{9,25},{17,1},{25,9},{2,18},{10... | collective-permute-start | bytes 3145736 | tf_op jit(solution)/shard_map/ppermute | solution.py:332
  504.0 21.9 %collective-permute-start.41 = (bf16[128,1024]{1,0:T(8,128)(2,1)S(1)}, bf16[128,1024]{1,0:T(8,128)(2,1)S(1)}, u32[]{:S(2)}, u32[]{:S(2)}) collective-permute-start(bf16[128,1024]{1,0:T(8,128)(2,1)S(1)} %get-tuple-element.191), channel_id=1, source_target_pairs={{0,4},{2,6},{4,0},{6,2},{1,5},{3,7},{5,1},{7,3},{8,12},{10,14},{12... | collective-permute-start | bytes 786440 | tf_op jit(solution)/shard_map/ppermute | solution.py:329
  529.2 24.0 %collective-permute-start.48 = (bf16[128,1024]{1,0:T(8,128)(2,1)S(1)}, bf16[128,1024]{1,0:T(8,128)(2,1)S(1)}, u32[]{:S(2)}, u32[]{:S(2)}) collective-permute-start(bf16[128,1024]{1,0:T(8,128)(2,1)S(1)} %get-tuple-element.186), channel_id=1, source_target_pairs={{0,6},{2,0},{4,2},{6,4},{1,7},{3,1},{5,3},{7,5},{8,14},{10,8},{12,... | collective-permute-start | bytes 786440 | tf_op jit(solution)/shard_map/ppermute | solution.py:329
  529.3 24.0 %collective-permute-start.47 = (bf16[128,1024]{1,0:T(8,128)(2,1)S(1)}, bf16[128,1024]{1,0:T(8,128)(2,1)S(1)}, u32[]{:S(2)}, u32[]{:S(2)}) collective-permute-start(bf16[128,1024]{1,0:T(8,128)(2,1)S(1)} %get-tuple-element.187), channel_id=1, source_target_pairs={{0,4},{2,6},{4,0},{6,2},{1,5},{3,7},{5,1},{7,3},{8,12},{10,14},{12... | collective-permute-start | bytes 786440 | tf_op jit(solution)/shard_map/ppermute | solution.py:329
  571.7 49.6 %collective-permute-start.50 = (bf16[512,1024]{1,0:T(8,128)(2,1)S(1)}, bf16[512,1024]{1,0:T(8,128)(2,1)S(1)}, u32[]{:S(2)}, u32[]{:S(2)}) collective-permute-start(bf16[512,1024]{1,0:T(8,128)(2,1)S(1)} %pad_maximum_fusion.8), channel_id=1, source_target_pairs={{0,8},{8,0},{16,24},{24,16},{1,9},{9,1},{17,25},{25,17},{2,10},{10... | collective-permute-start | bytes 3145736 | tf_op jit(solution)/shard_map/ppermute | solution.py:332
  573.6 47.7 %collective-permute-start.54 = (bf16[512,1024]{1,0:T(8,128)(2,1)}, bf16[512,1024]{1,0:T(8,128)(2,1)S(1)}, u32[]{:S(2)}, u32[]{:S(2)}) collective-permute-start(bf16[512,1024]{1,0:T(8,128)(2,1)} %pad_maximum_fusion.9), channel_id=1, source_target_pairs={{0,16},{8,24},{16,0},{24,8},{1,17},{9,25},{17,1},{25,9},{2,18},{10... | collective-permute-start | bytes 3145736 | tf_op jit(solution)/shard_map/ppermute | solution.py:332
  576.3 45.1 %collective-permute-start.55 = (bf16[512,1024]{1,0:T(8,128)(2,1)}, bf16[512,1024]{1,0:T(8,128)(2,1)S(1)}, u32[]{:S(2)}, u32[]{:S(2)}) collective-permute-start(bf16[512,1024]{1,0:T(8,128)(2,1)} %pad_maximum_fusion.10), channel_id=1, source_target_pairs={{0,24},{8,16},{16,8},{24,0},{1,25},{9,17},{17,9},{25,1},{2,26},{10... | collective-permute-start | bytes 3145736 | tf_op jit(solution)/shard_map/ppermute | solution.py:332
  578.6 40.9 %collective-permute-start.52 = (bf16[128,1024]{1,0:T(8,128)(2,1)S(1)}, bf16[128,1024]{1,0:T(8,128)(2,1)S(1)}, u32[]{:S(2)}, u32[]{:S(2)}) collective-permute-start(bf16[128,1024]{1,0:T(8,128)(2,1)S(1)} %get-tuple-element.177), channel_id=1, source_target_pairs={{0,4},{2,6},{4,0},{6,2},{1,5},{3,7},{5,1},{7,3},{8,12},{10,14},{12... | collective-permute-start | bytes 786440 | tf_op jit(solution)/shard_map/ppermute | solution.py:329
  592.4 27.1 %collective-permute-start.51 = (bf16[128,1024]{1,0:T(8,128)(2,1)S(1)}, bf16[128,1024]{1,0:T(8,128)(2,1)S(1)}, u32[]{:S(2)}, u32[]{:S(2)}) collective-permute-start(bf16[128,1024]{1,0:T(8,128)(2,1)S(1)} %get-tuple-element.178), channel_id=1, source_target_pairs={{0,2},{2,4},{4,6},{6,0},{1,3},{3,5},{5,7},{7,1},{8,10},{10,12},{12... | collective-permute-start | bytes 786440 | tf_op jit(solution)/shard_map/ppermute | solution.py:329
  641.8 17.8 %collective-permute-start.63 = (bf16[128,1024]{1,0:T(8,128)(2,1)S(1)}, bf16[128,1024]{1,0:T(8,128)(2,1)S(1)}, u32[]{:S(2)}, u32[]{:S(2)}) collective-permute-start(bf16[128,1024]{1,0:T(8,128)(2,1)S(1)} %get-tuple-element.169), channel_id=1, source_target_pairs={{0,4},{2,6},{4,0},{6,2},{1,5},{3,7},{5,1},{7,3},{8,12},{10,14},{12... | collective-permute-start | bytes 786440 | tf_op jit(solution)/shard_map/ppermute | solution.py:329
  643.4 18.2 %collective-permute-start.60 = (f32[1,260]{1,0:T(1,128)S(1)}, f32[1,260]{1,0:T(1,128)S(1)}, u32[]{:S(2)}, u32[]{:S(2)}) collective-permute-start(f32[1,260]{1,0:T(1,128)S(1)} %get-tuple-element.250), channel_id=1, source_target_pairs={{0,2},{2,4},{4,6},{6,0},{1,3},{3,5},{5,7},{7,1},{8,10},{10,12},{12... | collective-permute-start | bytes 3128 | tf_op jit(solution)/shard_map/ppermute | solution.py:329
  (92 other events, 1039.3 us)
Sparse Core Ops, SparseCore 0:
  39.9 49.2 all-gather.4
  161.7 61.0 reduce-scatter.4
  238.7 45.3 all-gather.8
  286.2 45.8 all-gather.6
  334.2 48.7 reduce-scatter.6
  385.2 48.1 reduce-scatter.8
  446.2 52.2 all-gather.10
  563.8 69.8 reduce-scatter.10

commit v6 on v4

--- a/solution.py
+++ b/solution.py
@@ -450,7 +450,6 @@
     silu_gate = gate_act * sig_gate
     hidden = (silu_gate * up_act).astype(bf16)
     mlp_partial = dot_rt(hidden, down_full).astype(bf16)
-    mlp_sum = scatter_tokens(mlp_partial)
     grad_hidden = dot(after(cot_all, mlp_partial), down_full)
     silu_slope = sig_gate * (1.0 + gate_act * (1.0 - sig_gate))
     grad_gate = (grad_hidden * up_act * silu_slope).astype(bf16)
@@ -458,7 +457,6 @@
     back_two = (dot_rt(grad_gate, gate_full) + dot_rt(grad_up, up_full)).astype(bf16)
     hidden_late, gate_late, up_late = (after(g, back_two) for g in (hidden, grad_gate, grad_up))
     grad_w_down = dot_lt(cot_all, hidden_late).astype(bf16)
-    back_two, mlp_sum = lax.optimization_barrier((back_two, mlp_sum))
     grad_normed_two = scatter_tokens(back_two)
     grad_w_gate = dot_lt(normed_two, gate_late).astype(bf16)
     grad_w_up = dot_lt(normed_two, up_late).astype(bf16)
@@ -474,13 +472,15 @@
     gate_sum = scatter_plane(after(grad_w_gate, down_sum))
     (down_out,) = swap_rows(down_sum, ("turned",))
     grad_low = after(grad_low, gate_sum, down_out)
-    block_out_mine = (resid + mlp_sum.astype(f32)).astype(bf16)
+    mlp_sum = scatter_tokens(after(mlp_partial, grad_low))
 
     grad_attended = dot(grad_low, out_full).astype(bf16)
     grad_proj = attend_back(order_row, qkv, grad_attended, log_total, cosine, sine)
     up_sum = scatter_plane(after(grad_w_up, gate_sum), late=(grad_proj,))
     (gate_out,) = swap_rows(after(gate_sum, grad_low), ("side",), late=(grad_proj,))
     back_one = dot_rt(after(grad_proj, up_sum, gate_out), qkv_full).astype(bf16)
+    back_one, mlp_sum = lax.optimization_barrier((back_one, mlp_sum))
+    block_out_mine = (resid + mlp_sum.astype(f32)).astype(bf16)
     grad_normed_one = scatter_tokens(back_one)
     proj_late, attn_late, back_late = (after(g, back_one) for g in (grad_proj, attn_low, back_one))
     grad_w_qkv = dot_lt(normed_one, proj_late).astype(bf16)

time: 681 us -> 686 us (level)
    ppermute x30, waiting for transfers between devices: 104 us -> 128 us  [along(): lax.ppermute(tensor, 'ctx', [(i, (i + shift) % n_ctx) for i in range(n_ct...]
    reduce_scatter x4, waiting for transfers between devices: 20.9 us -> 6.45 us  [scatter_tokens(): lax.psum_scatter(partial.astype(bf16), ('ctx', 'tp'), scatter_dimension=0...]
    ppermute x32, waiting for transfers between devices: 181 us -> 174 us  [across(): return lax.ppermute(tensor, 'fsdp', [(i, i ^ mask) for i in range(n_fsdp)])]
  transfers between devices with their start and end apart: 73 -> 73, of which waited for: 33 -> 34; matrix products, arithmetic and copies ran while one was open for 22% -> 18% of each run, Pallas kernels for 6% -> 6%
where the time goes in v6:
time: 686 us; the launch traced here: 679 us
  waiting for transfers between devices  345 us (50%)
  starting transfers between devices  96.2 us (14%)
  matrix products  94.7 us (14%)
  other arithmetic  46.9 us (7%)
  local copies, waits for them, and re-layouts  40.7 us (6%)
  Pallas kernels  39.8 us (6%)
  between operations  15.8 us (2%)
    ppermute x32, waiting for transfers between devices, across(): return lax.ppermute(tensor, 'fsdp', [(i, i ^ mask) for i in range(n_fsdp)])  174 us
    ppermute x30, waiting for transfers between devices, along(): lax.ppermute(tensor, 'ctx', [(i, (i + shift) % n_ctx) for i in range(n_ct...  128 us
    ppermute x30, starting transfers between devices, along(): lax.ppermute(tensor, 'ctx', [(i, (i + shift) % n_ctx) for i in range(n_ct...  55.5 us
    ppermute x32, starting transfers between devices, across(): return lax.ppermute(tensor, 'fsdp', [(i, i ^ mask) for i in range(n_fsdp)])  39.9 us
    dot_general x5, matrix products, dot_rt(): lax.dot_general(left, right, (((1,), (1,)), ((), ())), preferred_element_...  37.9 us
    all_gather x4, waiting for transfers between devices, gather_tokens(): return lax.all_gather(own, ('ctx', 'tp'), axis=0, tiled=True)  36.4 us
    dot_general x4, matrix products, dot(): return jnp.dot(left, right, preferred_element_type=f32)  29.1 us
    dot_general x5, matrix products, dot_lt(): lax.dot_general(left, right, (((0,), (0,)), ((), ())), preferred_element_...  27.7 us
  transfers between devices with their start and end apart: 73, of which 34 were waited for; matrix products, arithmetic and copies ran while one was open for 18% of the time, Pallas kernels for 6%

profile of v6, /device:TPU:0, one launch (start us, length us, event | category | flops | bytes accessed | tf_op | source)
XLA Modules:
  0.0 679.1 jit_solution(14457299676652396012)
XLA Ops:
  8.0 4.1 collective-permute-start.4
  20.5 3.3 collective-permute-start.2
  31.2 6.7 collective-permute-done.1.refs_2_
  42.9 20.4 %collective-permute-done.9.refs_2_ = bf16[512,1024]{1,0:T(8,128)(2,1)S(1)} collective-permute-done((bf16[512,1024]{1,0:T(8,128)(2,1)S(1)}, bf16[512,1024]{1,0:T(8,128)(2,1)S(1)}, u32[]{:S(2)}, u32[]{:S(2)}) %collective-permute-start.9) | collective-permute-done | bytes 1048608 | tf_op jit(solution)/shard_map/ppermute | solution.py:332
  72.8 3.1 collective-permute-done.11
  75.9 2.9 collective-permute-done.10
  82.4 6.8 all-gather.5.cloned.1.call-done.x_ref
  97.5 8.3 %project.1 = (bf16[1024,2048]{1,0:T(8,128)(2,1)}, bf16[1024,768]{1,0:T(8,128)(2,1)}) custom-call(bf16[1024,2048]{1,0:T(8,128)(2,1)} %all-gather.5.cloned.1.call-done.x_ref, f32[1,2048]{1,0:T(1,128)S(1)} %get-tuple-element.239.gain_ref, f32[1024,128]{1,0:T(8,128)S(1)} %copy-done.4, f32[1024,128]{1,0:T(8,128)S(1)} %copy-done.6, ...), custom_call_target="tpu_custom_call" | custom-call | flops 536870912 | bytes 12582912 | tf_op jit(solution)/shard_map/project/pallas_call | solution.py:121
  105.8 9.4 %collective-permute-done.13.refs_2_ = bf16[128,1024]{1,0:T(8,128)(2,1)S(1)} collective-permute-done((bf16[128,1024]{1,0:T(8,128)(2,1)S(1)}, bf16[128,1024]{1,0:T(8,128)(2,1)S(1)}, u32[]{:S(2)}, u32[]{:S(2)}) %collective-permute-start.13) | collective-permute-done | bytes 262176 | tf_op jit(solution)/shard_map/ppermute | solution.py:329
  123.4 15.4 %collective-permute-done.19 = bf16[512,1024]{1,0:T(8,128)(2,1)S(1)} collective-permute-done((bf16[512,1024]{1,0:T(8,128)(2,1)S(1)}, bf16[512,1024]{1,0:T(8,128)(2,1)S(1)}, u32[]{:S(2)}, u32[]{:S(2)}) %collective-permute-start.19) | collective-permute-done | bytes 1048608 | tf_op jit(solution)/shard_map/ppermute | solution.py:332
  144.0 9.7 %attend.1 = (bf16[1024,256]{1,0:T(8,128)(2,1)S(1)}, f32[2,1024,128]{2,1,0:T(8,128)S(1)}, f32[2,8,128]{2,1,0:T(8,128)S(1)}) custom-call(s32[8]{0:T(128)S(1)} %bitcast.95, bf16[1024,768]{1,0:T(8,128)(2,1)S(1)} %copy-done, bf16[1024,768]{1,0:T(8,128)(2,1)S(1)} %copy-done, bf16[1024,768]{1,0:T(8,128)(2,1)S(1)} %copy-done), custom_call_target="tpu_custom_call" | custom-call | flops 536870912 | bytes 2097152 | tf_op jit(solution)/shard_map/attend/pallas_call | solution.py:194
  157.0 4.6 convolution_convert_fusion
  162.8 23.0 %collective-permute-done.26 = bf16[512,1024]{1,0:T(8,128)(2,1)S(1)} collective-permute-done((bf16[512,1024]{1,0:T(8,128)(2,1)}, bf16[512,1024]{1,0:T(8,128)(2,1)S(1)}, u32[]{:S(2)}, u32[]{:S(2)}) %collective-permute-start.26) | collective-permute-done | bytes 1048608 | tf_op jit(solution)/shard_map/ppermute | solution.py:332
  199.1 9.9 %collective-permute-done.24.refs_3_ = bf16[128,1024]{1,0:T(8,128)(2,1)S(1)} collective-permute-done((bf16[128,1024]{1,0:T(8,128)(2,1)S(1)}, bf16[128,1024]{1,0:T(8,128)(2,1)S(1)}, u32[]{:S(2)}, u32[]{:S(2)}) %collective-permute-start.24) | collective-permute-done | bytes 262176 | tf_op jit(solution)/shard_map/ppermute | solution.py:329
  209.0 22.8 %collective-permute-done.23.refs_2_ = bf16[128,1024]{1,0:T(8,128)(2,1)S(1)} collective-permute-done((bf16[128,1024]{1,0:T(8,128)(2,1)S(1)}, bf16[128,1024]{1,0:T(8,128)(2,1)S(1)}, u32[]{:S(2)}, u32[]{:S(2)}) %collective-permute-start.23) | collective-permute-done | bytes 262176 | tf_op jit(solution)/shard_map/ppermute | solution.py:329
  244.6 20.2 %collective-permute-done.30 = bf16[512,1024]{1,0:T(8,128)(2,1)S(1)} collective-permute-done((bf16[512,1024]{1,0:T(8,128)(2,1)}, bf16[512,1024]{1,0:T(8,128)(2,1)S(1)}, u32[]{:S(2)}, u32[]{:S(2)}) %collective-permute-start.30) | collective-permute-done | bytes 1048608 | tf_op jit(solution)/shard_map/ppermute | solution.py:332
  267.8 9.1 %collective-permute-done.32 = bf16[256,1024]{1,0:T(8,128)(2,1)S(1)} collective-permute-done((bf16[256,1024]{1,0:T(8,128)(2,1)S(1)}, bf16[256,1024]{1,0:T(8,128)(2,1)S(1)}, u32[]{:S(2)}, u32[]{:S(2)}) %collective-permute-start.32) | collective-permute-done | bytes 524320 | tf_op jit(solution)/shard_map/ppermute | solution.py:332
  278.0 6.2 all-gather.9.cloned.1.call-done
  284.2 7.9 %fusion.40 = f32[1024,1024]{1,0:T(8,128)S(1)} fusion(bf16[1024,2048]{1,0:T(8,128)(2,1)} %all-gather.9.cloned.1.call-done, bf16[2048,1024]{1,0:T(8,128)(2,1)} %copy-done.35), kind=kOutput, calls=%fused_computation.204 | convolution fusion | flops 4294967296 | bytes 12582912 | tf_op jit(solution)/shard_map/dot_general | solution.py:35
  292.2 6.6 multiply_convert_fusion.2
  300.1 9.1 %convolution_convert_fusion.5 = bf16[1024,2048]{1,0:T(8,128)(2,1)} fusion(bf16[1024,1024]{1,0:T(8,128)(2,1)S(1)} %get-tuple-element.106, bf16[512,1024]{1,0:T(8,128)(2,1)S(1)} %copy-done.33, bf16[512,1024]{1,0:T(8,128)(2,1)S(1)} %copy-done.44, bf16[512,1024]{1,0:T(8,128)(2,1)S(1)} %copy-done.46, bf16[512,1024]{1,0:T(8,128)(2,1)S(1)} %copy-done.14), kind=kOutput, calls=%fused_computation.19 | convolution fusion | flops 4313841664 | bytes 10485760 | tf_op jit(solution)/shard_map/dot_general | solution.py:43
  309.2 22.9 %all-gather.7.cloned.1.call-done = bf16[1024,2048]{1,0:T(8,128)(2,1)} async-done(((bf16[128,2048]{1,0:T(8,128)(2,1)}), bf16[1024,2048]{1,0:T(8,128)(2,1)}) %all-gather.7.cloned.1.call-update) | async-done | bytes 4194320 | tf_op jit(solution)/shard_map/all_gather | solution.py:391
  332.1 11.2 %multiply_convert_fusion = (bf16[1024,1024]{1,0:T(8,128)(2,1)}, bf16[1024,1024]{1,0:T(8,128)(2,1)S(1)}) fusion(f32[1024,1024]{1,0:T(8,128)} %copy-done.59, f32[1024,1024]{1,0:T(8,128)} %get-tuple-element.254, bf16[1024,2048]{1,0:T(8,128)(2,1)} %all-gather.7.cloned.1.call-done, bf16[512,1024]{1,0:T(8,128)(2,1)} %pad_maximum_fusion.6, ...), kind=kOutput, calls=%fused_computation.9 | convolution fusion | flops 4325376000 | bytes 20971520 | tf_op jit(solution)/shard_map/dot_general | solution.py:35
  343.4 6.8 %fusion.41 = f32[1024,2048]{1,0:T(8,128)} fusion(bf16[1024,1024]{1,0:T(8,128)(2,1)S(1)} %get-tuple-element.107, bf16[2048,1024]{1,0:T(8,128)(2,1)S(1)} %copy-done.36), kind=kOutput, calls=%fused_computation.205 | convolution fusion | flops 4294967296 | bytes 14680064 | tf_op jit(solution)/shard_map/dot_general | solution.py:43
  350.2 12.3 %add_convert_fusion = bf16[1024,2048]{1,0:T(8,128)(2,1)} fusion(f32[1024,2048]{1,0:T(8,128)} %fusion.41, bf16[1024,1024]{1,0:T(8,128)(2,1)} %get-tuple-element.108, bf16[512,1024]{1,0:T(8,128)(2,1)S(1)} %copy-done.32, bf16[512,1024]{1,0:T(8,128)(2,1)S(1)} %copy-done.39, bf16[512,1024]{1,0:T(8,128)(2,1)S(1)} %copy-done.42, bf16[512,1024]{1,0:T(8,128)(2,1)S(1)} %copy-done.12), kind=kOutput, calls=%fused_computation.5 | convolution fusion | flops 4315938816 | bytes 18874368 | tf_op jit(solution)/shard_map/dot_general | solution.py:43
  362.6 7.4 %convolution_convert_fusion.4 = bf16[2048,1024]{1,0:T(8,128)(2,1)S(1)} fusion(bf16[1024,2048]{1,0:T(8,128)(2,1)} %all-gather.7.cloned.1.call-done, bf16[1024,1024]{1,0:T(8,128)(2,1)} %copy-done.63), kind=kOutput, calls=%fused_computation.18 | convolution fusion | flops 4297064448 | bytes 10485760 | tf_op jit(solution)/shard_map/dot_general | solution.py:39
  373.9 6.4 convolution_convert_fusion.3
  380.3 6.3 convolution_convert_fusion.2
  386.6 9.8 %collective-permute-done.33 = bf16[512,1024]{1,0:T(8,128)(2,1)S(1)} collective-permute-done((bf16[512,1024]{1,0:T(8,128)(2,1)S(1)}, bf16[512,1024]{1,0:T(8,128)(2,1)S(1)}, u32[]{:S(2)}, u32[]{:S(2)}) %collective-permute-start.33) | collective-permute-done | bytes 1048608 | tf_op jit(solution)/shard_map/ppermute | solution.py:332
  396.4 22.8 %collective-permute-done.35 = bf16[512,1024]{1,0:T(8,128)(2,1)S(1)} collective-permute-done((bf16[512,1024]{1,0:T(8,128)(2,1)S(1)}, bf16[512,1024]{1,0:T(8,128)(2,1)S(1)}, u32[]{:S(2)}, u32[]{:S(2)}) %collective-permute-start.35) | collective-permute-done | bytes 1048608 | tf_op jit(solution)/shard_map/ppermute | solution.py:332
  428.1 3.6 fusion.35
  438.0 17.6 %collective-permute-done.41.refs_3_ = bf16[128,1024]{1,0:T(8,128)(2,1)S(1)} collective-permute-done((bf16[128,1024]{1,0:T(8,128)(2,1)S(1)}, bf16[128,1024]{1,0:T(8,128)(2,1)S(1)}, u32[]{:S(2)}, u32[]{:S(2)}) %collective-permute-start.41) | collective-permute-done | bytes 262176 | tf_op jit(solution)/shard_map/ppermute | solution.py:329
  455.6 9.7 %collective-permute-start.39 = (bf16[128,1024]{1,0:T(8,128)(2,1)S(1)}, bf16[128,1024]{1,0:T(8,128)(2,1)S(1)}, u32[]{:S(2)}, u32[]{:S(2)}) collective-permute-start(bf16[128,1024]{1,0:T(8,128)(2,1)S(1)} %get-tuple-element.194), channel_id=1, source_target_pairs={{0,2},{2,4},{4,6},{6,0},{1,3},{3,5},{5,7},{7,1},{8,10},{10,12},{12... | collective-permute-start | bytes 786440 | tf_op jit(solution)/shard_map/ppermute | solution.py:329
  465.3 22.4 %collective-permute-done.40.refs_2_ = bf16[128,1024]{1,0:T(8,128)(2,1)S(1)} collective-permute-done((bf16[128,1024]{1,0:T(8,128)(2,1)S(1)}, bf16[128,1024]{1,0:T(8,128)(2,1)S(1)}, u32[]{:S(2)}, u32[]{:S(2)}) %collective-permute-start.40) | collective-permute-done | bytes 262176 | tf_op jit(solution)/shard_map/ppermute | solution.py:329
  489.7 4.1 add_convert_fusion.3
  494.4 3.7 fusion.34
  503.8 3.5 convolution_convert_fusion.8.g_ref
  507.3 13.3 %attend_back.1 = bf16[1024,768]{1,0:T(8,128)(2,1)S(1)} custom-call(s32[8]{0:T(128)S(1)} %bitcast.96, bf16[1024,768]{1,0:T(8,128)(2,1)S(1)} %copy-done, bf16[1024,768]{1,0:T(8,128)(2,1)S(1)} %copy-done, bf16[1024,768]{1,0:T(8,128)(2,1)S(1)} %copy-done, bf16[1024,256]{1,0:T(8,128)(2,1)S(1)} %convolution_convert_fusion.8.g_ref, ...), custom_call_target="tpu_custom_call" | custom-call | flops 536870912 | bytes 4194304 | tf_op jit(solution)/shard_map/attend_back/pallas_call | solution.py:272
  520.7 3.7 collective-permute-done.42
  524.4 21.9 %collective-permute-done.44 = bf16[512,1024]{1,0:T(8,128)(2,1)S(1)} collective-permute-done((bf16[512,1024]{1,0:T(8,128)(2,1)}, bf16[512,1024]{1,0:T(8,128)(2,1)S(1)}, u32[]{:S(2)}, u32[]{:S(2)}) %collective-permute-start.44) | collective-permute-done | bytes 1048608 | tf_op jit(solution)/shard_map/ppermute | solution.py:332
  551.7 5.1 convolution_convert_fusion.1
  556.8 6.4 reduce-scatter.9.cloned.1.call-done
  563.4 4.8 collective-permute-start.53
  568.1 3.5 convolution_convert_fusion.7
  571.7 4.1 convolution_convert_fusion.6
  586.3 26.4 %collective-permute-done.52.refs_2_ = bf16[128,1024]{1,0:T(8,128)(2,1)S(1)} collective-permute-done((bf16[128,1024]{1,0:T(8,128)(2,1)S(1)}, bf16[128,1024]{1,0:T(8,128)(2,1)S(1)}, u32[]{:S(2)}, u32[]{:S(2)}) %collective-permute-start.52) | collective-permute-done | bytes 262176 | tf_op jit(solution)/shard_map/ppermute | solution.py:329
  614.5 9.5 %collective-permute-done.54 = bf16[512,1024]{1,0:T(8,128)(2,1)S(1)} collective-permute-done((bf16[512,1024]{1,0:T(8,128)(2,1)S(1)}, bf16[512,1024]{1,0:T(8,128)(2,1)S(1)}, u32[]{:S(2)}, u32[]{:S(2)}) %collective-permute-start.54) | collective-permute-done | bytes 1048608 | tf_op jit(solution)/shard_map/ppermute | solution.py:332
  655.2 10.5 %collective-permute-done.63.refs_2_ = bf16[128,1024]{1,0:T(8,128)(2,1)S(1)} collective-permute-done((bf16[128,1024]{1,0:T(8,128)(2,1)}, bf16[128,1024]{1,0:T(8,128)(2,1)S(1)}, u32[]{:S(2)}, u32[]{:S(2)}) %collective-permute-start.63) | collective-permute-done | bytes 262176 | tf_op jit(solution)/shard_map/ppermute | solution.py:329
  (381 shorter events, 174.2 us)
Async XLA Ops:
  7.2 82.0 %all-gather.5.cloned.1.call-start = ((), (), s32[]{:S(2)}) async-start(), calls=%async_computation.4 | async-start | bytes 4718592 | tf_op jit(solution)/shard_map/all_gather | solution.py:391
  39.8 195.4 %reduce-scatter.5.cloned.1.call-start = ((), (), s32[]{:S(2)}) async-start(), calls=%async_computation.5 | async-start | bytes 4718592 | tf_op jit(solution)/shard_map/reduce_scatter | solution.py:394
  39.8 23.5 %collective-permute-start.9 = (bf16[512,1024]{1,0:T(8,128)(2,1)S(1)}, bf16[512,1024]{1,0:T(8,128)(2,1)S(1)}, u32[]{:S(2)}, u32[]{:S(2)}) collective-permute-start(bf16[512,1024]{1,0:T(8,128)(2,1)S(1)} %place.8.refs_0_), channel_id=1, source_target_pairs={{0,16},{8,24},{16,0},{24,8},{1,17},{9,25},{17,1},{25,9},{2,18},{10... | collective-permute-start | bytes 3145736 | tf_op jit(solution)/shard_map/ppermute | solution.py:332
  41.4 24.2 %collective-permute-start.8 = (bf16[512,1024]{1,0:T(8,128)(2,1)S(1)}, bf16[512,1024]{1,0:T(8,128)(2,1)S(1)}, u32[]{:S(2)}, u32[]{:S(2)}) collective-permute-start(bf16[512,1024]{1,0:T(8,128)(2,1)S(1)} %place.8.refs_0_), channel_id=1, source_target_pairs={{0,8},{8,0},{16,24},{24,16},{1,9},{9,1},{17,25},{25,17},{2,10},{10... | collective-permute-start | bytes 3145736 | tf_op jit(solution)/shard_map/ppermute | solution.py:332
  91.6 23.6 %collective-permute-start.13 = (bf16[128,1024]{1,0:T(8,128)(2,1)S(1)}, bf16[128,1024]{1,0:T(8,128)(2,1)S(1)}, u32[]{:S(2)}, u32[]{:S(2)}) collective-permute-start(bf16[128,1024]{1,0:T(8,128)(2,1)S(1)} %get-tuple-element.209), channel_id=1, source_target_pairs={{0,4},{2,6},{4,0},{6,2},{1,5},{3,7},{5,1},{7,3},{8,12},{10,14},{12... | collective-permute-start | bytes 786440 | tf_op jit(solution)/shard_map/ppermute | solution.py:329
  92.9 22.2 %collective-permute-start.12 = (bf16[128,1024]{1,0:T(8,128)(2,1)S(1)}, bf16[128,1024]{1,0:T(8,128)(2,1)S(1)}, u32[]{:S(2)}, u32[]{:S(2)}) collective-permute-start(bf16[128,1024]{1,0:T(8,128)(2,1)S(1)} %get-tuple-element.210), channel_id=1, source_target_pairs={{0,2},{2,4},{4,6},{6,0},{1,3},{3,5},{5,7},{7,1},{8,10},{10,12},{12... | collective-permute-start | bytes 786440 | tf_op jit(solution)/shard_map/ppermute | solution.py:329
  115.4 23.4 %collective-permute-start.19 = (bf16[512,1024]{1,0:T(8,128)(2,1)S(1)}, bf16[512,1024]{1,0:T(8,128)(2,1)S(1)}, u32[]{:S(2)}, u32[]{:S(2)}) collective-permute-start(bf16[512,1024]{1,0:T(8,128)(2,1)S(1)} %place.9), channel_id=1, source_target_pairs={{0,16},{8,24},{16,0},{24,8},{1,17},{9,25},{17,1},{25,9},{2,18},{10... | collective-permute-start | bytes 3145736 | tf_op jit(solution)/shard_map/ppermute | solution.py:332
  116.9 24.4 %collective-permute-start.18 = (bf16[512,1024]{1,0:T(8,128)(2,1)S(1)}, bf16[512,1024]{1,0:T(8,128)(2,1)S(1)}, u32[]{:S(2)}, u32[]{:S(2)}) collective-permute-start(bf16[512,1024]{1,0:T(8,128)(2,1)S(1)} %place.9), channel_id=1, source_target_pairs={{0,8},{8,0},{16,24},{24,16},{1,9},{9,1},{17,25},{25,17},{2,10},{10... | collective-permute-start | bytes 3145736 | tf_op jit(solution)/shard_map/ppermute | solution.py:332
  118.5 24.4 %collective-permute-start.17 = (bf16[128,1024]{1,0:T(8,128)(2,1)S(1)}, bf16[128,1024]{1,0:T(8,128)(2,1)S(1)}, u32[]{:S(2)}, u32[]{:S(2)}) collective-permute-start(bf16[128,1024]{1,0:T(8,128)(2,1)S(1)} %get-tuple-element.204), channel_id=1, source_target_pairs={{0,6},{2,0},{4,2},{6,4},{1,7},{3,1},{5,3},{7,5},{8,14},{10,8},{12,... | collective-permute-start | bytes 786440 | tf_op jit(solution)/shard_map/ppermute | solution.py:329
  118.5 25.4 %collective-permute-start.16 = (bf16[128,1024]{1,0:T(8,128)(2,1)S(1)}, bf16[128,1024]{1,0:T(8,128)(2,1)S(1)}, u32[]{:S(2)}, u32[]{:S(2)}) collective-permute-start(bf16[128,1024]{1,0:T(8,128)(2,1)S(1)} %get-tuple-element.205), channel_id=1, source_target_pairs={{0,4},{2,6},{4,0},{6,2},{1,5},{3,7},{5,1},{7,3},{8,12},{10,14},{12... | collective-permute-start | bytes 786440 | tf_op jit(solution)/shard_map/ppermute | solution.py:329
  121.3 22.7 %collective-permute-start.15 = (bf16[128,1024]{1,0:T(8,128)(2,1)S(1)}, bf16[128,1024]{1,0:T(8,128)(2,1)S(1)}, u32[]{:S(2)}, u32[]{:S(2)}) collective-permute-start(bf16[128,1024]{1,0:T(8,128)(2,1)S(1)} %get-tuple-element.206), channel_id=1, source_target_pairs={{0,2},{2,4},{4,6},{6,0},{1,3},{3,5},{5,7},{7,1},{8,10},{10,12},{12... | collective-permute-start | bytes 786440 | tf_op jit(solution)/shard_map/ppermute | solution.py:329
  161.6 122.6 %all-gather.9.cloned.1.call-start = ((), (), s32[]{:S(2)}) async-start(), calls=%async_computation.7 | async-start | bytes 4718592 | tf_op jit(solution)/shard_map/all_gather | solution.py:391
  161.6 24.2 %collective-permute-start.26 = (bf16[512,1024]{1,0:T(8,128)(2,1)}, bf16[512,1024]{1,0:T(8,128)(2,1)S(1)}, u32[]{:S(2)}, u32[]{:S(2)}) collective-permute-start(bf16[512,1024]{1,0:T(8,128)(2,1)} %copy-done.10), channel_id=1, source_target_pairs={{0,16},{8,24},{16,0},{24,8},{1,17},{9,25},{17,1},{25,9},{2,18},{10... | collective-permute-start | bytes 3145736 | tf_op jit(solution)/shard_map/ppermute | solution.py:332
  162.3 25.9 %collective-permute-start.25 = (bf16[512,1024]{1,0:T(8,128)(2,1)}, bf16[512,1024]{1,0:T(8,128)(2,1)S(1)}, u32[]{:S(2)}, u32[]{:S(2)}) collective-permute-start(bf16[512,1024]{1,0:T(8,128)(2,1)} %copy-done.10), channel_id=1, source_target_pairs={{0,8},{8,0},{16,24},{24,16},{1,9},{9,1},{17,25},{25,17},{2,10},{10... | collective-permute-start | bytes 3145736 | tf_op jit(solution)/shard_map/ppermute | solution.py:332
  187.6 45.3 %collective-permute-start.28 = (bf16[256,1024]{1,0:T(8,128)(2,1)}, bf16[256,1024]{1,0:T(8,128)(2,1)}, u32[]{:S(2)}, u32[]{:S(2)}) collective-permute-start(bf16[256,1024]{1,0:T(8,128)(2,1)} %slice.207), channel_id=1, source_target_pairs={{0,8},{8,0},{16,24},{24,16},{1,9},{9,1},{17,25},{25,17},{2,10},{10... | collective-permute-start | bytes 1572872 | tf_op jit(solution)/shard_map/ppermute | solution.py:332
  190.1 42.9 %collective-permute-start.27 = (bf16[256,1024]{1,0:T(8,128)(2,1)}, bf16[256,1024]{1,0:T(8,128)(2,1)}, u32[]{:S(2)}, u32[]{:S(2)}) collective-permute-start(bf16[256,1024]{1,0:T(8,128)(2,1)} %slice.206), channel_id=1, source_target_pairs={{0,16},{8,24},{16,0},{24,8},{1,17},{9,25},{17,1},{25,9},{2,18},{10... | collective-permute-start | bytes 1572872 | tf_op jit(solution)/shard_map/ppermute | solution.py:332
  194.2 37.5 %collective-permute-start.23 = (bf16[128,1024]{1,0:T(8,128)(2,1)S(1)}, bf16[128,1024]{1,0:T(8,128)(2,1)S(1)}, u32[]{:S(2)}, u32[]{:S(2)}) collective-permute-start(bf16[128,1024]{1,0:T(8,128)(2,1)S(1)} %get-tuple-element.201), channel_id=1, source_target_pairs={{0,4},{2,6},{4,0},{6,2},{1,5},{3,7},{5,1},{7,3},{8,12},{10,14},{12... | collective-permute-start | bytes 786440 | tf_op jit(solution)/shard_map/ppermute | solution.py:329
  197.1 34.6 %collective-permute-start.22 = (bf16[128,1024]{1,0:T(8,128)(2,1)S(1)}, bf16[128,1024]{1,0:T(8,128)(2,1)S(1)}, u32[]{:S(2)}, u32[]{:S(2)}) collective-permute-start(bf16[128,1024]{1,0:T(8,128)(2,1)S(1)} %get-tuple-element.202), channel_id=1, source_target_pairs={{0,2},{2,4},{4,6},{6,0},{1,3},{3,5},{5,7},{7,1},{8,10},{10,12},{12... | collective-permute-start | bytes 786440 | tf_op jit(solution)/shard_map/ppermute | solution.py:329
  238.6 93.5 %all-gather.7.cloned.1.call-start = ((), (), s32[]{:S(2)}) async-start(), calls=%async_computation.6 | async-start | bytes 4718592 | tf_op jit(solution)/shard_map/all_gather | solution.py:391
  241.8 180.6 %reduce-scatter.7.cloned.1.call-start = ((), (), s32[]{:S(2)}) async-start(), calls=%async_computation.8 | async-start | bytes 4718592 | tf_op jit(solution)/shard_map/reduce_scatter | solution.py:394
  241.9 22.9 %collective-permute-start.30 = (bf16[512,1024]{1,0:T(8,128)(2,1)}, bf16[512,1024]{1,0:T(8,128)(2,1)S(1)}, u32[]{:S(2)}, u32[]{:S(2)}) collective-permute-start(bf16[512,1024]{1,0:T(8,128)(2,1)} %copy-done.13), channel_id=1, source_target_pairs={{0,16},{8,24},{16,0},{24,8},{1,17},{9,25},{17,1},{25,9},{2,18},{10... | collective-permute-start | bytes 3145736 | tf_op jit(solution)/shard_map/ppermute | solution.py:332
  243.2 24.0 %collective-permute-start.29 = (bf16[512,1024]{1,0:T(8,128)(2,1)}, bf16[512,1024]{1,0:T(8,128)(2,1)S(1)}, u32[]{:S(2)}, u32[]{:S(2)}) collective-permute-start(bf16[512,1024]{1,0:T(8,128)(2,1)} %copy-done.13), channel_id=1, source_target_pairs={{0,8},{8,0},{16,24},{24,16},{1,9},{9,1},{17,25},{25,17},{2,10},{10... | collective-permute-start | bytes 3145736 | tf_op jit(solution)/shard_map/ppermute | solution.py:332
  362.5 131.8 %all-gather.11.cloned.1.call-start = ((), (), s32[]{:S(2)}) async-start(), calls=%async_computation.9 | async-start | bytes 4718592 | tf_op jit(solution)/shard_map/all_gather | solution.py:391
  370.3 26.1 %collective-permute-start.33 = (bf16[512,1024]{1,0:T(8,128)(2,1)S(1)}, bf16[512,1024]{1,0:T(8,128)(2,1)S(1)}, u32[]{:S(2)}, u32[]{:S(2)}) collective-permute-start(bf16[512,1024]{1,0:T(8,128)(2,1)S(1)} %get-tuple-element.159), channel_id=1, source_target_pairs={{0,8},{8,0},{16,24},{24,16},{1,9},{9,1},{17,25},{25,17},{2,10},{10... | collective-permute-start | bytes 3145736 | tf_op jit(solution)/shard_map/ppermute | solution.py:332
  371.9 47.3 %collective-permute-start.35 = (bf16[512,1024]{1,0:T(8,128)(2,1)S(1)}, bf16[512,1024]{1,0:T(8,128)(2,1)S(1)}, u32[]{:S(2)}, u32[]{:S(2)}) collective-permute-start(bf16[512,1024]{1,0:T(8,128)(2,1)S(1)} %get-tuple-element.160), channel_id=1, source_target_pairs={{0,24},{8,16},{16,8},{24,0},{1,25},{9,17},{17,9},{25,1},{2,26},{10... | collective-permute-start | bytes 3145736 | tf_op jit(solution)/shard_map/ppermute | solution.py:332
  373.3 47.2 %collective-permute-start.34 = (bf16[512,1024]{1,0:T(8,128)(2,1)S(1)}, bf16[512,1024]{1,0:T(8,128)(2,1)S(1)}, u32[]{:S(2)}, u32[]{:S(2)}) collective-permute-start(bf16[512,1024]{1,0:T(8,128)(2,1)S(1)} %get-tuple-element.161), channel_id=1, source_target_pairs={{0,16},{8,24},{16,0},{24,8},{1,17},{9,25},{17,1},{25,9},{2,18},{10... | collective-permute-start | bytes 3145736 | tf_op jit(solution)/shard_map/ppermute | solution.py:332
  428.1 135.1 %reduce-scatter.9.cloned.1.call-start = ((), (), s32[]{:S(2)}) async-start(), calls=%async_computation.10 | async-start | bytes 4718592 | tf_op jit(solution)/shard_map/reduce_scatter | solution.py:394
  431.7 58.0 %collective-permute-start.36 = (bf16[512,1024]{1,0:T(8,128)(2,1)}, bf16[512,1024]{1,0:T(8,128)(2,1)}, u32[]{:S(2)}, u32[]{:S(2)}) collective-permute-start(bf16[512,1024]{1,0:T(8,128)(2,1)} %get-tuple-element.156), channel_id=1, source_target_pairs={{0,8},{8,0},{16,24},{24,16},{1,9},{9,1},{17,25},{25,17},{2,10},{10... | collective-permute-start | bytes 3145736 | tf_op jit(solution)/shard_map/ppermute | solution.py:332
  433.2 56.6 %collective-permute-start.38 = (bf16[512,1024]{1,0:T(8,128)(2,1)}, bf16[512,1024]{1,0:T(8,128)(2,1)}, u32[]{:S(2)}, u32[]{:S(2)}) collective-permute-start(bf16[512,1024]{1,0:T(8,128)(2,1)} %get-tuple-element.157), channel_id=1, source_target_pairs={{0,24},{8,16},{16,8},{24,0},{1,25},{9,17},{17,9},{25,1},{2,26},{10... | collective-permute-start | bytes 3145736 | tf_op jit(solution)/shard_map/ppermute | solution.py:332
  433.7 56.0 %collective-permute-start.37 = (bf16[512,1024]{1,0:T(8,128)(2,1)}, bf16[512,1024]{1,0:T(8,128)(2,1)}, u32[]{:S(2)}, u32[]{:S(2)}) collective-permute-start(bf16[512,1024]{1,0:T(8,128)(2,1)} %get-tuple-element.158), channel_id=1, source_target_pairs={{0,16},{8,24},{16,0},{24,8},{1,17},{9,25},{17,1},{25,9},{2,18},{10... | collective-permute-start | bytes 3145736 | tf_op jit(solution)/shard_map/ppermute | solution.py:332
  436.5 19.1 %collective-permute-start.41 = (bf16[128,1024]{1,0:T(8,128)(2,1)S(1)}, bf16[128,1024]{1,0:T(8,128)(2,1)S(1)}, u32[]{:S(2)}, u32[]{:S(2)}) collective-permute-start(bf16[128,1024]{1,0:T(8,128)(2,1)S(1)} %get-tuple-element.192), channel_id=1, source_target_pairs={{0,6},{2,0},{4,2},{6,4},{1,7},{3,1},{5,3},{7,5},{8,14},{10,8},{12,... | collective-permute-start | bytes 786440 | tf_op jit(solution)/shard_map/ppermute | solution.py:329
  437.7 49.9 %collective-permute-start.40 = (bf16[128,1024]{1,0:T(8,128)(2,1)S(1)}, bf16[128,1024]{1,0:T(8,128)(2,1)S(1)}, u32[]{:S(2)}, u32[]{:S(2)}) collective-permute-start(bf16[128,1024]{1,0:T(8,128)(2,1)S(1)} %get-tuple-element.193), channel_id=1, source_target_pairs={{0,4},{2,6},{4,0},{6,2},{1,5},{3,7},{5,1},{7,3},{8,12},{10,14},{12... | collective-permute-start | bytes 786440 | tf_op jit(solution)/shard_map/ppermute | solution.py:329
  455.6 32.1 %collective-permute-start.39 = (bf16[128,1024]{1,0:T(8,128)(2,1)S(1)}, bf16[128,1024]{1,0:T(8,128)(2,1)S(1)}, u32[]{:S(2)}, u32[]{:S(2)}) collective-permute-start(bf16[128,1024]{1,0:T(8,128)(2,1)S(1)} %get-tuple-element.194), channel_id=1, source_target_pairs={{0,2},{2,4},{4,6},{6,0},{1,3},{3,5},{5,7},{7,1},{8,10},{10,12},{12... | collective-permute-start | bytes 786440 | tf_op jit(solution)/shard_map/ppermute | solution.py:329
  494.3 152.4 %reduce-scatter.11.cloned.1.call-start = ((), (), s32[]{:S(2)}) async-start(), calls=%async_computation.11 | async-start | bytes 4718592 | tf_op jit(solution)/shard_map/reduce_scatter | solution.py:394
  498.1 26.2 %collective-permute-start.42 = (bf16[512,1024]{1,0:T(8,128)(2,1)}, bf16[512,1024]{1,0:T(8,128)(2,1)S(1)}, u32[]{:S(2)}, u32[]{:S(2)}) collective-permute-start(bf16[512,1024]{1,0:T(8,128)(2,1)} %get-tuple-element.153), channel_id=1, source_target_pairs={{0,8},{8,0},{16,24},{24,16},{1,9},{9,1},{17,25},{25,17},{2,10},{10... | collective-permute-start | bytes 3145736 | tf_op jit(solution)/shard_map/ppermute | solution.py:332
  499.6 46.6 %collective-permute-start.44 = (bf16[512,1024]{1,0:T(8,128)(2,1)}, bf16[512,1024]{1,0:T(8,128)(2,1)S(1)}, u32[]{:S(2)}, u32[]{:S(2)}) collective-permute-start(bf16[512,1024]{1,0:T(8,128)(2,1)} %get-tuple-element.154), channel_id=1, source_target_pairs={{0,24},{8,16},{16,8},{24,0},{1,25},{9,17},{17,9},{25,1},{2,26},{10... | collective-permute-start | bytes 3145736 | tf_op jit(solution)/shard_map/ppermute | solution.py:332
  500.2 47.4 %collective-permute-start.43 = (bf16[512,1024]{1,0:T(8,128)(2,1)}, bf16[512,1024]{1,0:T(8,128)(2,1)S(1)}, u32[]{:S(2)}, u32[]{:S(2)}) collective-permute-start(bf16[512,1024]{1,0:T(8,128)(2,1)} %get-tuple-element.155), channel_id=1, source_target_pairs={{0,16},{8,24},{16,0},{24,8},{1,17},{9,25},{17,1},{25,9},{2,18},{10... | collective-permute-start | bytes 3145736 | tf_op jit(solution)/shard_map/ppermute | solution.py:332
  501.7 48.0 %collective-permute-start.47 = (bf16[128,1024]{1,0:T(8,128)(2,1)S(1)}, bf16[128,1024]{1,0:T(8,128)(2,1)S(1)}, u32[]{:S(2)}, u32[]{:S(2)}) collective-permute-start(bf16[128,1024]{1,0:T(8,128)(2,1)S(1)} %get-tuple-element.188), channel_id=1, source_target_pairs={{0,6},{2,0},{4,2},{6,4},{1,7},{3,1},{5,3},{7,5},{8,14},{10,8},{12,... | collective-permute-start | bytes 786440 | tf_op jit(solution)/shard_map/ppermute | solution.py:329
  503.8 45.9 %collective-permute-start.46 = (bf16[128,1024]{1,0:T(8,128)(2,1)S(1)}, bf16[128,1024]{1,0:T(8,128)(2,1)S(1)}, u32[]{:S(2)}, u32[]{:S(2)}) collective-permute-start(bf16[128,1024]{1,0:T(8,128)(2,1)S(1)} %get-tuple-element.189), channel_id=1, source_target_pairs={{0,4},{2,6},{4,0},{6,2},{1,5},{3,7},{5,1},{7,3},{8,12},{10,14},{12... | collective-permute-start | bytes 786440 | tf_op jit(solution)/shard_map/ppermute | solution.py:329
  524.4 25.4 %collective-permute-start.45 = (bf16[128,1024]{1,0:T(8,128)(2,1)S(1)}, bf16[128,1024]{1,0:T(8,128)(2,1)S(1)}, u32[]{:S(2)}, u32[]{:S(2)}) collective-permute-start(bf16[128,1024]{1,0:T(8,128)(2,1)S(1)} %get-tuple-element.190), channel_id=1, source_target_pairs={{0,2},{2,4},{4,6},{6,0},{1,3},{3,5},{5,7},{7,1},{8,10},{10,12},{12... | collective-permute-start | bytes 786440 | tf_op jit(solution)/shard_map/ppermute | solution.py:329
  563.4 19.6 %collective-permute-start.53 = (bf16[128,1024]{1,0:T(8,128)(2,1)S(1)}, bf16[128,1024]{1,0:T(8,128)(2,1)S(1)}, u32[]{:S(2)}, u32[]{:S(2)}) collective-permute-start(bf16[128,1024]{1,0:T(8,128)(2,1)S(1)} %get-tuple-element.176), channel_id=1, source_target_pairs={{0,6},{2,0},{4,2},{6,4},{1,7},{3,1},{5,3},{7,5},{8,14},{10,8},{12,... | collective-permute-start | bytes 786440 | tf_op jit(solution)/shard_map/ppermute | solution.py:329
  576.2 38.4 %collective-permute-start.50 = (bf16[512,1024]{1,0:T(8,128)(2,1)S(1)}, bf16[512,1024]{1,0:T(8,128)(2,1)S(1)}, u32[]{:S(2)}, u32[]{:S(2)}) collective-permute-start(bf16[512,1024]{1,0:T(8,128)(2,1)S(1)} %pad_maximum_fusion.8), channel_id=1, source_target_pairs={{0,8},{8,0},{16,24},{24,16},{1,9},{9,1},{17,25},{25,17},{2,10},{10... | collective-permute-start | bytes 3145736 | tf_op jit(solution)/shard_map/ppermute | solution.py:332
  577.9 46.2 %collective-permute-start.54 = (bf16[512,1024]{1,0:T(8,128)(2,1)S(1)}, bf16[512,1024]{1,0:T(8,128)(2,1)S(1)}, u32[]{:S(2)}, u32[]{:S(2)}) collective-permute-start(bf16[512,1024]{1,0:T(8,128)(2,1)S(1)} %pad_maximum_fusion.9), channel_id=1, source_target_pairs={{0,16},{8,24},{16,0},{24,8},{1,17},{9,25},{17,1},{25,9},{2,18},{10... | collective-permute-start | bytes 3145736 | tf_op jit(solution)/shard_map/ppermute | solution.py:332
  579.5 44.6 %collective-permute-start.55 = (bf16[512,1024]{1,0:T(8,128)(2,1)S(1)}, bf16[512,1024]{1,0:T(8,128)(2,1)S(1)}, u32[]{:S(2)}, u32[]{:S(2)}) collective-permute-start(bf16[512,1024]{1,0:T(8,128)(2,1)S(1)} %pad_maximum_fusion.10), channel_id=1, source_target_pairs={{0,24},{8,16},{16,8},{24,0},{1,25},{9,17},{17,9},{25,1},{2,26},{10... | collective-permute-start | bytes 3145736 | tf_op jit(solution)/shard_map/ppermute | solution.py:332
  581.0 31.6 %collective-permute-start.52 = (bf16[128,1024]{1,0:T(8,128)(2,1)S(1)}, bf16[128,1024]{1,0:T(8,128)(2,1)S(1)}, u32[]{:S(2)}, u32[]{:S(2)}) collective-permute-start(bf16[128,1024]{1,0:T(8,128)(2,1)S(1)} %get-tuple-element.177), channel_id=1, source_target_pairs={{0,4},{2,6},{4,0},{6,2},{1,5},{3,7},{5,1},{7,3},{8,12},{10,14},{12... | collective-permute-start | bytes 786440 | tf_op jit(solution)/shard_map/ppermute | solution.py:329
  583.0 29.7 %collective-permute-start.51 = (bf16[128,1024]{1,0:T(8,128)(2,1)S(1)}, bf16[128,1024]{1,0:T(8,128)(2,1)S(1)}, u32[]{:S(2)}, u32[]{:S(2)}) collective-permute-start(bf16[128,1024]{1,0:T(8,128)(2,1)S(1)} %get-tuple-element.178), channel_id=1, source_target_pairs={{0,2},{2,4},{4,6},{6,0},{1,3},{3,5},{5,7},{7,1},{8,10},{10,12},{12... | collective-permute-start | bytes 786440 | tf_op jit(solution)/shard_map/ppermute | solution.py:329
  643.8 22.0 %collective-permute-start.63 = (bf16[128,1024]{1,0:T(8,128)(2,1)}, bf16[128,1024]{1,0:T(8,128)(2,1)S(1)}, u32[]{:S(2)}, u32[]{:S(2)}) collective-permute-start(bf16[128,1024]{1,0:T(8,128)(2,1)} %get-tuple-element.169), channel_id=1, source_target_pairs={{0,4},{2,6},{4,0},{6,2},{1,5},{3,7},{5,1},{7,3},{8,12},{10,14},{12... | collective-permute-start | bytes 786440 | tf_op jit(solution)/shard_map/ppermute | solution.py:329
  644.4 21.3 %collective-permute-start.62 = (bf16[128,1024]{1,0:T(8,128)(2,1)}, bf16[128,1024]{1,0:T(8,128)(2,1)S(1)}, u32[]{:S(2)}, u32[]{:S(2)}) collective-permute-start(bf16[128,1024]{1,0:T(8,128)(2,1)} %get-tuple-element.170), channel_id=1, source_target_pairs={{0,2},{2,4},{4,6},{6,0},{1,3},{3,5},{5,7},{7,1},{8,10},{10,12},{12... | collective-permute-start | bytes 786440 | tf_op jit(solution)/shard_map/ppermute | solution.py:329
  (89 other events, 893.3 us)
Sparse Core Ops, SparseCore 0:
  39.9 49.2 all-gather.4
  161.7 61.0 reduce-scatter.4
  238.7 45.3 all-gather.8
  286.2 45.8 all-gather.6
  362.6 48.7 reduce-scatter.6
  428.2 66.0 all-gather.10
  496.6 66.5 reduce-scatter.8
  565.5 66.0 reduce-scatter.10
